TPU v7x, 128 devices: a whole 4x4x4 slice. The times are simulated.
128 devices in a mesh: pw: 16 (over z, y), band: 8 (over x, core).
Axes of the slice: x: 4, y: 4, z: 4, core: 2. Of those that a mesh axis runs over, the one named last changes fastest.
Arguments:
- coefficients: float32 [128, 393216], P(None, ('pw', 'band')), may hold values from -24 to 24
- occupancy: float32 [128], replicated, may hold values from 0.5 to 2
- kinetic: float32 [393216], P(('pw', 'band')), may hold values from 0.1 to 3
- cell_map: int32 [393216], P('pw'), may hold values from 0 to 884735, as said below
- potential_ext: float32 [96, 9216], P('pw'), may hold values from -6 to 6
- core_density: float32 [96, 9216], P('pw'), may hold values from 0.2 to 1
Outputs:
- grad_coef: float32 [128, 393216], P(None, ('pw', 'band'))
- density: float32 [96, 9216], P('pw')
Inputs may be any that keep to these rules, and one draw needn't show every extreme that they name: `cell_map`: positions p * 24576 to (p + 1) * 24576 - 1 hold distinct cell numbers whose y lies from p * 6 to (p + 1) * 6 - 1; each such block holds the first and the last cell of its planes.
All inputs are finite; a program needn't handle non-finite values.
Results may differ from a plain program's by a relative error of at most 0.0003.
Values sent between devices are 32-bit elements; how exact they have to be, the bound alone decides.
No kernel may reach another device: no remote copies, remote signals or barrier semaphores. Data moves between devices by JAX's collectives and lax.ppermute only.
A program may use at most 128 MiB of HBM per device.

v0:
```python
import math

import jax
import jax.numpy as jnp
from jax import lax
from jax.sharding import PartitionSpec as P

G = 96
NPW = 393216
NB = 128
NS_ITERS = 4


highest = lax.Precision.HIGHEST
slater = 0.9847450218426965


def cas_table(length):
    counter = jnp.arange(length, dtype=jnp.int32)
    product = counter[:, None] * counter[None, :] % length
    phases = product.astype(jnp.float32) * (2.0 * math.pi / length)
    return jnp.cos(phases) + jnp.sin(phases)


def matmul(left_side, right_side):
    return jnp.dot(left_side, right_side, precision=highest, preferred_element_type=jnp.float32)


def along_axis(values, cas_values, pattern):
    return jnp.einsum(
        pattern, values, cas_values, precision=highest, preferred_element_type=jnp.float32
    )


def loewdin(intersection):
    frob_norm = jnp.sqrt(jnp.sum(intersection * intersection))
    identity = jnp.eye(intersection.shape[0], dtype=jnp.float32)
    y_iter = intersection / frob_norm
    z_iter = identity
    for repeat in range(NS_ITERS):
        middle = 1.5 * identity - 0.5 * matmul(z_iter, y_iter)
        y_iter = matmul(y_iter, middle)
        z_iter = matmul(middle, z_iter)
    return z_iter / jnp.sqrt(frob_norm)


def shards(coefficients, occupancy, kinetic, cell_map, potential_ext, core_density):
    cas_values = cas_table(G)
    inv_root = 1.0 / math.sqrt(NPW)
    count_pw = lax.axis_size("pw")
    pw_pos = lax.axis_index("pw")
    band_pos = lax.axis_index("band")
    intersection = lax.psum(matmul(coefficients, coefficients.T), ("pw", "band")) / NPW
    weights, pullback = jax.vjp(loewdin, intersection)
    rotated = matmul(weights.T, coefficients)
    spread = rotated * inv_root
    block_coeffs = lax.all_to_all(spread, "band", split_axis=0, concat_axis=1, tiled=True)
    local_bands = block_coeffs.shape[0]
    band_share = lax.dynamic_slice_in_dim(occupancy / NB, band_pos * local_bands, local_bands)
    plane_rows = G // count_pw
    slab_cells = plane_rows * G * G
    local_cells = cell_map - pw_pos * slab_cells
    placed = jnp.zeros((local_bands, slab_cells), jnp.float32).at[:, local_cells].set(block_coeffs)
    along_z = lax.dot_general(
        cas_values,
        placed.reshape(local_bands * slab_cells // G, G),
        (((0,), (1,)), ((), ())),
        precision=highest,
        preferred_element_type=jnp.float32,
    )
    along_z = along_z.reshape(G, local_bands, slab_cells // G)
    received = lax.all_to_all(along_z, "pw", split_axis=0, concat_axis=2, tiled=True)
    shaped = received.reshape(received.shape[0], received.shape[1], G, G)
    shaped = along_axis(shaped, cas_values, "abyx,yk->abkx")
    shaped = along_axis(shaped, cas_values, "abyx,xk->abyk")
    fields = shaped.reshape(received.shape[0], received.shape[1], G * G)
    local_density = jnp.sum(band_share[None, :, None] * fields * fields, axis=1)
    density = core_density + lax.psum(local_density, "band")
    potential = potential_ext - slater * jnp.cbrt(density)
    shaped = (potential[:, None, :] * fields).reshape(plane_rows, local_bands, G, G)
    shaped = along_axis(shaped, cas_values, "abyx,xk->abyk")
    shaped = along_axis(shaped, cas_values, "abyx,yk->abkx").reshape(plane_rows, local_bands, G * G)
    received = lax.all_to_all(shaped, "pw", split_axis=2, concat_axis=0, tiled=True)
    members = received.shape[1]
    turned = lax.dot_general(
        received.reshape(G, members * slab_cells // G),
        cas_values,
        (((0,), (0,)), ((), ())),
        precision=highest,
        preferred_element_type=jnp.float32,
    )
    grid_term = turned.reshape(members, slab_cells)[:, local_cells] * inv_root
    row_term = lax.all_to_all(grid_term, "band", split_axis=1, concat_axis=0, tiled=True)
    grad_rotated = occupancy[:, None] * (kinetic[None, :] * rotated + row_term)
    grad_weights = lax.psum(matmul(coefficients, grad_rotated.T), ("pw", "band"))
    (grad_intersection,) = pullback(grad_weights)
    grad_coef = (
        matmul(weights, grad_rotated)
        + matmul(grad_intersection + grad_intersection.T, coefficients) / NPW
    )
    return (grad_coef, density)


def solution(mesh):
    placed = (
        P(None, ("pw", "band")),
        P(),
        P(("pw", "band")),
        P("pw"),
        P("pw", None),
        P("pw", None),
    )
    return jax.shard_map(
        shards,
        mesh=mesh,
        in_specs=placed,
        out_specs=(P(None, ("pw", "band")), P("pw", None)),
        check_vma=False,
    )
```

profile of v0, /device:TPU:1, one launch (start us, length us, event | category | flops | bytes accessed | tf_op | source)
XLA Modules:
  0.0 957.5 jit_solution(7226617847568424015)
XLA Ops:
  10.6 143.8 %all-reduce.4.cloned.1.call-done = f32[128,128]{1,0:T(8,128)} async-done(((f32[128,128]{1,0:T(8,128)}), f32[128,128]{1,0:T(8,128)}) %all-reduce.4.cloned.1.call-update) | async-done | bytes 65552 | tf_op jit(solution)/shard_map/psum | solution.py:53
  163.9 3.8 all-to-all-start
  169.4 19.1 %all-to-all-done = f32[8,16,3072]{2,1,0:T(8,128)S(1)} async-done(((f32[8,16,3072]{2,1,0:T(8,128)}), f32[8,16,3072]{2,1,0:T(8,128)S(1)}, u32[]{:S(2)}, u32[]{:S(2)}) %all-to-all-start) | async-done | bytes 1572896 | tf_op jit(solution)/shard_map/all_to_all | solution.py:57
  188.5 6.6 copy.36
  195.2 71.8 %scatter_custom_fusion = f32[16,55296]{0,1:T(8,128)} fusion(s32[24576]{0:T(1024)} %get-tuple-element.3, f32[24576,16]{1,0:T(8,128)} %bitcast.127, f32[]{:T(128)} %constant.18.clone.1), kind=kCustom, calls=%fused_computation.2 | custom fusion | bytes 3539456 | tf_op jit(solution)/shard_map/scatter | solution.py:63
  267.0 17.4 %copy.37 = f32[16,576,96]{1,2,0:T(8,128)} copy(f32[16,576,96]{0,2,1:T(8,128)} %bitcast.125) | data formatting | bytes 7077888 | tf_op jit(solution)/shard_map/dot_general | solution.py:64
  284.4 6.0 fusion.24
  290.4 4.2 copy.38
  294.5 4.6 all-to-all-start.1
  299.6 58.3 %all-to-all-done.1 = f32[96,16,576]{2,1,0:T(8,128)} async-done(((f32[96,16,576]{2,1,0:T(8,128)}), f32[96,16,576]{2,1,0:T(8,128)}, u32[]{:S(2)}, u32[]{:S(2)}) %all-to-all-start.1) | async-done | bytes 3538976 | tf_op jit(solution)/shard_map/all_to_all | solution.py:72
  357.9 6.3 copy.39
  364.2 6.1 reshape.40
  370.3 6.4 fusion.29
  376.8 6.0 fusion.2
  384.3 55.3 %all-reduce.6.cloned.1.call-done = f32[6,9216]{1,0:T(8,128)} async-done(((f32[6,9216]{1,0:T(8,128)}), f32[6,9216]{1,0:T(8,128)}) %all-reduce.6.cloned.1.call-update) | async-done | bytes 221200 | tf_op jit(solution)/shard_map/psum | solution.py:78
  441.6 6.3 fusion.5
  447.9 6.2 convolution_bitcast_fusion
  454.1 17.8 %copy.57 = f32[6,16,96,96]{1,0,3,2:T(8,128)} copy(f32[6,16,96,96]{3,2,1,0:T(8,128)} %convolution_bitcast_fusion) | data formatting | bytes 7077888 | tf_op jit(solution)/shard_map/reshape | solution.py:82
  471.9 23.1 %reshape.68 = f32[16,1,55296]{2,1,0:T(1,128)} reshape(f32[9216,6,16]{2,1,0:T(8,128)} %bitcast.123) | data formatting | bytes 7077888
  495.1 47.7 %all_to_all.65 = f32[16,1,55296]{2,1,0:T(1,128)} all-to-all(f32[16,1,55296]{2,1,0:T(1,128)} %reshape.68), channel_id=1, replica_groups=mesh['pw'=16,'band'=8] {'pw'}, dimensions={0} | all-to-all | bytes 7077888 | tf_op jit(solution)/shard_map/all_to_all | solution.py:83
  543.3 21.7 %reduce.1 = f32[16,55296]{1,0:T(8,128)} reduce(f32[16,1,55296]{2,1,0:T(1,128)} %all_to_all.65, f32[]{:T(128)} %broadcast.61), dimensions={1}, to_apply=%all_to_all.55.reduce_sub_computation | reduce | bytes 7077892 | tf_op jit(solution)/shard_map/all_to_all | solution.py:83
  565.0 32.4 %reshape.69 = f32[9216,6,16]{2,1,0:T(8,128)} reshape(f32[16,55296]{1,0:T(8,128)} %reduce.1) | data formatting | bytes 7077888
  597.4 21.0 %copy.44 = f32[16,6,16,576]{3,2,1,0:T(8,128)} copy(f32[16,6,16,576]{2,1,3,0:T(8,128)} %bitcast.124) | data formatting | bytes 7077888 | tf_op jit(solution)/shard_map/all_to_all | solution.py:83
  618.4 5.5 reshape.42
  623.9 11.0 %fusion.36 = f32[9216,96]{1,0:T(8,128)} fusion(f32[96,9216]{1,0:T(8,128)} %reshape.42), kind=kOutput, calls=%fused_computation.75 | convolution fusion | flops 1019308032 | bytes 7077888 | tf_op jit(solution)/shard_map/dot_general | solution.py:85
  634.9 5.5 reshape.43
  640.4 14.5 %copy.46 = f32[16,55296]{0,1:T(8,128)} copy(f32[16,55296]{1,0:T(8,128)} %reshape.43) | data formatting | bytes 7077888 | tf_op jit(solution)/shard_map/reshape | solution.py:92
  654.9 90.5 %gather_fusion = f32[24576,16]{1,0:T(8,128)} fusion(f32[16,55296]{0,1:T(8,128)} %copy.46, s32[24576]{0:T(1024)S(1)} %copy-done.6), kind=kCustom, calls=%fused_computation | custom fusion | bytes 3244032 | tf_op jit(solution)/shard_map/gather | solution.py:92
  745.5 10.2 %broadcast_multiply_fusion = f32[24576,16]{1,0:T(8,128)} fusion(f32[24576,16]{1,0:T(8,128)} %gather_fusion), kind=kLoop, calls=%fused_computation.5 | loop fusion | flops 393216 | bytes 3145728 | tf_op jit(solution)/shard_map/mul | solution.py:92
  755.6 7.4 copy.47
  763.1 31.1 %all_to_all.66 = f32[16,8,3072]{2,0,1:T(8,128)S(1)} all-to-all(f32[16,8,3072]{2,0,1:T(8,128)S(1)} %copy.47), channel_id=1, replica_groups=mesh['pw'=16,'band'=8] {'band'}, dimensions={1} | all-to-all | bytes 3145728 | tf_op jit(solution)/shard_map/all_to_all | solution.py:93
  796.7 133.7 %all-reduce.8.cloned.1.call-done = f32[128,128]{1,0:T(8,128)} async-done(((f32[128,128]{1,0:T(8,128)}), f32[128,128]{1,0:T(8,128)}) %all-reduce.8.cloned.1.call-update) | async-done | bytes 65552 | tf_op jit(solution)/shard_map/psum | solution.py:95
  (80 shorter events, 39.1 us)
Async XLA Ops:
  7.2 1.4 copy-start
  7.2 147.2 %all-reduce.4.cloned.1.call-start = ((), (), s32[]{:S(2)}) async-start(), calls=%async_computation.4 | async-start | bytes 131072 | tf_op jit(solution)/shard_map/psum | solution.py:53
  157.6 1.5 copy-start.10
  158.8 0.6 copy-start.3
  160.1 3.9 copy-start.4
  160.3 3.6 copy-start.2
  160.6 3.4 copy-start.9
  163.9 24.6 %all-to-all-start = ((f32[8,16,3072]{2,1,0:T(8,128)}), f32[8,16,3072]{2,1,0:T(8,128)S(1)}, u32[]{:S(2)}, u32[]{:S(2)}) async-start(f32[8,16,3072]{2,1,0:T(8,128)} %bitcast.129), calls=%async_computation | async-start | bytes 3145728 | tf_op jit(solution)/shard_map/all_to_all | solution.py:57
  294.5 5.0 copy-start.12
  294.5 63.4 %all-to-all-start.1 = ((f32[96,16,576]{2,1,0:T(8,128)}), f32[96,16,576]{2,1,0:T(8,128)}, u32[]{:S(2)}, u32[]{:S(2)}) async-start(f32[96,16,576]{2,1,0:T(8,128)} %copy.38), calls=%async_computation.1 | async-start | bytes 7864320 | tf_op jit(solution)/shard_map/all_to_all | solution.py:72
  299.2 140.4 %all-reduce.6.cloned.1.call-start = ((), (), s32[]{:S(2)}) async-start(), calls=%async_computation.5 | async-start | bytes 589824 | tf_op jit(solution)/shard_map/psum | solution.py:78
  376.7 62.8 %copy-start.7 = (f32[6,9216]{1,0:T(8,128)S(1)}, f32[6,9216]{1,0:T(8,128)}, u32[]{:S(2)}) copy-start(f32[6,9216]{1,0:T(8,128)} %param.10) | copy-start | bytes 663556
  376.8 62.8 %copy-start.8 = (f32[6,9216]{1,0:T(8,128)S(1)}, f32[6,9216]{1,0:T(8,128)}, u32[]{:S(2)}) copy-start(f32[6,9216]{1,0:T(8,128)} %param.11) | copy-start | bytes 663556
  383.7 546.7 %all-reduce.8.cloned.1.call-start = ((), (), s32[]{:S(2)}) async-start(), calls=%async_computation.6 | async-start | bytes 131072 | tf_op jit(solution)/shard_map/psum | solution.py:95
  640.4 14.5 %copy-start.6 = (s32[24576]{0:T(1024)S(1)}, s32[24576]{0:T(1024)}, u32[]{:S(2)}) copy-start(s32[24576]{0:T(1024)} %get-tuple-element.2) | copy-start | bytes 294916
  755.6 38.6 %copy-start.11 = (f32[3072]{0:T(1024)S(1)}, f32[3072]{0:T(1024)}, u32[]{:S(2)}) copy-start(f32[3072]{0:T(1024)} %param.8) | copy-start | bytes 36868
  763.1 31.1 %copy-start.1 = (f32[128,3072]{1,0:T(8,128)S(1)}, f32[128,3072]{1,0:T(8,128)}, u32[]{:S(2)}) copy-start(f32[128,3072]{1,0:T(8,128)} %get-tuple-element.7) | copy-start | bytes 4718596
  930.5 11.0 %copy-start.5 = (f32[128,128]{1,0:T(8,128)S(1)}, f32[128,128]{1,0:T(8,128)}, u32[]{:S(2)}) copy-start(f32[128,128]{1,0:T(8,128)} %all-reduce.4.cloned.1.call-done) | copy-start | bytes 196612
Sparse Core Ops, SparseCore 0:
  13.3 141.0 all-reduce.3
  383.9 55.6 all-reduce.5
  796.7 133.7 all-reduce.7
where the time goes:
time: 967 us; the launch traced here: 957 us
  waiting for transfers between devices  410 us (42%)
  local copies, waits for them, and re-layouts  334 us (35%)
  blocking collectives  78.8 us (8%)
  matrix products  69.2 us (7%)
  other arithmetic  39.4 us (4%)
  between operations  16.8 us (2%)
    psum x1, waiting for transfers between devices, shards(): lax.psum(matmul(coefficients, coefficients.T), ('pw', 'band')) / NPW  144 us
    psum x1, waiting for transfers between devices, shards(): lax.psum(matmul(coefficients, grad_rotated.T), ('pw', 'band'))  134 us
    gather x1, local copies, waits for them, and re-layouts, shards(): grid_term = turned.reshape(members, slab_cells)[:, local_cells] * inv_root  90.5 us
    scatter x1, local copies, waits for them, and re-layouts, shards(): jnp.zeros((local_bands, slab_cells), jnp.float32).at[:, local_cells]  71.8 us
    all_to_all x1, waiting for transfers between devices, shards(): lax.all_to_all(along_z, 'pw', split_axis=0, concat_axis=2, tiled=True)  58.3 us
    unnamed x28, local copies, waits for them, and re-layouts  57.2 us
    psum x1, waiting for transfers between devices, shards(): density = core_density + lax.psum(local_density, 'band')  55.3 us
    all_to_all x1, blocking collectives, shards(): lax.all_to_all(shaped, 'pw', split_axis=2, concat_axis=0, tiled=True)  47.7 us
  transfers between devices with their start and end apart: 5, of which 5 were waited for; matrix products, arithmetic and copies ran while one was open for 0% of the time, Pallas kernels for 0%

commit v1 on v0

v1 whole, which is shorter than its diff:
```python
import math

import jax
import jax.numpy as jnp
import ml_dtypes
import numpy as np
from jax import lax
from jax.experimental import pallas as pl
from jax.experimental.pallas import tpu as pltpu
from jax.sharding import PartitionSpec as P

G = 96
NPW = 393216
NB = 128
NS_ITERS = 4
PW = 16
BD = 8
LB = NB // BD
GY = G // PW
COLS = G * G // (G * BD) * GY
SLAB = GY * G * G
KW = NPW // (PW * BD)
BLK = GY * COLS
ROWS = PW * BLK
SUM_ROWS = ROWS // LB
LANES = 128

highest = lax.Precision.HIGHEST
slater = 0.9847450218426965
bf16 = jnp.bfloat16
f32 = jnp.float32


def halves(table):
    high = table.astype(ml_dtypes.bfloat16)
    low = (table - high.astype(np.float64)).astype(ml_dtypes.bfloat16)
    return high, low


def tables():
    counter = np.arange(G)
    phases = 2.0 * np.pi / G * (counter[:, None] * counter[None, :] % G)
    cas = np.cos(phases) + np.sin(phases)
    order = (np.arange(PW)[None, :] * GY + np.arange(GY)[:, None]).reshape(-1)
    scaled = cas / math.sqrt(NPW)
    mixes = []
    small = np.arange(8)

    def mix(m):
        beta = 2.0 * np.pi / G * (small[:, None] * (m + 12 * small[None, :]))
        even = np.kron(np.cos(beta) + np.sin(beta), np.eye(LB))
        odd = np.kron(np.cos(beta) - np.sin(beta), np.eye(LB))
        return even, odd

    zero = np.zeros((LANES, LANES))
    mixes.append(np.block([[mix(0)[0], zero], [zero, mix(6)[0]]]))
    for m in range(1, 6):
        here, there = mix(m), mix(12 - m)
        mixes.append(np.block([[here[0], there[0]], [here[1], -there[1]]]))
    mixes = np.stack(mixes)
    return dict(
        z_out=halves(scaled[order, :]),
        y_out=halves(cas[:, order]),
        y_in=halves(cas[order, :]),
        z_in=halves(scaled[:, order]),
        mix=halves(mixes),
        mix_t=halves(np.swapaxes(mixes, 1, 2)),
    )


ROOT3 = math.sqrt(3.0) / 2.0


def cos12(e):
    a0, a1, a2 = e[0] + e[6], e[1] + e[5], e[2] + e[4]
    b0, b1, b2 = e[0] - e[6], e[1] - e[5], e[2] - e[4]
    t = ROOT3 * b1
    h = b0 + 0.5 * b2
    r = 0.5 * (a1 + a2)
    d = 0.5 * (a1 - a2)
    return [
        a0 + a1 + a2 + e[3],
        h + t,
        a0 + d - e[3],
        b0 - b2,
        a0 - r + e[3],
        h - t,
        a0 - a1 + a2 - e[3],
    ]


def sin12(o):
    p1, p2 = o[1] + o[5], o[2] + o[4]
    r1, r2 = o[1] - o[5], o[2] - o[4]
    h = 0.5 * p1 + o[3]
    t = ROOT3 * p2
    return [None, h + t, ROOT3 * (r1 + r2), p1 - o[3], ROOT3 * (r1 - r2), h - t]


def split(values):
    high = values.astype(bf16)
    return high, (values - high.astype(f32)).astype(bf16)


def dot(a, b):
    return jnp.dot(a, b, preferred_element_type=f32)


def dot3(a, b):
    return dot(a[0], b[0]) + (dot(a[0], b[1]) + dot(a[1], b[0]))


def lane_bit(shape, bit):
    return (lax.broadcasted_iota(jnp.int32, shape, 1) & bit) == 0


def gather_groups(parts, shape):
    for width in (16, 32, 64):
        first = lane_bit(shape, width)
        parts = [
            jnp.where(first, a, b) + pltpu.roll(jnp.where(first, b, a), width, 1)
            for a, b in zip(parts[0::2], parts[1::2])
        ]
    return parts[0]


def spread_groups(value, shape):
    parts = [value]
    for width in (64, 32, 16):
        first = lane_bit(shape, width)
        turned = [pltpu.roll(part, width, 1) for part in parts]
        parts = [
            side
            for part, turn in zip(parts, turned)
            for side in (jnp.where(first, part, turn), jnp.where(first, turn, part))
        ]
    return parts


def band_sums(parts, shape):
    for width in (1, 2, 4, 8):
        first = lane_bit(shape, width)
        merged = []
        for a, b in zip(parts[0::2], parts[1::2]):
            other = jnp.where(first, b, a)
            other = jnp.where(first, pltpu.roll(other, LANES - width, 1), pltpu.roll(other, width, 1))
            merged.append(jnp.where(first, a, b) + other)
        parts = merged
    return parts[0]


def band_copies(value, shape):
    parts = [value]
    for width in (8, 4, 2, 1):
        first = lane_bit(shape, width)
        parts = [
            side
            for part in parts
            for side in (
                jnp.where(first, part, pltpu.roll(part, width, 1)),
                jnp.where(first, pltpu.roll(part, LANES - width, 1), part),
            )
        ]
    return parts


def lines(ref, start):
    return jnp.concatenate([ref[pl.ds(row, PW, stride=BLK), :] for row in start], axis=0)


def source_masks():
    group = lax.broadcasted_iota(jnp.int32, (1, LANES), 1) // LB
    return [group == s for s in range(BD)]


def scatter_kernel(cells, recv, zh, zl, mh, ml, sent, dense, turned, fields, bh, bl):
    zero = jnp.zeros((256, LANES), f32)

    def clear(i, carry):
        dense[pl.ds(pl.multiple_of(i * 256, 256), 256), :] = zero
        return carry

    lax.fori_loop(0, SLAB // 256, clear, 0)

    def turn(i, carry):
        at = pl.multiple_of(i * LANES, LANES)
        turned[pl.ds(at, LANES), :] = recv[:, pl.ds(at, LANES)].T
        return carry

    lax.fori_loop(0, KW // LANES, turn, 0)
    masks = source_masks()

    def place(i, carry):
        for j in range(8):
            k = i * 8 + j
            row = turned[pl.ds(k, 1), :]
            for s in range(BD):
                cell = cells[s * KW + k]
                pltpu.store(dense.at[pl.ds(cell, 1), :], row, mask=masks[s])
        return carry

    lax.fori_loop(0, KW // 8, place, 0)
    table = (zh[...], zl[...])

    def along_z(i, carry):
        y, pair = i // 6, i % 6
        folded = []
        for side in range(2):
            base = (y * G + (pair * 2 + side) * 8) * G
            tiles = []
            for r in range(0, G, 8):
                parts = [dense[pl.ds(pl.multiple_of(base + xl * G + r, 8), 8), :] for xl in range(8)]
                tiles.append(gather_groups(parts, (8, LANES)))
            folded.append(jnp.concatenate(tiles, axis=0))
        out = dot3(table, split(jnp.concatenate(folded, axis=1)))
        at = pl.multiple_of(y * G, G)
        fields[pair * 2, pl.ds(at, G), :] = out[:, :LANES]
        fields[pair * 2 + 1, pl.ds(at, G), :] = out[:, LANES:]
        return carry

    lax.fori_loop(0, GY * 6, along_z, 0)

    def twelve(i, carry):
        at = pl.multiple_of(i * 16, 16)
        e = [fields[xh, pl.ds(at, 16), :] for xh in range(12)]
        c = cos12([e[0]] + [e[j] + e[12 - j] for j in range(1, 6)] + [e[6]])
        s = sin12([None] + [e[j] - e[12 - j] for j in range(1, 6)])
        for p in range(6):
            high, low = split(jnp.concatenate([c[p], c[6] if p == 0 else s[p]], axis=1))
            bh[p, pl.ds(at, 16), :] = high
            bl[p, pl.ds(at, 16), :] = low
        return carry

    lax.fori_loop(0, GY * G // 16, twelve, 0)

    def along_x(y, carry):
        at = pl.multiple_of(y * G, G)
        for p in range(6):
            data = (bh[p, pl.ds(at, G), :], bl[p, pl.ds(at, G), :])
            out = dot3(data, (mh[p], ml[p]))
            for side, m in enumerate((p, 6 if p == 0 else 12 - p)):
                for z in range(GY):
                    sent[pl.ds(y * COLS + z * 12 + m, PW, stride=BLK), :] = out[
                        z * PW : (z + 1) * PW, side * LANES : (side + 1) * LANES
                    ]
        return carry

    lax.fori_loop(0, GY, along_x, 0)


def density_kernel(recv, yh, yl, share, fields, sums):
    table = (yh[...], yl[...])

    def along_y(i, carry):
        data = [lines(recv, [y * COLS + i * 2 + side for y in range(GY)]) for side in range(2)]
        out = dot3(table, split(jnp.concatenate(data, axis=1)))
        for side in range(2):
            fields[pl.ds(pl.multiple_of((i * 2 + side) * G, G), G), :] = out[:, side * LANES : (side + 1) * LANES]
        return carry

    lax.fori_loop(0, COLS // 2, along_y, 0)
    weight = share[...]

    def squares(i, carry):
        parts = []
        for j in range(LB):
            value = fields[pl.ds(pl.multiple_of(j * SUM_ROWS + i * 8, 8), 8), :]
            parts.append(weight * value * value)
        sums[pl.ds(pl.multiple_of(i * 8, 8), 8), :] = band_sums(parts, (8, LANES))
        return carry

    lax.fori_loop(0, SUM_ROWS // 8, squares, 0)


def potential_kernel(density, external, fields, yh, yl, sent, product):
    def multiply(i, carry):
        at = pl.multiple_of(i * 8, 8)
        dens = density[pl.ds(at, 8), :]
        root = jnp.exp(jnp.log(dens) * (1.0 / 3.0))
        root = root - (root - dens / (root * root)) * (1.0 / 3.0)
        copies = band_copies(external[pl.ds(at, 8), :] - slater * root, (8, LANES))
        for j in range(LB):
            row = pl.ds(pl.multiple_of(j * SUM_ROWS + i * 8, 8), 8)
            product[row, :] = copies[j] * fields[row, :]
        return carry

    lax.fori_loop(0, SUM_ROWS // 8, multiply, 0)
    table = (yh[...], yl[...])

    def along_y(i, carry):
        data = [product[pl.ds(pl.multiple_of((i * 2 + side) * G, G), G), :] for side in range(2)]
        out = dot3(table, split(jnp.concatenate(data, axis=1)))
        for side in range(2):
            for y in range(GY):
                sent[pl.ds(y * COLS + i * 2 + side, PW, stride=BLK), :] = out[
                    y * PW : (y + 1) * PW, side * LANES : (side + 1) * LANES
                ]
        return carry

    lax.fori_loop(0, COLS // 2, along_y, 0)


def gather_kernel(cells, recv, zh, zl, mh, ml, terms, dense, turned, uv, bh, bl):
    table = (zh[...], zl[...])

    def plane(y, carry):
        for p in range(6):
            data = [
                lines(recv, [y * COLS + z * 12 + m for z in range(GY)]) for m in (p, 6 if p == 0 else 12 - p)
            ]
            out = dot3(split(jnp.concatenate(data, axis=1)), (mh[p], ml[p]))
            uv[p] = out

        def twelve(i, inner):
            at = pl.multiple_of(i * 16, 16)
            u = [uv[p, pl.ds(at, 16), :LANES] for p in range(6)] + [uv[0, pl.ds(at, 16), LANES:]]
            v = [None] + [uv[p, pl.ds(at, 16), LANES:] for p in range(1, 6)]
            c, s = cos12(u), sin12(v)
            x = [c[0]] + [c[j] + s[j] for j in range(1, 6)] + [c[6]] + [c[j] - s[j] for j in range(5, 0, -1)]
            for p in range(6):
                high, low = split(jnp.concatenate([x[2 * p], x[2 * p + 1]], axis=1))
                bh[p, pl.ds(at, 16), :] = high
                bl[p, pl.ds(at, 16), :] = low
            return inner

        lax.fori_loop(0, G // 16, twelve, 0)

        def along_z(pair, inner):
            out = dot3(table, (bh[pair], bl[pair]))
            for side in range(2):
                base = (y * G + (pair * 2 + side) * 8) * G
                for r in range(0, G, 8):
                    copies = spread_groups(out[r : r + 8, side * LANES : (side + 1) * LANES], (8, LANES))
                    for xl in range(8):
                        dense[pl.ds(pl.multiple_of(base + xl * G + r, 8), 8), :] = copies[xl]
            return inner

        lax.fori_loop(0, 6, along_z, 0)
        return carry

    lax.fori_loop(0, GY, plane, 0)
    masks = source_masks()

    def pick(i, carry):
        for j in range(8):
            k = i * 8 + j
            row = dense[pl.ds(cells[k], 1), :]
            for s in range(1, BD):
                row = jnp.where(masks[s], dense[pl.ds(cells[s * KW + k], 1), :], row)
            turned[pl.ds(k, 1), :] = row
        return carry

    lax.fori_loop(0, KW // 8, pick, 0)

    def turn(i, carry):
        at = pl.multiple_of(i * LANES, LANES)
        terms[:, pl.ds(at, LANES)] = turned[pl.ds(at, LANES), :].T
        return carry

    lax.fori_loop(0, KW // LANES, turn, 0)


def call(kernel, out_shapes, scratch, scalars, *operands):
    vmem = pl.BlockSpec(memory_space=pltpu.VMEM)
    smem = pl.BlockSpec(memory_space=pltpu.SMEM)
    return pl.pallas_call(
        kernel,
        out_shape=out_shapes,
        in_specs=[smem] * scalars + [vmem] * (len(operands) - scalars),
        out_specs=jax.tree.map(lambda _: vmem, out_shapes),
        scratch_shapes=scratch,
        compiler_params=pltpu.CompilerParams(vmem_limit_bytes=56 * 1024 * 1024),
    )(*operands)


def array(*shape):
    return jax.ShapeDtypeStruct(shape, f32)


def matmul(left_side, right_side):
    return jnp.dot(left_side, right_side, precision=highest, preferred_element_type=f32)


def loewdin(intersection):
    frob_norm = jnp.sqrt(jnp.sum(intersection * intersection))
    identity = jnp.eye(intersection.shape[0], dtype=f32)
    y_iter = intersection / frob_norm
    z_iter = identity
    for repeat in range(NS_ITERS):
        middle = 1.5 * identity - 0.5 * matmul(z_iter, y_iter)
        y_iter = matmul(y_iter, middle)
        z_iter = matmul(middle, z_iter)
    return z_iter / jnp.sqrt(frob_norm)


def total(values):
    axes = ("pw", "band")
    pieces = lax.all_to_all(values, axes, split_axis=0, concat_axis=0, tiled=True)
    row = jnp.sum(pieces, axis=0, keepdims=True)
    copies = jnp.broadcast_to(row, values.shape)
    return lax.all_to_all(copies, axes, split_axis=0, concat_axis=0, tiled=True)


def band_total(values):
    values = values + lax.ppermute(values, "band", [(i, i ^ 1) for i in range(BD)])
    others = [lax.ppermute(values, "band", [(i, (i + 2 * step) % BD) for i in range(BD)]) for step in (1, 2, 3)]
    return values + ((others[0] + others[2]) + others[1])


def to_sums(planes):
    values = planes.reshape(GY, G, BD, 12).transpose(0, 3, 1, 2).reshape(LB, SUM_ROWS, BD)
    return values.transpose(1, 2, 0).reshape(SUM_ROWS, LANES)


def from_sums(sums):
    values = sums.reshape(SUM_ROWS, BD, LB).transpose(2, 0, 1).reshape(GY, 12, G, BD)
    return values.transpose(0, 2, 3, 1).reshape(GY, G * G)


def shards(coefficients, occupancy, kinetic, cell_map, potential_ext, core_density):
    table = tables()
    pw_pos = lax.axis_index("pw")
    band_pos = lax.axis_index("band")
    cells = cell_map - pw_pos * SLAB
    share = lax.dynamic_slice_in_dim(occupancy / NB, band_pos * LB, LB)
    share = jnp.tile(share, BD).reshape(1, LANES)
    core = to_sums(core_density)
    external = to_sums(potential_ext)

    intersection = total(matmul(coefficients, coefficients.T)) / NPW
    weights, pullback = jax.vjp(loewdin, intersection)
    rotated = matmul(weights.T, coefficients)
    block = lax.all_to_all(rotated, "band", split_axis=0, concat_axis=0, tiled=True)
    sent = call(
        scatter_kernel,
        array(ROWS, LANES),
        [
            pltpu.VMEM((SLAB, LANES), f32),
            pltpu.VMEM((KW, LANES), f32),
            pltpu.VMEM((12, GY * G, LANES), f32),
            pltpu.VMEM((6, GY * G, 2 * LANES), bf16),
            pltpu.VMEM((6, GY * G, 2 * LANES), bf16),
        ],
        1,
        cells,
        block,
        *table["z_out"],
        *table["mix"],
    )
    received = lax.all_to_all(sent, "pw", split_axis=0, concat_axis=0, tiled=True)
    fields, sums = call(
        density_kernel,
        (array(ROWS, LANES), array(SUM_ROWS, LANES)),
        [],
        0,
        received,
        *table["y_out"],
        share,
    )
    density = core + band_total(sums)
    sent = call(
        potential_kernel,
        array(ROWS, LANES),
        [pltpu.VMEM((ROWS, LANES), f32)],
        0,
        density,
        external,
        fields,
        *table["y_in"],
    )
    received = lax.all_to_all(sent, "pw", split_axis=0, concat_axis=0, tiled=True)
    terms = call(
        gather_kernel,
        array(NB, KW),
        [
            pltpu.VMEM((SLAB, LANES), f32),
            pltpu.VMEM((KW, LANES), f32),
            pltpu.VMEM((6, G, 2 * LANES), f32),
            pltpu.VMEM((6, G, 2 * LANES), bf16),
            pltpu.VMEM((6, G, 2 * LANES), bf16),
        ],
        1,
        cells,
        received,
        *table["z_in"],
        *table["mix_t"],
    )
    row_term = lax.all_to_all(terms, "band", split_axis=0, concat_axis=0, tiled=True)
    grad_rotated = occupancy[:, None] * (kinetic[None, :] * rotated + row_term)
    grad_weights = total(matmul(coefficients, grad_rotated.T))
    (grad_intersection,) = pullback(grad_weights)
    grad_coef = (
        matmul(weights, grad_rotated) + matmul(grad_intersection + grad_intersection.T, coefficients) / NPW
    )
    return (grad_coef, from_sums(density))


def solution(mesh):
    placed = (
        P(None, ("pw", "band")),
        P(),
        P(("pw", "band")),
        P("pw"),
        P("pw", None),
        P("pw", None),
    )
    return jax.shard_map(
        shards,
        mesh=mesh,
        in_specs=placed,
        out_specs=(P(None, ("pw", "band")), P("pw", None)),
        check_vma=False,
    )
```

time: 967 us -> 447 us (0.46)
  waiting for transfers between devices: 410 us -> 73.3 us
  local copies, waits for them, and re-layouts: 334 us -> 30.8 us
  Pallas kernels: 0 us -> 157 us
  blocking collectives: 78.8 us -> 125 us
  matrix products: 69.2 us -> 28.1 us
  other arithmetic: 39.4 us -> 9.34 us
  between operations: 16.8 us -> 3.32 us
    psum x3 -> x0, waiting for transfers between devices: 333 us -> none  [the longest x1 144 us: shards(): lax.psum(matmul(coefficients, coefficients.T), ('pw', 'band')) / NPW]
    pallas_call x0 -> x4, Pallas kernels: none -> 157 us  [call(): pl.pallas_call(kernel, out_shape=out_shapes, in_specs=[smem] * scalars +...]
    gather x1 -> x0, local copies, waits for them, and re-layouts: 90.5 us -> none  [shards(): grid_term = turned.reshape(members, slab_cells)[:, local_cells] * inv_root]
    scatter x1 -> x0, local copies, waits for them, and re-layouts: 71.8 us -> none  [shards(): jnp.zeros((local_bands, slab_cells), jnp.float32).at[:, local_cells]]
    unnamed x28 -> x50, local copies, waits for them, and re-layouts: 57.2 us -> 3.22 us
    all_to_all x2 -> x5, blocking collectives: 78.8 us -> 125 us  [the longest x1 47.3 us: shards(): lax.all_to_all(sent, 'pw', split_axis=0, concat_axis=0, tiled=True)]
    dot_general x6 -> x0, matrix products: 41.9 us -> none  [the longest x4 25 us: along_axis(): jnp.einsum(pattern, values, cas_values, precision=highest, preferred_elem...]
    reshape x5 -> x8, local copies, waits for them, and re-layouts: 49.5 us -> 15.7 us  [the longest x4 8.29 us: to_sums(): planes.reshape(GY, G, BD, 12).transpose(0, 3, 1, 2)]
  transfers between devices with their start and end apart: 5 -> 7, of which waited for: 5 -> 3; matrix products, arithmetic and copies ran while one was open for 0% -> 6% of each run, Pallas kernels for 0% -> 0%
where the time goes in v1:
time: 447 us; the launch traced here: 445 us
  Pallas kernels  157 us (35%)
  blocking collectives  125 us (28%)
  waiting for transfers between devices  73.3 us (16%)
  local copies, waits for them, and re-layouts  30.8 us (7%)
  matrix products  28.1 us (6%)
  starting transfers between devices  18.9 us (4%)
  other arithmetic  9.34 us (2%)
    pallas_call x4, Pallas kernels, call(): pl.pallas_call(kernel, out_shape=out_shapes, in_specs=[smem] * scalars +...  157 us
    all_to_all x1, waiting for transfers between devices, shards(): lax.all_to_all(sent, 'pw', split_axis=0, concat_axis=0, tiled=True)  51.9 us
    all_to_all x1, blocking collectives, shards(): lax.all_to_all(sent, 'pw', split_axis=0, concat_axis=0, tiled=True)  47.3 us
    all_to_all x2, blocking collectives, total(): lax.all_to_all(values, axes, split_axis=0, concat_axis=0, tiled=True)  36.1 us
    dot_general x36, matrix products, matmul(): jnp.dot(left_side, right_side, precision=highest, preferred_element_type=...  28.1 us
    all_to_all x1, blocking collectives, shards(): lax.all_to_all(terms, 'band', split_axis=0, concat_axis=0, tiled=True)  27.4 us
    all_to_all x1, waiting for transfers between devices, shards(): lax.all_to_all(rotated, 'band', split_axis=0, concat_axis=0, tiled=True)  20.1 us
    all_to_all x1, blocking collectives, total(): return lax.all_to_all(copies, axes, split_axis=0, concat_axis=0, tiled=True)  13.9 us
  transfers between devices with their start and end apart: 7, of which 3 were waited for; matrix products, arithmetic and copies ran while one was open for 6% of the time, Pallas kernels for 0%

profile of v1, /device:TPU:1, one launch (start us, length us, event | category | flops | bytes accessed | tf_op | source)
XLA Modules:
  0.0 445.3 jit_solution(2895003453980884579)
XLA Ops:
  0.6 1.4 copy-done
  3.4 20.9 %all_to_all.75 = f32[128,1,128]{2,1,0:T(1,128)S(1)} all-to-all(f32[128,1,128]{2,1,0:T(1,128)S(1)} %bitcast.145), channel_id=1, replica_groups=mesh['pw'=16,'band'=8] {'pw','band'}, dimensions={0} | all-to-all | bytes 131072 | tf_op jit(solution)/shard_map/all_to_all | solution.py:398
  24.5 13.9 %all_to_all.76 = f32[128,1,128]{2,1,0:T(1,128)S(1)} all-to-all(f32[128,1,128]{2,1,0:T(1,128)S(1)} %broadcast_in_dim.4), channel_id=1, replica_groups=mesh['pw'=16,'band'=8] {'pw','band'}, dimensions={0} | all-to-all | bytes 131072 | tf_op jit(solution)/shard_map/all_to_all | solution.py:401
  42.8 2.6 fusion.17
  45.4 4.4 all-to-all-start.2
  50.4 20.1 %all-to-all-done.2 = f32[8,16,3072]{2,1,0:T(8,128)S(1)} async-done(((f32[8,16,3072]{2,1,0:T(8,128)}), f32[8,16,3072]{2,1,0:T(8,128)S(1)}, u32[]{:S(2)}, u32[]{:S(2)}) %all-to-all-start.2) | async-done | bytes 1572896 | tf_op jit(solution)/shard_map/all_to_all | solution.py:433
  71.7 52.8 %shard_map.185 = f32[6912,128]{1,0:T(8,128)} custom-call(s32[24576]{0:T(1024)} %broadcast_subtract_fusion.cells, f32[128,3072]{1,0:T(8,128)} %bitcast.131, bf16[96,96]{1,0:T(8,128)(2,1)} %constant.59.clone.zh, bf16[96,96]{1,0:T(8,128)(2,1)} %constant.60.clone.zl, bf16[6,256,256]{2,1,0:T(8,128)(2,1)} %constant.61.clone.mh, bf16[6,256,256]{2,1,0:T(8,128)(2,1)} %constant.62.clone.ml), custom_call_target="tpu_custom_call" | custom-call | tf_op jit(solution)/shard_map/pallas_call | solution.py:366
  124.5 4.6 %all-to-all-start.3 = ((f32[16,432,128]{2,1,0:T(8,128)}), f32[16,432,128]{2,1,0:T(8,128)}, u32[]{:S(2)}, u32[]{:S(2)}) async-start(f32[16,432,128]{2,1,0:T(8,128)} %bitcast.126), calls=%async_computation.3 | async-start | bytes 7077888 | tf_op jit(solution)/shard_map/all_to_all | solution.py:450
  129.9 51.9 %all-to-all-done.3 = f32[16,432,128]{2,1,0:T(8,128)} async-done(((f32[16,432,128]{2,1,0:T(8,128)}), f32[16,432,128]{2,1,0:T(8,128)}, u32[]{:S(2)}, u32[]{:S(2)}) %all-to-all-start.3) | async-done | bytes 3538976 | tf_op jit(solution)/shard_map/all_to_all | solution.py:450
  181.8 27.1 %shard_map.186 = (f32[6912,128]{1,0:T(8,128)}, f32[432,128]{1,0:T(8,128)}) custom-call(f32[6912,128]{1,0:T(8,128)} %bitcast.10.recv, bf16[96,96]{1,0:T(8,128)(2,1)} %constant.63.clone.yh, bf16[96,96]{1,0:T(8,128)(2,1)} %constant.64.clone.yl, f32[1,128]{1,0:T(1,128)} %reshape_tile.3.share), custom_call_target="tpu_custom_call" | custom-call | tf_op jit(solution)/shard_map/pallas_call | solution.py:366
  208.9 1.7 collective-permute-start
  213.3 2.4 collective-permute-start.2
  215.6 4.0 reshape.66
  219.6 2.4 copy.30
  222.4 4.0 reshape.69
  226.4 2.4 copy.32
  229.8 1.8 add_add_fusion.density
  231.5 28.2 %shard_map.187 = f32[6912,128]{1,0:T(8,128)} custom-call(f32[432,128]{1,0:T(8,128)} %add_add_fusion.density, f32[432,128]{1,0:T(8,128)} %copy.33.external, f32[6912,128]{1,0:T(8,128)} %get-tuple-element.5.fields, bf16[96,96]{1,0:T(8,128)(2,1)} %constant.65.clone.yh, bf16[96,96]{1,0:T(8,128)(2,1)} %constant.66.clone.yl), custom_call_target="tpu_custom_call" | custom-call | tf_op jit(solution)/shard_map/pallas_call | solution.py:366
  259.7 47.3 %all_to_all.77 = f32[16,432,128]{2,1,0:T(8,128)} all-to-all(f32[16,432,128]{2,1,0:T(8,128)} %bitcast.128), channel_id=1, replica_groups=mesh['pw'=16,'band'=8] {'pw'}, dimensions={0} | all-to-all | bytes 7077888 | tf_op jit(solution)/shard_map/all_to_all | solution.py:471
  307.1 48.8 %shard_map.188 = f32[128,3072]{1,0:T(8,128)} custom-call(s32[24576]{0:T(1024)} %broadcast_subtract_fusion.cells, f32[6912,128]{1,0:T(8,128)} %bitcast.127, bf16[96,96]{1,0:T(8,128)(2,1)} %constant.67.clone.zh, bf16[96,96]{1,0:T(8,128)(2,1)} %constant.68.clone.zl, bf16[6,256,256]{2,1,0:T(8,128)(2,1)} %constant.69.clone.mh, bf16[6,256,256]{2,1,0:T(8,128)(2,1)} %constant.70.clone.ml), custom_call_target="tpu_custom_call" | custom-call | tf_op jit(solution)/shard_map/pallas_call | solution.py:366
  355.9 27.4 %all_to_all.78 = f32[8,16,3072]{2,1,0:T(8,128)S(1)} all-to-all(f32[8,16,3072]{2,1,0:T(8,128)} %bitcast.132), channel_id=1, replica_groups=mesh['pw'=16,'band'=8] {'band'}, dimensions={0} | all-to-all | bytes 3145728 | tf_op jit(solution)/shard_map/all_to_all | solution.py:488
  383.3 1.8 fusion
  385.1 2.0 convolution_bitcast_fusion
  387.2 1.6 copy.34
  388.7 15.1 %all_to_all.79 = f32[128,1,128]{2,1,0:T(1,128)} all-to-all(f32[128,1,128]{2,1,0:T(1,128)} %copy.34), channel_id=1, replica_groups=mesh['pw'=16,'band'=8] {'pw','band'}, dimensions={0} | all-to-all | bytes 131072 | tf_op jit(solution)/shard_map/all_to_all | solution.py:398
  405.5 5.4 %all-to-all-start.7 = ((f32[128,1,128]{2,1,0:T(1,128)}), f32[128,1,128]{2,1,0:T(1,128)}, u32[]{:S(2)}, u32[]{:S(2)}) async-start(f32[128,1,128]{2,1,0:T(1,128)} %broadcast_in_dim.5), calls=%async_computation.7 | async-start | bytes 131072 | tf_op jit(solution)/shard_map/all_to_all | solution.py:401
  411.9 1.9 reshape.73
  413.9 3.2 copy.39
  417.1 4.5 %reshape.74 = f32[6,9216]{1,0:T(8,128)} reshape(f32[6,96,8,12]{3,2,1,0:T(8,128)} %copy.39) | data formatting | bytes 442368 | tf_op jit(solution)/shard_map/reshape | solution.py:417
  430.9 1.5 fusion.12
  441.1 1.5 convolution_multiply_fusion
  442.6 2.7 convolution_add_fusion
  (107 shorter events, 30.7 us)
Async XLA Ops:
  0.6 1.4 copy-start
  38.5 3.0 copy-start.13
  40.0 1.7 copy-start.21
  40.2 0.6 copy-start.15
  40.4 5.0 %copy-start.7 = (f32[128,128]{1,0:T(8,128)}, f32[128,128]{1,0:T(8,128)S(1)}, u32[]{:S(2)}) copy-start(f32[128,128]{1,0:T(8,128)S(1)} %fusion.16) | copy-start | bytes 196612
  41.0 4.4 copy-start.9
  41.2 4.1 copy-start.5
  41.7 0.6 copy-start.17
  41.9 3.5 copy-start.3
  42.5 2.9 copy-start.16
  42.8 2.6 copy-start.10
  45.4 4.4 copy-start.22
  45.4 25.1 %all-to-all-start.2 = ((f32[8,16,3072]{2,1,0:T(8,128)}), f32[8,16,3072]{2,1,0:T(8,128)S(1)}, u32[]{:S(2)}, u32[]{:S(2)}) async-start(f32[8,16,3072]{2,1,0:T(8,128)} %bitcast.7), calls=%async_computation.2 | async-start | bytes 3145728 | tf_op jit(solution)/shard_map/all_to_all | solution.py:433
  70.5 1.2 copy-start.1
  124.5 4.7 %copy-start.24 = (f32[128]{0:T(128)S(1)}, f32[128]{0:T(128)}, u32[]{:S(2)}) copy-start(f32[128]{0:T(128)} %param.19) | copy-start | bytes 1540
  124.5 57.3 %all-to-all-start.3 = ((f32[16,432,128]{2,1,0:T(8,128)}), f32[16,432,128]{2,1,0:T(8,128)}, u32[]{:S(2)}, u32[]{:S(2)}) async-start(f32[16,432,128]{2,1,0:T(8,128)} %bitcast.126), calls=%async_computation.3 | async-start | bytes 7077888 | tf_op jit(solution)/shard_map/all_to_all | solution.py:450
  181.8 33.8 %copy-start.19 = (f32[6,9216]{1,0:T(8,128)S(1)}, f32[6,9216]{1,0:T(8,128)}, u32[]{:S(2)}) copy-start(f32[6,9216]{1,0:T(8,128)} %param.23) | copy-start | bytes 663556
  208.9 3.0 collective-permute-start
  212.9 16.9 %collective-permute-start.1 = (f32[432,128]{1,0:T(8,128)S(1)}, f32[432,128]{1,0:T(8,128)S(1)}, u32[]{:S(2)}, u32[]{:S(2)}) collective-permute-start(f32[432,128]{1,0:T(8,128)S(1)} %add.28), channel_id=1, source_target_pairs={{0,2},{1,3},{2,4},{3,5},{4,6},{5,7},{6,0},{7,1},{8,10},{9,11},{10,... | collective-permute-start | bytes 663560 | tf_op jit(solution)/shard_map/ppermute | solution.py:406
  213.3 16.5 %collective-permute-start.2 = (f32[432,128]{1,0:T(8,128)S(1)}, f32[432,128]{1,0:T(8,128)}, u32[]{:S(2)}, u32[]{:S(2)}) collective-permute-start(f32[432,128]{1,0:T(8,128)S(1)} %add.28), channel_id=1, source_target_pairs={{0,6},{1,7},{2,0},{3,1},{4,2},{5,3},{6,4},{7,5},{8,14},{9,15},{10,... | collective-permute-start | bytes 663560 | tf_op jit(solution)/shard_map/ppermute | solution.py:406
  215.6 14.1 %collective-permute-start.3 = (f32[432,128]{1,0:T(8,128)S(1)}, f32[432,128]{1,0:T(8,128)}, u32[]{:S(2)}, u32[]{:S(2)}) collective-permute-start(f32[432,128]{1,0:T(8,128)S(1)} %add.28), channel_id=1, source_target_pairs={{0,4},{1,5},{2,6},{3,7},{4,0},{5,1},{6,2},{7,3},{8,12},{9,13},{10,... | collective-permute-start | bytes 663560 | tf_op jit(solution)/shard_map/ppermute | solution.py:406
  219.6 2.7 copy-start.20
  355.9 27.4 %copy-start.23 = (f32[3072]{0:T(1024)S(1)}, f32[3072]{0:T(1024)}, u32[]{:S(2)}) copy-start(f32[3072]{0:T(1024)} %param.20) | copy-start | bytes 36868
  385.1 26.0 %copy-start.2 = (f32[432,128]{1,0:T(8,128)S(1)}, f32[432,128]{1,0:T(8,128)}, u32[]{:S(2)}) copy-start(f32[432,128]{1,0:T(8,128)} %add_add_fusion.density) | copy-start | bytes 663556
  405.5 16.0 %all-to-all-start.7 = ((f32[128,1,128]{2,1,0:T(1,128)}), f32[128,1,128]{2,1,0:T(1,128)}, u32[]{:S(2)}, u32[]{:S(2)}) async-start(f32[128,1,128]{2,1,0:T(1,128)} %broadcast_in_dim.5), calls=%async_computation.7 | async-start | bytes 131072 | tf_op jit(solution)/shard_map/all_to_all | solution.py:401
  417.0 6.5 %copy-start.4 = (f32[128,128]{1,0:T(8,128)S(1)}, f32[128,128]{1,0:T(8,128)}, u32[]{:S(2)}) copy-start(f32[128,128]{1,0:T(8,128)} %copy-done.3) | copy-start | bytes 196612
  417.1 8.2 %copy-start.6 = (f32[128,128]{1,0:T(8,128)S(1)}, f32[128,128]{1,0:T(8,128)}, u32[]{:S(2)}) copy-start(f32[128,128]{1,0:T(8,128)} %copy-done.5) | copy-start | bytes 196612
  421.5 7.5 %copy-start.8 = (f32[128,128]{1,0:T(8,128)S(1)}, f32[128,128]{1,0:T(8,128)}, u32[]{:S(2)}) copy-start(f32[128,128]{1,0:T(8,128)} %copy-done.7) | copy-start | bytes 196612
  421.5 9.3 %copy-start.11 = (f32[128,128]{1,0:T(8,128)S(1)}, f32[128,128]{1,0:T(8,128)}, u32[]{:S(2)}) copy-start(f32[128,128]{1,0:T(8,128)} %copy-done.10) | copy-start | bytes 196612
  425.8 13.7 %copy-start.14 = (f32[128,1,128]{2,1,0:T(1,128)S(1)}, f32[128,1,128]{2,1,0:T(1,128)}, u32[]{:S(2)}) copy-start(f32[128,1,128]{2,1,0:T(1,128)} %copy-done.13) | copy-start | bytes 196612
  427.0 3.9 copy-start.18
  441.1 1.5 copy-start.12

commit v2 on v1

v2 whole, which is shorter than its diff:
```python
import functools
import math

import jax
import jax.numpy as jnp
import ml_dtypes
import numpy as np
from jax import lax
from jax.experimental import pallas as pl
from jax.experimental.pallas import tpu as pltpu
from jax.sharding import PartitionSpec as P

G = 96
NPW = 393216
NB = 128
NS_ITERS = 4
PW = 16
BD = 8
LB = NB // BD
GY = G // PW
PARTS = 2
BLOCKS = ((0, 6), (1, 11), (2, 10), (3, 9), (4, 8), (5, 7))
PAIRS = len(BLOCKS) // PARTS
XB = 2 * PAIRS
COLS = GY * XB
HALF = G // 2
WIDE = XB * 128
SLAB = GY * G * G
KW = NPW // (PW * BD)
BLK = GY * COLS
ROWS = PW * BLK
SUM_ROWS = GY * HALF
LANES = 128

highest = lax.Precision.HIGHEST
slater = 0.9847450218426965
bf16 = jnp.bfloat16
f32 = jnp.float32


def halves(table):
    high = table.astype(ml_dtypes.bfloat16)
    low = (table - high.astype(np.float64)).astype(ml_dtypes.bfloat16)
    return high, low


def tables():
    counter = np.arange(G)
    phases = 2.0 * np.pi / G * (counter[:, None] * counter[None, :] % G)
    cas = np.cos(phases) + np.sin(phases)
    order = (np.arange(PW)[None, :] * GY + np.arange(GY)[:, None]).reshape(-1)
    scaled = cas / math.sqrt(NPW)
    mixes = []
    small = np.arange(8)

    def mix(m):
        beta = 2.0 * np.pi / G * (small[:, None] * (m + 12 * small[None, :]))
        even = np.kron(np.cos(beta) + np.sin(beta), np.eye(LB))
        odd = np.kron(np.cos(beta) - np.sin(beta), np.eye(LB))
        return even, odd

    zero = np.zeros((LANES, LANES))
    mixes.append(np.block([[mix(0)[0], zero], [zero, mix(6)[0]]]))
    for m in range(1, 6):
        here, there = mix(m), mix(12 - m)
        mixes.append(np.block([[here[0], there[0]], [here[1], -there[1]]]))
    mixes = np.stack(mixes)
    return dict(
        z_out=halves(scaled[order, :]),
        y_out=halves(cas[:, order]),
        y_in=halves(cas[order, :]),
        z_in=halves(scaled[:, order]),
        mix=halves(mixes),
        mix_t=halves(np.swapaxes(mixes, 1, 2)),
    )


ROOT3 = math.sqrt(3.0) / 2.0


def cos12(e):
    a0, a1, a2 = e[0] + e[6], e[1] + e[5], e[2] + e[4]
    b0, b1, b2 = e[0] - e[6], e[1] - e[5], e[2] - e[4]
    t = ROOT3 * b1
    h = b0 + 0.5 * b2
    r = 0.5 * (a1 + a2)
    d = 0.5 * (a1 - a2)
    return [
        a0 + a1 + a2 + e[3],
        h + t,
        a0 + d - e[3],
        b0 - b2,
        a0 - r + e[3],
        h - t,
        a0 - a1 + a2 - e[3],
    ]


def sin12(o):
    p1, p2 = o[1] + o[5], o[2] + o[4]
    r1, r2 = o[1] - o[5], o[2] - o[4]
    h = 0.5 * p1 + o[3]
    t = ROOT3 * p2
    return [None, h + t, ROOT3 * (r1 + r2), p1 - o[3], ROOT3 * (r1 - r2), h - t]


def split(values):
    high = values.astype(bf16)
    return high, (values - high.astype(f32)).astype(bf16)


def dot(a, b):
    return jnp.dot(a, b, preferred_element_type=f32)


def dot3(a, b):
    return dot(a[0], b[0]) + (dot(a[0], b[1]) + dot(a[1], b[0]))


def lane_bit(shape, bit):
    return (lax.broadcasted_iota(jnp.int32, shape, 1) & bit) == 0


def gather_groups(parts, shape):
    for width in (16, 32, 64):
        first = lane_bit(shape, width)
        parts = [
            jnp.where(first, a, b) + pltpu.roll(jnp.where(first, b, a), width, 1)
            for a, b in zip(parts[0::2], parts[1::2])
        ]
    return parts[0]


def spread_groups(value, shape):
    parts = [value]
    for width in (64, 32, 16):
        first = lane_bit(shape, width)
        turned = [pltpu.roll(part, width, 1) for part in parts]
        parts = [
            side
            for part, turn in zip(parts, turned)
            for side in (jnp.where(first, part, turn), jnp.where(first, turn, part))
        ]
    return parts


def lines(ref, start):
    return jnp.concatenate([ref[pl.ds(row, PW, stride=BLK), :] for row in start], axis=0)


def source_masks():
    group = lax.broadcasted_iota(jnp.int32, (1, LANES), 1) // LB
    return [group == s for s in range(BD)]


def scatter_kernel(cells, recv, zh, zl, mh, ml, sent0, sent1, dense, turned, fields, bh, bl):
    zero = jnp.zeros((256, LANES), f32)

    def clear(i, carry):
        dense[pl.ds(pl.multiple_of(i * 256, 256), 256), :] = zero
        return carry

    lax.fori_loop(0, SLAB // 256, clear, 0)

    def turn(i, carry):
        at = pl.multiple_of(i * LANES, LANES)
        turned[pl.ds(at, LANES), :] = recv[:, pl.ds(at, LANES)].T
        return carry

    lax.fori_loop(0, KW // LANES, turn, 0)
    masks = source_masks()

    def place(i, carry):
        for j in range(8):
            k = i * 8 + j
            row = turned[pl.ds(k, 1), :]
            for s in range(BD):
                cell = cells[s * KW + k]
                pltpu.store(dense.at[pl.ds(cell, 1), :], row, mask=masks[s])
        return carry

    lax.fori_loop(0, KW // 8, place, 0)
    table = (zh[...], zl[...])

    def along_z(i, carry):
        y, quad = i // 3, i % 3
        folded = []
        for side in range(4):
            base = (y * G + (quad * 4 + side) * 8) * G
            tiles = []
            for r in range(0, G, 8):
                parts = [dense[pl.ds(pl.multiple_of(base + xl * G + r, 8), 8), :] for xl in range(8)]
                tiles.append(gather_groups(parts, (8, LANES)))
            folded.append(jnp.concatenate(tiles, axis=0))
        out = dot3(table, split(jnp.concatenate(folded, axis=1)))
        at = pl.multiple_of(y * G, G)
        for side in range(4):
            fields[quad * 4 + side, pl.ds(at, G), :] = out[:, side * LANES : (side + 1) * LANES]
        return carry

    lax.fori_loop(0, GY * 3, along_z, 0)

    def twelve(i, carry):
        at = pl.multiple_of(i * 16, 16)
        e = [fields[xh, pl.ds(at, 16), :] for xh in range(12)]
        c = cos12([e[0]] + [e[j] + e[12 - j] for j in range(1, 6)] + [e[6]])
        s = sin12([None] + [e[j] - e[12 - j] for j in range(1, 6)])
        for p in range(6):
            high, low = split(jnp.concatenate([c[p], c[6] if p == 0 else s[p]], axis=1))
            bh[p, pl.ds(at, 16), :] = high
            bl[p, pl.ds(at, 16), :] = low
        return carry

    lax.fori_loop(0, GY * G // 16, twelve, 0)

    sent = (sent0, sent1)

    def along_x(y, carry):
        at = pl.multiple_of(y * G, G)
        for p in range(6):
            data = (bh[p, pl.ds(at, G), :], bl[p, pl.ds(at, G), :])
            out = dot3(data, (mh[p], ml[p]))
            for side in range(2):
                for z in range(GY):
                    row = y * COLS + z * XB + p % PAIRS * 2 + side
                    sent[p // PAIRS][pl.ds(row, PW, stride=BLK), :] = out[
                        z * PW : (z + 1) * PW, side * LANES : (side + 1) * LANES
                    ]
        return carry

    lax.fori_loop(0, GY, along_x, 0)


def density_kernel(recv, yh, yl, pack0, pack1, share, *rest):
    fields, sums = rest[-2:]
    table = (yh[...], yl[...])
    weight = share[...]

    def along_y(z, carry):
        data = [lines(recv, [y * COLS + z * XB + i for y in range(GY)]) for i in range(XB)]
        out = dot3(table, split(jnp.concatenate(data, axis=1)))
        for i in range(XB):
            at = pl.multiple_of((z * XB + i) * G, G)
            fields[pl.ds(at, G), :] = out[:, i * LANES : (i + 1) * LANES]
        high, low = split(weight * out * out)
        first, second = pack0[...], pack1[...]
        added = dot(high[:HALF], first) + dot(low[:HALF], first)
        added = added + (dot(high[HALF:], second) + dot(low[HALF:], second))
        sums[pl.ds(pl.multiple_of(z * HALF, HALF), HALF), :] = added
        return carry

    lax.fori_loop(0, GY, along_y, 0)


def potential_kernel(density, external, fields, yh, yl, open0, open1, sent):
    table = (yh[...], yl[...])

    def along_y(z, carry):
        at = pl.multiple_of(z * HALF, HALF)
        dens = density[pl.ds(at, HALF), :]
        root = jnp.exp(jnp.log(dens) * (1.0 / 3.0))
        root = root - (root - dens / (root * root)) * (1.0 / 3.0)
        high, low = split(external[pl.ds(at, HALF), :] - slater * root)
        first, second = open0[...], open1[...]
        spread = [dot(high, first) + dot(low, first), dot(high, second) + dot(low, second)]
        value = [fields[pl.ds(pl.multiple_of((z * XB + i) * G, G), G), :] for i in range(XB)]
        product = jnp.concatenate(spread, axis=0) * jnp.concatenate(value, axis=1)
        out = dot3(table, split(product))
        for i in range(XB):
            for y in range(GY):
                sent[pl.ds(y * COLS + z * XB + i, PW, stride=BLK), :] = out[
                    y * PW : (y + 1) * PW, i * LANES : (i + 1) * LANES
                ]
        return carry

    lax.fori_loop(0, GY, along_y, 0)


def gather_kernel(cells, recv0, recv1, zh, zl, mh, ml, terms, dense, turned, uv, bh, bl):
    table = (zh[...], zl[...])
    recv = (recv0, recv1)

    def along_x(y, carry):
        at = pl.multiple_of(y * G, G)
        for p in range(6):
            first = p % PAIRS * 2
            data = [
                lines(recv[p // PAIRS], [y * COLS + z * XB + first + side for z in range(GY)]) for side in range(2)
            ]
            uv[p, pl.ds(at, G), :] = dot3(split(jnp.concatenate(data, axis=1)), (mh[p], ml[p]))
        return carry

    lax.fori_loop(0, GY, along_x, 0)

    def twelve(i, carry):
        at = pl.multiple_of(i * 16, 16)
        u = [uv[p, pl.ds(at, 16), :LANES] for p in range(6)] + [uv[0, pl.ds(at, 16), LANES:]]
        v = [None] + [uv[p, pl.ds(at, 16), LANES:] for p in range(1, 6)]
        c, s = cos12(u), sin12(v)
        x = [c[0]] + [c[j] + s[j] for j in range(1, 6)] + [c[6]] + [c[j] - s[j] for j in range(5, 0, -1)]
        for quad in range(3):
            high, low = split(jnp.concatenate(x[4 * quad : 4 * quad + 4], axis=1))
            bh[quad, pl.ds(at, 16), :] = high
            bl[quad, pl.ds(at, 16), :] = low
        return carry

    lax.fori_loop(0, GY * G // 16, twelve, 0)

    def along_z(i, carry):
        y, quad = i // 3, i % 3
        at = pl.multiple_of(y * G, G)
        out = dot3(table, (bh[quad, pl.ds(at, G), :], bl[quad, pl.ds(at, G), :]))
        for side in range(4):
            base = (y * G + (quad * 4 + side) * 8) * G
            for r in range(0, G, 8):
                copies = spread_groups(out[r : r + 8, side * LANES : (side + 1) * LANES], (8, LANES))
                for xl in range(8):
                    dense[pl.ds(pl.multiple_of(base + xl * G + r, 8), 8), :] = copies[xl]
        return carry

    lax.fori_loop(0, GY * 3, along_z, 0)
    masks = source_masks()

    def pick(i, carry):
        for j in range(8):
            k = i * 8 + j
            row = dense[pl.ds(cells[k], 1), :]
            for s in range(1, BD):
                row = jnp.where(masks[s], dense[pl.ds(cells[s * KW + k], 1), :], row)
            turned[pl.ds(k, 1), :] = row
        return carry

    lax.fori_loop(0, KW // 8, pick, 0)

    def turn(i, carry):
        at = pl.multiple_of(i * LANES, LANES)
        terms[:, pl.ds(at, LANES)] = turned[pl.ds(at, LANES), :].T
        return carry

    lax.fori_loop(0, KW // LANES, turn, 0)


def pullback_kernel(grads, s, y0, y1, y2, y3, z1, z2, z3, z4, t1, t2, t3, t4, out):
    def mul(a, b):
        return jnp.dot(a[...], b[...], precision=highest, preferred_element_type=f32)

    y, z, t = (y0, y1, y2, y3), (None, z1, z2, z3, z4), (None, t1, t2, t3, t4)
    values = s[...]
    squared = jnp.sum(values * values, keepdims=True)
    frob = jnp.sqrt(squared)
    root = jnp.sqrt(frob)
    given = grads[...]
    zb = given / root
    fb = -0.5 * jnp.sum(given * z4[...], keepdims=True) / (frob * root)
    yb = None
    for k in range(NS_ITERS, 0, -1):
        tb = zb if k == 1 else mul(zb, z[k - 1])
        if yb is not None:
            tb = tb + mul(y[k - 1], yb)
        before = tb if k == 1 else mul(z[k - 1], tb)
        before = -0.5 * before
        if yb is not None:
            before = before + mul(yb, t[k])
        if k > 1:
            zb = mul(t[k], zb) - 0.5 * mul(tb, y[k - 1])
        yb = before
    fb = fb - jnp.sum(yb * values, keepdims=True) / squared
    grad = yb / frob + fb * (values / frob)
    out[...] = (grad + grad.T) / NPW


def call(kernel, out_shapes, scratch, scalars, *operands, unread=()):
    vmem = pl.BlockSpec(memory_space=pltpu.VMEM)
    smem = pl.BlockSpec(memory_space=pltpu.SMEM)
    return pl.pallas_call(
        kernel,
        out_shape=out_shapes,
        in_specs=[smem] * scalars
        + [vmem] * (len(operands) - scalars)
        + [pl.BlockSpec(memory_space=pl.ANY)] * len(unread),
        out_specs=jax.tree.map(lambda _: vmem, out_shapes),
        scratch_shapes=scratch,
        compiler_params=pltpu.CompilerParams(vmem_limit_bytes=58 * 1024 * 1024),
    )(*operands, *unread)


def array(*shape):
    return jax.ShapeDtypeStruct(shape, f32)


def matmul(left_side, right_side):
    return jnp.dot(left_side, right_side, precision=highest, preferred_element_type=f32)


def loewdin(intersection):
    frob_norm = jnp.sqrt(jnp.sum(intersection * intersection))
    identity = jnp.eye(intersection.shape[0], dtype=f32)
    ys, zs, ts = [intersection / frob_norm], [], []
    for repeat in range(NS_ITERS):
        product = matmul(zs[-1], ys[-1]) if zs else ys[-1]
        ts.append(1.5 * identity - 0.5 * product)
        zs.append(matmul(ts[-1], zs[-1]) if zs else ts[-1])
        if repeat < NS_ITERS - 1:
            ys.append(matmul(ys[-1], ts[-1]))
    return zs[-1] / jnp.sqrt(frob_norm), (*ys, *zs, *ts)


def total(values):
    axes = ("pw", "band")
    pieces = lax.all_to_all(values, axes, split_axis=0, concat_axis=0, tiled=True)
    row = jnp.sum(pieces, axis=0, keepdims=True)
    copies = jnp.broadcast_to(row, values.shape)
    return lax.all_to_all(copies, axes, split_axis=0, concat_axis=0, tiled=True)


def band_total(values):
    values = values + lax.ppermute(values, "band", [(i, i ^ 1) for i in range(BD)])
    others = [lax.ppermute(values, "band", [(i, (i + 2 * step) % BD) for i in range(BD)]) for step in (1, 2, 3)]
    return values + ((others[0] + others[2]) + others[1])


def packings():
    chosen = np.zeros((PARTS, 2, G, LANES))
    packed = np.zeros((PARTS, 2, WIDE, LANES))
    for part in range(PARTS):
        blocks = [m for pair in BLOCKS[part * PAIRS : (part + 1) * PAIRS] for m in pair]
        for half in range(2):
            for i, m in enumerate(blocks):
                for q in range(BD):
                    lane = half * 64 + i * BD + q
                    chosen[part, half, m + 12 * q, lane] = 1
                    row = i * LANES + q * LB
                    packed[part, half, row : row + LB, lane] = 1
    return chosen, packed


def to_sums(planes, chosen):
    values = planes.reshape(GY, 2, HALF, G)
    packed = matmul(values[:, 0], chosen[0]) + matmul(values[:, 1], chosen[1])
    return packed.reshape(SUM_ROWS, LANES)


def from_sums(parts, chosen):
    halves_of_y = [
        sum(matmul(parts[part], chosen[part, half].T) for part in range(PARTS)).reshape(GY, 1, HALF, G)
        for half in range(2)
    ]
    return jnp.concatenate(halves_of_y, axis=1).reshape(GY, G * G)


def shards(coefficients, occupancy, kinetic, cell_map, potential_ext, core_density):
    table = tables()
    chosen, packed = packings()
    chosen = chosen.astype(np.float32)
    pack = packed[0].astype(ml_dtypes.bfloat16)
    unpack = np.swapaxes(pack, 1, 2)
    unused = (1.0 - chosen.sum(axis=(1, 2))).astype(np.float32)
    pw_pos = lax.axis_index("pw")
    band_pos = lax.axis_index("band")
    cells = cell_map - pw_pos * SLAB
    share = lax.dynamic_slice_in_dim(occupancy / NB, band_pos * LB, LB)
    share = jnp.tile(share, XB * BD).reshape(1, WIDE)
    core = [to_sums(core_density, chosen[part]) + unused[part] for part in range(PARTS)]
    external = [to_sums(potential_ext, chosen[part]) for part in range(PARTS)]

    intersection = total(matmul(coefficients, coefficients.T)) / NPW
    weights, iterates = loewdin(intersection)
    rotated = matmul(weights.T, coefficients)
    block = lax.all_to_all(rotated, "band", split_axis=0, concat_axis=0, tiled=True)
    sent = call(
        scatter_kernel,
        [array(ROWS, LANES)] * PARTS,
        [
            pltpu.VMEM((SLAB, LANES), f32),
            pltpu.VMEM((KW, LANES), f32),
            pltpu.VMEM((12, GY * G, LANES), f32),
            pltpu.VMEM((6, GY * G, 2 * LANES), bf16),
            pltpu.VMEM((6, GY * G, 2 * LANES), bf16),
        ],
        1,
        cells,
        block,
        *table["z_out"],
        *table["mix"],
    )
    exchange = functools.partial(lax.all_to_all, axis_name="pw", split_axis=0, concat_axis=0, tiled=True)
    density, returned, after = [], [], []
    for part in range(PARTS):
        received = exchange(sent[part])
        fields, sums = call(
            density_kernel,
            (array(ROWS, LANES), array(SUM_ROWS, LANES)),
            [],
            0,
            received,
            *table["y_out"],
            *pack,
            share,
            unread=after,
        )
        density.append(core[part] + band_total(sums))
        product = call(
            potential_kernel,
            array(ROWS, LANES),
            [],
            0,
            density[part],
            external[part],
            fields,
            *table["y_in"],
            *unpack,
        )
        after = [product]
        returned.append(exchange(product))
    terms = call(
        gather_kernel,
        array(NB, KW),
        [
            pltpu.VMEM((SLAB, LANES), f32),
            pltpu.VMEM((KW, LANES), f32),
            pltpu.VMEM((6, GY * G, 2 * LANES), f32),
            pltpu.VMEM((3, GY * G, 4 * LANES), bf16),
            pltpu.VMEM((3, GY * G, 4 * LANES), bf16),
        ],
        1,
        cells,
        *returned,
        *table["z_in"],
        *table["mix_t"],
    )
    row_term = lax.all_to_all(terms, "band", split_axis=0, concat_axis=0, tiled=True)
    grad_rotated = occupancy[:, None] * (kinetic[None, :] * rotated + row_term)
    grad_weights = total(matmul(coefficients, grad_rotated.T))
    grad_intersection = call(pullback_kernel, array(NB, NB), [], 0, grad_weights, intersection, *iterates)
    grad_coef = matmul(weights, grad_rotated) + matmul(grad_intersection, coefficients)
    return (grad_coef, from_sums(density, chosen))


def solution(mesh):
    placed = (
        P(None, ("pw", "band")),
        P(),
        P(("pw", "band")),
        P("pw"),
        P("pw", None),
        P("pw", None),
    )
    return jax.shard_map(
        shards,
        mesh=mesh,
        in_specs=placed,
        out_specs=(P(None, ("pw", "band")), P("pw", None)),
        check_vma=False,
    )
```

time: 447 us -> 371 us (0.83)
  Pallas kernels: 157 us -> 119 us
  blocking collectives: 125 us -> 93.6 us
  starting transfers between devices: 18.9 us -> 42.4 us
  local copies, waits for them, and re-layouts: 30.8 us -> 13.6 us
  waiting for transfers between devices: 73.3 us -> 67.5 us
  matrix products: 28.1 us -> 22.8 us
    pallas_call x4 -> x7, Pallas kernels: 157 us -> 119 us  [call(): pl.pallas_call(kernel, out_shape=out_shapes, in_specs=[smem] * scalars +...]
    all_to_all x1 -> x4, waiting for transfers between devices: 51.9 us -> 27.7 us  [the longest x1 19 us: shards(): lax.all_to_all(terms, 'band', split_axis=0, concat_axis=0, tiled=True)]
    all_to_all x1 -> x4, starting transfers between devices: 4.65 us -> 22.9 us  [the longest x1 6.93 us: shards(): returned.append(exchange(product))]
    all_to_all x2, blocking collectives: 74.8 us -> 58.8 us  [the longest x1 30.3 us: shards(): returned.append(exchange(product))]
    all_to_all x2 -> x1, blocking collectives: 36.1 us -> 20.9 us  [total(): lax.all_to_all(values, axes, split_axis=0, concat_axis=0, tiled=True)]
    reshape x8 -> x3, local copies, waits for them, and re-layouts: 15.7 us -> 4.54 us  [the longest x2 3.6 us: to_sums(): values = planes.reshape(GY, 2, HALF, G)]
    ppermute x3 -> x6, waiting for transfers between devices: 0.01 us -> 10.9 us  [band_total(): lax.ppermute(values, 'band', [(i, (i + 2 * step) % BD) for i in range(BD)])]
    transpose x3 -> x0, local copies, waits for them, and re-layouts: 8 us -> none  [the longest x2 4.84 us: to_sums(): planes.reshape(GY, G, BD, 12).transpose(0, 3, 1, 2)]
  transfers between devices with their start and end apart: 7 -> 14, of which waited for: 3 -> 10; matrix products, arithmetic and copies ran while one was open for 6% -> 6% of each run, Pallas kernels for 0% -> 6%
where the time goes in v2:
time: 371 us; the launch traced here: 370 us
  Pallas kernels  119 us (32%)
  blocking collectives  93.6 us (25%)
  waiting for transfers between devices  67.5 us (18%)
  starting transfers between devices  42.4 us (11%)
  matrix products  22.8 us (6%)
  local copies, waits for them, and re-layouts  13.6 us (4%)
  other arithmetic  9.12 us (2%)
    pallas_call x7, Pallas kernels, call(): pl.pallas_call(kernel, out_shape=out_shapes, in_specs=[smem] * scalars +...  119 us
    all_to_all x1, blocking collectives, shards(): returned.append(exchange(product))  30.3 us
    all_to_all x1, blocking collectives, shards(): received = exchange(sent[part])  28.5 us
    dot_general x26, matrix products, matmul(): jnp.dot(left_side, right_side, precision=highest, preferred_element_type=...  22.8 us
    all_to_all x1, blocking collectives, total(): lax.all_to_all(values, axes, split_axis=0, concat_axis=0, tiled=True)  20.9 us
    all_to_all x1, waiting for transfers between devices, shards(): lax.all_to_all(rotated, 'band', split_axis=0, concat_axis=0, tiled=True)  20.1 us
    all_to_all x1, waiting for transfers between devices, shards(): lax.all_to_all(terms, 'band', split_axis=0, concat_axis=0, tiled=True)  19 us
    all_to_all x1, blocking collectives, total(): return lax.all_to_all(copies, axes, split_axis=0, concat_axis=0, tiled=True)  13.9 us
  transfers between devices with their start and end apart: 14, of which 10 were waited for; matrix products, arithmetic and copies ran while one was open for 6% of the time, Pallas kernels for 6%

profile of v2, /device:TPU:1, one launch (start us, length us, event | category | flops | bytes accessed | tf_op | source)
XLA Modules:
  0.0 369.8 jit_solution(16223523418858092621)
XLA Ops:
  3.4 20.9 %all_to_all.99 = f32[128,1,128]{2,1,0:T(1,128)S(1)} all-to-all(f32[128,1,128]{2,1,0:T(1,128)S(1)} %bitcast.142), channel_id=1, replica_groups=mesh['pw'=16,'band'=8] {'pw','band'}, dimensions={0} | all-to-all | bytes 131072 | tf_op jit(solution)/shard_map/all_to_all | solution.py:410
  24.5 13.9 %all_to_all.100 = f32[128,1,128]{2,1,0:T(1,128)S(1)} all-to-all(f32[128,1,128]{2,1,0:T(1,128)S(1)} %broadcast_in_dim.4), channel_id=1, replica_groups=mesh['pw'=16,'band'=8] {'pw','band'}, dimensions={0} | all-to-all | bytes 131072 | tf_op jit(solution)/shard_map/all_to_all | solution.py:413
  44.0 2.6 fusion.24
  46.6 4.4 %all-to-all-start.2 = ((f32[8,16,3072]{2,1,0:T(8,128)}), f32[8,16,3072]{2,1,0:T(8,128)S(1)}, u32[]{:S(2)}, u32[]{:S(2)}) async-start(f32[8,16,3072]{2,1,0:T(8,128)} %bitcast.12), calls=%async_computation.2 | async-start | bytes 3145728 | tf_op jit(solution)/shard_map/all_to_all | solution.py:469
  51.7 20.1 %all-to-all-done.2 = f32[8,16,3072]{2,1,0:T(8,128)S(1)} async-done(((f32[8,16,3072]{2,1,0:T(8,128)}), f32[8,16,3072]{2,1,0:T(8,128)S(1)}, u32[]{:S(2)}, u32[]{:S(2)}) %all-to-all-start.2) | async-done | bytes 1572896 | tf_op jit(solution)/shard_map/all_to_all | solution.py:469
  72.9 47.1 %shard_map.383 = (f32[3456,128]{1,0:T(8,128)}, f32[3456,128]{1,0:T(8,128)}) custom-call(s32[24576]{0:T(1024)} %broadcast_subtract_fusion.cells, f32[128,3072]{1,0:T(8,128)} %bitcast.130, bf16[96,96]{1,0:T(8,128)(2,1)} %constant.85.clone.zh, bf16[96,96]{1,0:T(8,128)(2,1)} %constant.86.clone.zl, bf16[6,256,256]{2,1,0:T(8,128)(2,1)} %constant.87.clone.mh, ...), custom_call_target="tpu_custom_call" | custom-call | tf_op jit(solution)/shard_map/pallas_call | solution.py:375
  120.0 28.5 %all_to_all.101 = f32[16,216,128]{2,1,0:T(8,128)} all-to-all(f32[16,216,128]{2,1,0:T(8,128)} %bitcast.133), channel_id=1, replica_groups=mesh['pw'=16,'band'=8] {'pw'}, dimensions={0} | all-to-all | bytes 3538944 | tf_op jit(solution)/shard_map/all_to_all | solution.py:489
  148.6 3.8 %all-to-all-start.5 = ((f32[16,216,128]{2,1,0:T(8,128)}), f32[16,216,128]{2,1,0:T(8,128)S(1)}, u32[]{:S(2)}, u32[]{:S(2)}) async-start(f32[16,216,128]{2,1,0:T(8,128)} %bitcast.132), calls=%async_computation.5 | async-start | bytes 3538944 | tf_op jit(solution)/shard_map/all_to_all | solution.py:489
  159.3 5.8 %shard_map.384 = (f32[3456,128]{1,0:T(8,128)}, f32[288,128]{1,0:T(8,128)}) custom-call(f32[3456,128]{1,0:T(8,128)} %bitcast.126, bf16[96,96]{1,0:T(8,128)(2,1)} %constant.89.clone.yh, bf16[96,96]{1,0:T(8,128)(2,1)} %constant.90.clone.yl, bf16[768,128]{1,0:T(8,128)(2,1)} %constant.91.clone.pack0, bf16[768,128]{1,0:T(8,128)(2,1)} %constant.92.clone.pack1, ...), custom_call_target="tpu_custom_call" | custom-call | tf_op jit(solution)/shard_map/pallas_call | solution.py:375
  169.3 2.4 collective-permute-start.2
  172.6 2.6 collective-permute-done.1
  175.3 2.4 collective-permute-done.3
  178.4 6.1 %shard_map.385.rest_0_ = f32[3456,128]{1,0:T(8,128)} custom-call(f32[288,128]{1,0:T(8,128)} %fusion.5.density, f32[288,128]{1,0:T(8,128)} %bitcast.139, f32[3456,128]{1,0:T(8,128)} %get-tuple-element.10.fields, bf16[96,96]{1,0:T(8,128)(2,1)} %constant.93.clone.yh, bf16[96,96]{1,0:T(8,128)(2,1)} %constant.94.clone.yl, bf16[128,768]{1,0:T(8,128)(2,1)} %constant.95.clone.open0, ...), custom_call_target="tpu_custom_call" | custom-call | tf_op jit(solution)/shard_map/pallas_call | solution.py:375
  185.7 6.9 %all-to-all-start.4 = ((f32[16,216,128]{2,1,0:T(8,128)}), f32[16,216,128]{2,1,0:T(8,128)}, u32[]{:S(2)}, u32[]{:S(2)}) async-start(f32[16,216,128]{2,1,0:T(8,128)} %bitcast.125), calls=%async_computation.4 | async-start | bytes 3538944 | tf_op jit(solution)/shard_map/all_to_all | solution.py:514
  195.1 5.8 %shard_map.386 = (f32[3456,128]{1,0:T(8,128)}, f32[288,128]{1,0:T(8,128)}) custom-call(f32[3456,128]{1,0:T(8,128)} %bitcast.127, bf16[96,96]{1,0:T(8,128)(2,1)} %constant.89.clone.yh, bf16[96,96]{1,0:T(8,128)(2,1)} %constant.90.clone.yl, bf16[768,128]{1,0:T(8,128)(2,1)} %constant.91.clone.pack0, bf16[768,128]{1,0:T(8,128)(2,1)} %constant.92.clone.pack1, ...), custom_call_target="tpu_custom_call" | custom-call | tf_op jit(solution)/shard_map/pallas_call | solution.py:375
  200.8 2.2 collective-permute-start.4
  205.9 2.2 collective-permute-start.6
  211.7 4.2 %collective-permute-done.7 = f32[288,128]{1,0:T(8,128)S(1)} collective-permute-done((f32[288,128]{1,0:T(8,128)S(1)}, f32[288,128]{1,0:T(8,128)S(1)}, u32[]{:S(2)}, u32[]{:S(2)}) %collective-permute-start.7) | collective-permute-done | bytes 147488 | tf_op jit(solution)/shard_map/ppermute | solution.py:418
  216.6 6.1 %shard_map.387 = f32[3456,128]{1,0:T(8,128)} custom-call(f32[288,128]{1,0:T(8,128)} %fusion.4.density, f32[288,128]{1,0:T(8,128)} %bitcast.138, f32[3456,128]{1,0:T(8,128)} %get-tuple-element.13.fields, bf16[96,96]{1,0:T(8,128)(2,1)} %constant.93.clone.yh, bf16[96,96]{1,0:T(8,128)(2,1)} %constant.94.clone.yl, bf16[128,768]{1,0:T(8,128)(2,1)} %constant.95.clone.open0, ...), custom_call_target="tpu_custom_call" | custom-call | tf_op jit(solution)/shard_map/pallas_call | solution.py:375
  222.7 30.3 %all_to_all.102 = f32[16,216,128]{2,1,0:T(8,128)} all-to-all(f32[16,216,128]{2,1,0:T(8,128)} %bitcast.128), channel_id=1, replica_groups=mesh['pw'=16,'band'=8] {'pw'}, dimensions={0} | all-to-all | bytes 3538944 | tf_op jit(solution)/shard_map/all_to_all | solution.py:514
  253.0 43.8 %shard_map.388 = f32[128,3072]{1,0:T(8,128)} custom-call(s32[24576]{0:T(1024)} %broadcast_subtract_fusion.cells, f32[3456,128]{1,0:T(8,128)} %bitcast.21.recv0, f32[3456,128]{1,0:T(8,128)} %bitcast.129, bf16[96,96]{1,0:T(8,128)(2,1)} %constant.97.clone.zh, bf16[96,96]{1,0:T(8,128)(2,1)} %constant.98.clone.zl, bf16[6,256,256]{2,1,0:T(8,128)(2,1)} %constant.99.clone.mh, ...), custom_call_target="tpu_custom_call" | custom-call | tf_op jit(solution)/shard_map/pallas_call | solution.py:375
  296.9 6.9 %all-to-all-start.7 = ((f32[8,16,3072]{2,1,0:T(8,128)}), f32[8,16,3072]{2,1,0:T(8,128)}, u32[]{:S(2)}, u32[]{:S(2)}) async-start(f32[8,16,3072]{2,1,0:T(8,128)} %bitcast.131), calls=%async_computation.7 | async-start | bytes 3145728 | tf_op jit(solution)/shard_map/all_to_all | solution.py:531
  305.6 19.0 %all-to-all-done.7 = f32[8,16,3072]{2,1,0:T(8,128)} async-done(((f32[8,16,3072]{2,1,0:T(8,128)}), f32[8,16,3072]{2,1,0:T(8,128)}, u32[]{:S(2)}, u32[]{:S(2)}) %all-to-all-start.7) | async-done | bytes 1572896 | tf_op jit(solution)/shard_map/all_to_all | solution.py:531
  324.6 2.1 fusion
  326.8 2.0 convolution_bitcast_fusion
  330.4 5.2 %all-to-all-start.8 = ((f32[128,1,128]{2,1,0:T(1,128)}), f32[128,1,128]{2,1,0:T(1,128)}, u32[]{:S(2)}, u32[]{:S(2)}) async-start(f32[128,1,128]{2,1,0:T(1,128)} %copy.54), calls=%async_computation.8 | async-start | bytes 131072 | tf_op jit(solution)/shard_map/all_to_all | solution.py:410
  336.6 8.6 %all-to-all-done.8 = f32[128,1,128]{2,1,0:T(1,128)} async-done(((f32[128,1,128]{2,1,0:T(1,128)}), f32[128,1,128]{2,1,0:T(1,128)}, u32[]{:S(2)}, u32[]{:S(2)}) %all-to-all-start.8) | async-done | bytes 65568 | tf_op jit(solution)/shard_map/all_to_all | solution.py:410
  346.9 4.5 %all-to-all-start.9 = ((f32[128,1,128]{2,1,0:T(1,128)}), f32[128,1,128]{2,1,0:T(1,128)S(1)}, u32[]{:S(2)}, u32[]{:S(2)}) async-start(f32[128,1,128]{2,1,0:T(1,128)} %broadcast_in_dim.5), calls=%async_computation.9 | async-start | bytes 131072 | tf_op jit(solution)/shard_map/all_to_all | solution.py:413
  351.4 2.6 fusion.23
  354.0 7.0 %all-to-all-done.9 = f32[128,1,128]{2,1,0:T(1,128)S(1)} async-done(((f32[128,1,128]{2,1,0:T(1,128)}), f32[128,1,128]{2,1,0:T(1,128)S(1)}, u32[]{:S(2)}, u32[]{:S(2)}) %all-to-all-start.9) | async-done | bytes 65568 | tf_op jit(solution)/shard_map/all_to_all | solution.py:413
  361.6 4.1 %shard_map.389 = f32[128,128]{1,0:T(8,128)} custom-call(f32[128,128]{1,0:T(8,128)} %bitcast.143, f32[128,128]{1,0:T(8,128)} %multiply_bitcast_fusion.s, f32[128,128]{1,0:T(8,128)} %copy-done.7, f32[128,128]{1,0:T(8,128)} %copy-done.15, f32[128,128]{1,0:T(8,128)} %copy-done.10, f32[128,128]{1,0:T(8,128)} %copy-done.16, f32[128,128]{1,0:T(8,128)} %get-tuple-element.14.z1.t1, ...), custom_call_target="tpu_custom_call" | custom-call | tf_op jit(solution)/shard_map/pallas_call | solution.py:375
  365.7 4.1 %convolution_add_fusion = f32[128,3072]{1,0:T(8,128)} fusion(f32[128,3072]{1,0:T(8,128)} %fusion.23, f32[128,128]{1,0:T(8,128)} %shard_map.389, f32[128,3072]{1,0:T(8,128)S(1)} %copy-done), kind=kOutput, calls=%fused_computation | convolution fusion | flops 604372992 | bytes 4784128 | tf_op jit(solution)/shard_map/dot_general | solution.py:392
  (118 shorter events, 39.4 us)
Async XLA Ops:
  40.4 6.2 %copy-start.7 = (f32[128,128]{1,0:T(8,128)}, f32[128,128]{1,0:T(8,128)S(1)}, u32[]{:S(2)}) copy-start(f32[128,128]{1,0:T(8,128)S(1)} %get-tuple-element.15.y0) | copy-start | bytes 196612
  42.7 3.9 %copy-start.12 = (f32[128,128]{1,0:T(8,128)}, f32[128,128]{1,0:T(8,128)S(1)}, u32[]{:S(2)}) copy-start(f32[128,128]{1,0:T(8,128)S(1)} %fusion.32.z3) | copy-start | bytes 196612
  46.6 4.4 %copy-start.23 = (s32[24576]{0:T(1024)S(1)}, s32[24576]{0:T(1024)}, u32[]{:S(2)}) copy-start(s32[24576]{0:T(1024)} %param.43) | copy-start | bytes 294916
  46.6 25.1 %all-to-all-start.2 = ((f32[8,16,3072]{2,1,0:T(8,128)}), f32[8,16,3072]{2,1,0:T(8,128)S(1)}, u32[]{:S(2)}, u32[]{:S(2)}) async-start(f32[8,16,3072]{2,1,0:T(8,128)} %bitcast.12), calls=%async_computation.2 | async-start | bytes 3145728 | tf_op jit(solution)/shard_map/all_to_all | solution.py:469
  148.6 8.2 %copy-start.20 = (f32[96,128,1]{1,0,2:T(8,128)S(1)}, f32[96,128,1]{1,0,2:T(8,128)}, u32[]{:S(2)}) copy-start(f32[96,128,1]{1,0,2:T(8,128)} %constant.107) | copy-start | bytes 147460
  148.6 35.9 %all-to-all-start.5 = ((f32[16,216,128]{2,1,0:T(8,128)}), f32[16,216,128]{2,1,0:T(8,128)S(1)}, u32[]{:S(2)}, u32[]{:S(2)}) async-start(f32[16,216,128]{2,1,0:T(8,128)} %bitcast.132), calls=%async_computation.5 | async-start | bytes 3538944 | tf_op jit(solution)/shard_map/all_to_all | solution.py:489
  152.4 5.6 %copy-start.22 = (f32[96,128,1]{1,0,2:T(8,128)S(1)}, f32[96,128,1]{1,0,2:T(8,128)}, u32[]{:S(2)}) copy-start(f32[96,128,1]{1,0,2:T(8,128)} %constant.108) | copy-start | bytes 147460
  156.8 10.0 %copy-start.3 = (f32[6,2,48,96]{3,2,1,0:T(8,128)S(1)}, f32[6,2,48,96]{3,2,1,0:T(8,128)}, u32[]{:S(2)}) copy-start(f32[6,2,48,96]{3,2,1,0:T(8,128)} %reshape.86) | copy-start | bytes 663556
  159.2 18.4 %copy-start.29 = (f32[128]{0:T(128)S(1)}, f32[128]{0:T(128)}, u32[]{:S(2)}) copy-start(f32[128]{0:T(128)} %constant.82.clone) | copy-start | bytes 1540
  165.0 2.9 collective-permute-start
  168.9 6.3 %collective-permute-start.1 = (f32[288,128]{1,0:T(8,128)S(1)}, f32[288,128]{1,0:T(8,128)S(1)}, u32[]{:S(2)}, u32[]{:S(2)}) collective-permute-start(f32[288,128]{1,0:T(8,128)S(1)} %add.77), channel_id=1, source_target_pairs={{0,2},{1,3},{2,4},{3,5},{4,6},{5,7},{6,0},{7,1},{8,10},{9,11},{10,... | collective-permute-start | bytes 442376 | tf_op jit(solution)/shard_map/ppermute | solution.py:418
  169.3 6.0 %collective-permute-start.2 = (f32[288,128]{1,0:T(8,128)S(1)}, f32[288,128]{1,0:T(8,128)S(1)}, u32[]{:S(2)}, u32[]{:S(2)}) collective-permute-start(f32[288,128]{1,0:T(8,128)S(1)} %add.77), channel_id=1, source_target_pairs={{0,6},{1,7},{2,0},{3,1},{4,2},{5,3},{6,4},{7,5},{8,14},{9,15},{10,... | collective-permute-start | bytes 442376 | tf_op jit(solution)/shard_map/ppermute | solution.py:418
  171.6 6.0 %collective-permute-start.3 = (f32[288,128]{1,0:T(8,128)S(1)}, f32[288,128]{1,0:T(8,128)S(1)}, u32[]{:S(2)}, u32[]{:S(2)}) collective-permute-start(f32[288,128]{1,0:T(8,128)S(1)} %add.77), channel_id=1, source_target_pairs={{0,4},{1,5},{2,6},{3,7},{4,0},{5,1},{6,2},{7,3},{8,12},{9,13},{10,... | collective-permute-start | bytes 442376 | tf_op jit(solution)/shard_map/ppermute | solution.py:418
  184.5 8.2 %copy-start.19 = (f32[96,128,1]{1,0,2:T(8,128)S(1)}, f32[96,128,1]{1,0,2:T(8,128)}, u32[]{:S(2)}) copy-start(f32[96,128,1]{1,0,2:T(8,128)} %constant.109) | copy-start | bytes 147460
  184.5 9.4 %copy-start.21 = (f32[96,128,1]{1,0,2:T(8,128)S(1)}, f32[96,128,1]{1,0,2:T(8,128)}, u32[]{:S(2)}) copy-start(f32[96,128,1]{1,0,2:T(8,128)} %constant.110) | copy-start | bytes 147460
  185.7 37.0 %all-to-all-start.4 = ((f32[16,216,128]{2,1,0:T(8,128)}), f32[16,216,128]{2,1,0:T(8,128)}, u32[]{:S(2)}, u32[]{:S(2)}) async-start(f32[16,216,128]{2,1,0:T(8,128)} %bitcast.125), calls=%async_computation.4 | async-start | bytes 3538944 | tf_op jit(solution)/shard_map/all_to_all | solution.py:514
  195.1 8.0 %copy-start.4 = (f32[6,2,48,96]{3,2,1,0:T(8,128)S(1)}, f32[6,2,48,96]{3,2,1,0:T(8,128)}, u32[]{:S(2)}) copy-start(f32[6,2,48,96]{3,2,1,0:T(8,128)} %reshape.86) | copy-start | bytes 663556
  200.8 3.4 collective-permute-start.4
  205.2 6.5 %collective-permute-start.5 = (f32[288,128]{1,0:T(8,128)S(1)}, f32[288,128]{1,0:T(8,128)S(1)}, u32[]{:S(2)}, u32[]{:S(2)}) collective-permute-start(f32[288,128]{1,0:T(8,128)S(1)} %add.86), channel_id=1, source_target_pairs={{0,2},{1,3},{2,4},{3,5},{4,6},{5,7},{6,0},{7,1},{8,10},{9,11},{10,... | collective-permute-start | bytes 442376 | tf_op jit(solution)/shard_map/ppermute | solution.py:418
  205.9 5.8 %collective-permute-start.6 = (f32[288,128]{1,0:T(8,128)S(1)}, f32[288,128]{1,0:T(8,128)S(1)}, u32[]{:S(2)}, u32[]{:S(2)}) collective-permute-start(f32[288,128]{1,0:T(8,128)S(1)} %add.86), channel_id=1, source_target_pairs={{0,6},{1,7},{2,0},{3,1},{4,2},{5,3},{6,4},{7,5},{8,14},{9,15},{10,... | collective-permute-start | bytes 442376 | tf_op jit(solution)/shard_map/ppermute | solution.py:418
  208.0 7.9 %collective-permute-start.7 = (f32[288,128]{1,0:T(8,128)S(1)}, f32[288,128]{1,0:T(8,128)S(1)}, u32[]{:S(2)}, u32[]{:S(2)}) collective-permute-start(f32[288,128]{1,0:T(8,128)S(1)} %add.86), channel_id=1, source_target_pairs={{0,4},{1,5},{2,6},{3,7},{4,0},{5,1},{6,2},{7,3},{8,12},{9,13},{10,... | collective-permute-start | bytes 442376 | tf_op jit(solution)/shard_map/ppermute | solution.py:418
  296.8 7.6 %copy-start.5 = (f32[288,128]{1,0:T(8,128)S(1)}, f32[288,128]{1,0:T(8,128)}, u32[]{:S(2)}) copy-start(f32[288,128]{1,0:T(8,128)} %fusion.4.density) | copy-start | bytes 442372
  296.8 7.6 %copy-start.25 = (f32[128,96]{1,0:T(8,128)S(1)}, f32[128,96]{1,0:T(8,128)}, u32[]{:S(2)}) copy-start(f32[128,96]{1,0:T(8,128)} %constant.102.clone) | copy-start | bytes 147460
  296.8 7.9 %copy-start.24 = (f32[128,96]{1,0:T(8,128)S(1)}, f32[128,96]{1,0:T(8,128)}, u32[]{:S(2)}) copy-start(f32[128,96]{1,0:T(8,128)} %constant.104.clone) | copy-start | bytes 147460
  296.8 8.2 %copy-start.6 = (f32[288,128]{1,0:T(8,128)S(1)}, f32[288,128]{1,0:T(8,128)}, u32[]{:S(2)}) copy-start(f32[288,128]{1,0:T(8,128)} %fusion.5.density) | copy-start | bytes 442372
  296.8 8.2 %copy-start.27 = (f32[128,96]{1,0:T(8,128)S(1)}, f32[128,96]{1,0:T(8,128)}, u32[]{:S(2)}) copy-start(f32[128,96]{1,0:T(8,128)} %constant.101.clone) | copy-start | bytes 147460
  296.9 8.4 %copy-start.26 = (f32[128,96]{1,0:T(8,128)S(1)}, f32[128,96]{1,0:T(8,128)}, u32[]{:S(2)}) copy-start(f32[128,96]{1,0:T(8,128)} %constant.103.clone) | copy-start | bytes 147460
  296.9 27.8 %all-to-all-start.7 = ((f32[8,16,3072]{2,1,0:T(8,128)}), f32[8,16,3072]{2,1,0:T(8,128)}, u32[]{:S(2)}, u32[]{:S(2)}) async-start(f32[8,16,3072]{2,1,0:T(8,128)} %bitcast.131), calls=%async_computation.7 | async-start | bytes 3145728 | tf_op jit(solution)/shard_map/all_to_all | solution.py:531
  303.8 20.8 %copy-start.28 = (f32[3072]{0:T(1024)S(1)}, f32[3072]{0:T(1024)}, u32[]{:S(2)}) copy-start(f32[3072]{0:T(1024)} %param.42) | copy-start | bytes 36868
  328.8 22.5 %copy-start.14 = (f32[128,128]{1,0:T(8,128)S(1)}, f32[128,128]{1,0:T(8,128)}, u32[]{:S(2)}) copy-start(f32[128,128]{1,0:T(8,128)} %copy-done.13) | copy-start | bytes 196612
  330.4 14.8 %all-to-all-start.8 = ((f32[128,1,128]{2,1,0:T(1,128)}), f32[128,1,128]{2,1,0:T(1,128)}, u32[]{:S(2)}, u32[]{:S(2)}) async-start(f32[128,1,128]{2,1,0:T(1,128)} %copy.54), calls=%async_computation.8 | async-start | bytes 131072 | tf_op jit(solution)/shard_map/all_to_all | solution.py:410
  346.9 14.1 %all-to-all-start.9 = ((f32[128,1,128]{2,1,0:T(1,128)}), f32[128,1,128]{2,1,0:T(1,128)S(1)}, u32[]{:S(2)}, u32[]{:S(2)}) async-start(f32[128,1,128]{2,1,0:T(1,128)} %broadcast_in_dim.5), calls=%async_computation.9 | async-start | bytes 131072 | tf_op jit(solution)/shard_map/all_to_all | solution.py:413
  (13 other events, 18.5 us)

commit v3 on v2

--- a/solution.py
+++ b/solution.py
@@ -66,10 +66,10 @@
         mixes.append(np.block([[here[0], there[0]], [here[1], -there[1]]]))
     mixes = np.stack(mixes)
     return dict(
-        z_out=halves(scaled[order, :]),
-        y_out=halves(cas[:, order]),
-        y_in=halves(cas[order, :]),
-        z_in=halves(scaled[:, order]),
+        z_out=np.concatenate(halves(scaled[order, :])),
+        y_out=np.concatenate(halves(cas[:, order])),
+        y_in=np.concatenate(halves(cas[order, :])),
+        z_in=np.concatenate(halves(scaled[:, order])),
         mix=halves(mixes),
         mix_t=halves(np.swapaxes(mixes, 1, 2)),
     )
@@ -117,6 +117,12 @@
     return dot(a[0], b[0]) + (dot(a[0], b[1]) + dot(a[1], b[0]))
 
 
+def transform(table, b):
+    rows = table.shape[0] // 2
+    both = dot(table, b[0])
+    return both[:rows] + (dot(table[:rows], b[1]) + both[rows:])
+
+
 def lane_bit(shape, bit):
     return (lax.broadcasted_iota(jnp.int32, shape, 1) & bit) == 0
 
@@ -153,7 +159,8 @@
     return [group == s for s in range(BD)]
 
 
-def scatter_kernel(cells, recv, zh, zl, mh, ml, sent0, sent1, dense, turned, fields, bh, bl):
+def scatter_kernel(cells, recv, zt, mh, ml, *rest):
+    sent, (dense, turned, fields, bh, bl) = rest[-7:-5], rest[-5:]
     zero = jnp.zeros((256, LANES), f32)
 
     def clear(i, carry):
@@ -171,16 +178,16 @@
     masks = source_masks()
 
     def place(i, carry):
-        for j in range(8):
-            k = i * 8 + j
+        for j in range(16):
+            k = i * 16 + j
             row = turned[pl.ds(k, 1), :]
             for s in range(BD):
                 cell = cells[s * KW + k]
                 pltpu.store(dense.at[pl.ds(cell, 1), :], row, mask=masks[s])
         return carry
 
-    lax.fori_loop(0, KW // 8, place, 0)
-    table = (zh[...], zl[...])
+    lax.fori_loop(0, KW // 16, place, 0)
+    table = zt[...]
 
     def along_z(i, carry):
         y, quad = i // 3, i % 3
@@ -192,7 +199,7 @@
                 parts = [dense[pl.ds(pl.multiple_of(base + xl * G + r, 8), 8), :] for xl in range(8)]
                 tiles.append(gather_groups(parts, (8, LANES)))
             folded.append(jnp.concatenate(tiles, axis=0))
-        out = dot3(table, split(jnp.concatenate(folded, axis=1)))
+        out = transform(table, split(jnp.concatenate(folded, axis=1)))
         at = pl.multiple_of(y * G, G)
         for side in range(4):
             fields[quad * 4 + side, pl.ds(at, G), :] = out[:, side * LANES : (side + 1) * LANES]
@@ -213,32 +220,26 @@
 
     lax.fori_loop(0, GY * G // 16, twelve, 0)
 
-    sent = (sent0, sent1)
-
-    def along_x(y, carry):
-        at = pl.multiple_of(y * G, G)
-        for p in range(6):
-            data = (bh[p, pl.ds(at, G), :], bl[p, pl.ds(at, G), :])
-            out = dot3(data, (mh[p], ml[p]))
-            for side in range(2):
+    for p in range(6):
+        out = dot3((bh[p], bl[p]), (mh[p], ml[p]))
+        for side in range(2):
+            for y in range(GY):
                 for z in range(GY):
                     row = y * COLS + z * XB + p % PAIRS * 2 + side
+                    at = y * G + z * PW
                     sent[p // PAIRS][pl.ds(row, PW, stride=BLK), :] = out[
-                        z * PW : (z + 1) * PW, side * LANES : (side + 1) * LANES
+                        at : at + PW, side * LANES : (side + 1) * LANES
                     ]
-        return carry
-
-    lax.fori_loop(0, GY, along_x, 0)
-
-
-def density_kernel(recv, yh, yl, pack0, pack1, share, *rest):
+
+
+def density_kernel(recv, yt, pack0, pack1, share, *rest):
     fields, sums = rest[-2:]
-    table = (yh[...], yl[...])
+    table = yt[...]
     weight = share[...]
 
     def along_y(z, carry):
         data = [lines(recv, [y * COLS + z * XB + i for y in range(GY)]) for i in range(XB)]
-        out = dot3(table, split(jnp.concatenate(data, axis=1)))
+        out = transform(table, split(jnp.concatenate(data, axis=1)))
         for i in range(XB):
             at = pl.multiple_of((z * XB + i) * G, G)
             fields[pl.ds(at, G), :] = out[:, i * LANES : (i + 1) * LANES]
@@ -252,8 +253,8 @@
     lax.fori_loop(0, GY, along_y, 0)
 
 
-def potential_kernel(density, external, fields, yh, yl, open0, open1, sent):
-    table = (yh[...], yl[...])
+def potential_kernel(density, external, fields, yt, open0, open1, sent):
+    table = yt[...]
 
     def along_y(z, carry):
         at = pl.multiple_of(z * HALF, HALF)
@@ -265,7 +266,7 @@
         spread = [dot(high, first) + dot(low, first), dot(high, second) + dot(low, second)]
         value = [fields[pl.ds(pl.multiple_of((z * XB + i) * G, G), G), :] for i in range(XB)]
         product = jnp.concatenate(spread, axis=0) * jnp.concatenate(value, axis=1)
-        out = dot3(table, split(product))
+        out = transform(table, split(product))
         for i in range(XB):
             for y in range(GY):
                 sent[pl.ds(y * COLS + z * XB + i, PW, stride=BLK), :] = out[
@@ -276,21 +277,14 @@
     lax.fori_loop(0, GY, along_y, 0)
 
 
-def gather_kernel(cells, recv0, recv1, zh, zl, mh, ml, terms, dense, turned, uv, bh, bl):
-    table = (zh[...], zl[...])
+def gather_kernel(cells, recv0, recv1, zt, mh, ml, terms, dense, turned, uv, bh, bl):
+    table = zt[...]
     recv = (recv0, recv1)
-
-    def along_x(y, carry):
-        at = pl.multiple_of(y * G, G)
-        for p in range(6):
-            first = p % PAIRS * 2
-            data = [
-                lines(recv[p // PAIRS], [y * COLS + z * XB + first + side for z in range(GY)]) for side in range(2)
-            ]
-            uv[p, pl.ds(at, G), :] = dot3(split(jnp.concatenate(data, axis=1)), (mh[p], ml[p]))
-        return carry
-
-    lax.fori_loop(0, GY, along_x, 0)
+    for p in range(6):
+        first = p % PAIRS * 2
+        starts = [y * COLS + z * XB + first for y in range(GY) for z in range(GY)]
+        data = [lines(recv[p // PAIRS], [row + side for row in starts]) for side in range(2)]
+        uv[p] = dot3(split(jnp.concatenate(data, axis=1)), (mh[p], ml[p]))
 
     def twelve(i, carry):
         at = pl.multiple_of(i * 16, 16)
@@ -309,7 +303,7 @@
     def along_z(i, carry):
         y, quad = i // 3, i % 3
         at = pl.multiple_of(y * G, G)
-        out = dot3(table, (bh[quad, pl.ds(at, G), :], bl[quad, pl.ds(at, G), :]))
+        out = transform(table, (bh[quad, pl.ds(at, G), :], bl[quad, pl.ds(at, G), :]))
         for side in range(4):
             base = (y * G + (quad * 4 + side) * 8) * G
             for r in range(0, G, 8):
@@ -322,15 +316,15 @@
     masks = source_masks()
 
     def pick(i, carry):
-        for j in range(8):
-            k = i * 8 + j
+        for j in range(16):
+            k = i * 16 + j
             row = dense[pl.ds(cells[k], 1), :]
             for s in range(1, BD):
                 row = jnp.where(masks[s], dense[pl.ds(cells[s * KW + k], 1), :], row)
             turned[pl.ds(k, 1), :] = row
         return carry
 
-    lax.fori_loop(0, KW // 8, pick, 0)
+    lax.fori_loop(0, KW // 16, pick, 0)
 
     def turn(i, carry):
         at = pl.multiple_of(i * LANES, LANES)
@@ -340,7 +334,7 @@
     lax.fori_loop(0, KW // LANES, turn, 0)
 
 
-def pullback_kernel(grads, s, y0, y1, y2, y3, z1, z2, z3, z4, t1, t2, t3, t4, out):
+def pullback_kernel(grads, s, y0, y1, y2, y3, z1, z2, z3, z4, t1, t2, t3, t4, coefs, first, out):
     def mul(a, b):
         return jnp.dot(a[...], b[...], precision=highest, preferred_element_type=f32)
 
@@ -366,7 +360,25 @@
         yb = before
     fb = fb - jnp.sum(yb * values, keepdims=True) / squared
     grad = yb / frob + fb * (values / frob)
-    out[...] = (grad + grad.T) / NPW
+    both = split((grad + grad.T) / NPW)
+    for at in range(0, KW, 512):
+        part = pl.ds(at, 512)
+        out[:, part] = first[:, part] + dot3(both, split(coefs[:, part]))
+
+
+def products_kernel(terms, rotated, coefs, kinetic, occupancy, grads, sums):
+    added = jnp.zeros((NB, NB), f32)
+
+    def dot_t(a, b):
+        return lax.dot_general(a, b, (((1,), (1,)), ((), ())), preferred_element_type=f32)
+
+    for at in range(0, KW, 512):
+        part = pl.ds(at, 512)
+        value = occupancy[...] * (kinetic[:, part] * rotated[:, part] + terms[:, part])
+        grads[:, part] = value
+        a, b = split(coefs[:, part]), split(value)
+        added = added + (dot_t(a[0], b[0]) + (dot_t(a[0], b[1]) + dot_t(a[1], b[0])))
+    sums[...] = added
 
 
 def call(kernel, out_shapes, scratch, scalars, *operands, unread=()):
@@ -480,8 +492,9 @@
         1,
         cells,
         block,
-        *table["z_out"],
+        table["z_out"],
         *table["mix"],
+        unread=(*core, *external),
     )
     exchange = functools.partial(lax.all_to_all, axis_name="pw", split_axis=0, concat_axis=0, tiled=True)
     density, returned, after = [], [], []
@@ -493,7 +506,7 @@
             [],
             0,
             received,
-            *table["y_out"],
+            table["y_out"],
             *pack,
             share,
             unread=after,
@@ -507,7 +520,7 @@
             density[part],
             external[part],
             fields,
-            *table["y_in"],
+            table["y_in"],
             *unpack,
         )
         after = [product]
@@ -525,14 +538,26 @@
         1,
         cells,
         *returned,
-        *table["z_in"],
+        table["z_in"],
         *table["mix_t"],
     )
     row_term = lax.all_to_all(terms, "band", split_axis=0, concat_axis=0, tiled=True)
-    grad_rotated = occupancy[:, None] * (kinetic[None, :] * rotated + row_term)
-    grad_weights = total(matmul(coefficients, grad_rotated.T))
-    grad_intersection = call(pullback_kernel, array(NB, NB), [], 0, grad_weights, intersection, *iterates)
-    grad_coef = matmul(weights, grad_rotated) + matmul(grad_intersection, coefficients)
+    grad_rotated, partial = call(
+        products_kernel,
+        (array(NB, KW), array(NB, NB)),
+        [],
+        0,
+        row_term,
+        rotated,
+        coefficients,
+        kinetic.reshape(1, KW),
+        occupancy.reshape(NB, 1),
+    )
+    grad_weights = total(partial)
+    first = matmul(weights, grad_rotated)
+    grad_coef = call(
+        pullback_kernel, array(NB, KW), [], 0, grad_weights, intersection, *iterates, coefficients, first
+    )
     return (grad_coef, from_sums(density, chosen))
 
 

time: 371 us -> 354 us (0.954)
  blocking collectives: 93.6 us -> 58.9 us
  waiting for transfers between devices: 67.5 us -> 83.5 us
  starting transfers between devices: 42.4 us -> 56.9 us
  matrix products: 22.8 us -> 15.7 us
  local copies, waits for them, and re-layouts: 13.6 us -> 9.56 us
    all_to_all x2 -> x0, blocking collectives: 34.8 us -> none  [the longest x1 20.9 us: total(): lax.all_to_all(values, axes, split_axis=0, concat_axis=0, tiled=True)]
    all_to_all x1 -> x2, starting transfers between devices: 5.19 us -> 15.9 us  [total(): lax.all_to_all(values, axes, split_axis=0, concat_axis=0, tiled=True)]
    all_to_all x1 -> x2, waiting for transfers between devices: 7 us -> 16.1 us  [total(): return lax.all_to_all(copies, axes, split_axis=0, concat_axis=0, tiled=True)]
    all_to_all x1 -> x2, waiting for transfers between devices: 8.61 us -> 15.9 us  [total(): lax.all_to_all(values, axes, split_axis=0, concat_axis=0, tiled=True)]
    dot_general x26 -> x24, matrix products: 22.8 us -> 15.7 us  [matmul(): jnp.dot(left_side, right_side, precision=highest, preferred_element_type=...]
    all_to_all x1 -> x2, starting transfers between devices: 4.47 us -> 9 us  [total(): return lax.all_to_all(copies, axes, split_axis=0, concat_axis=0, tiled=True)]
    pallas_call x7 -> x8, Pallas kernels: 119 us -> 119 us  [call(): pl.pallas_call(kernel, out_shape=out_shapes, in_specs=[smem] * scalars +...]
  transfers between devices with their start and end apart: 14 -> 16, of which waited for: 10 -> 12; matrix products, arithmetic and copies ran while one was open for 6% -> 4% of each run, Pallas kernels for 6% -> 7%
where the time goes in v3:
time: 354 us; the launch traced here: 353 us
  Pallas kernels  119 us (34%)
  waiting for transfers between devices  83.5 us (24%)
  blocking collectives  58.9 us (17%)
  starting transfers between devices  56.9 us (16%)
  matrix products  15.7 us (4%)
  local copies, waits for them, and re-layouts  9.56 us (3%)
  other arithmetic  6.88 us (2%)
    pallas_call x8, Pallas kernels, call(): pl.pallas_call(kernel, out_shape=out_shapes, in_specs=[smem] * scalars +...  119 us
    all_to_all x1, blocking collectives, shards(): returned.append(exchange(product))  30.3 us
    all_to_all x1, blocking collectives, shards(): received = exchange(sent[part])  28.5 us
    all_to_all x1, waiting for transfers between devices, shards(): lax.all_to_all(terms, 'band', split_axis=0, concat_axis=0, tiled=True)  18.2 us
    all_to_all x1, waiting for transfers between devices, shards(): lax.all_to_all(rotated, 'band', split_axis=0, concat_axis=0, tiled=True)  18.1 us
    all_to_all x2, waiting for transfers between devices, total(): return lax.all_to_all(copies, axes, split_axis=0, concat_axis=0, tiled=True)  16.1 us
    all_to_all x2, waiting for transfers between devices, total(): lax.all_to_all(values, axes, split_axis=0, concat_axis=0, tiled=True)  15.9 us
    all_to_all x2, starting transfers between devices, total(): lax.all_to_all(values, axes, split_axis=0, concat_axis=0, tiled=True)  15.9 us
  transfers between devices with their start and end apart: 16, of which 12 were waited for; matrix products, arithmetic and copies ran while one was open for 4% of the time, Pallas kernels for 7%

profile of v3, /device:TPU:1, one launch (start us, length us, event | category | flops | bytes accessed | tf_op | source)
XLA Modules:
  0.0 352.8 jit_solution(8993292900556483577)
XLA Ops:
  0.7 4.0 %fusion.27 = f32[128,128]{1,0:T(8,128)} fusion(f32[128,3072]{1,0:T(8,128)} %coefs.3), kind=kOutput, calls=%fused_computation.54 | convolution fusion | flops 603979776 | bytes 1638400 | tf_op jit(solution)/shard_map/dot_general | solution.py:404
  4.7 11.5 %all-to-all-start = ((f32[128,1,128]{2,1,0:T(1,128)}), f32[128,1,128]{2,1,0:T(1,128)S(1)}, u32[]{:S(2)}, u32[]{:S(2)}) async-start(f32[128,1,128]{2,1,0:T(1,128)} %bitcast.7), calls=%async_computation | async-start | bytes 131072 | tf_op jit(solution)/shard_map/all_to_all | solution.py:422
  18.6 7.2 %all-to-all-done = f32[128,1,128]{2,1,0:T(1,128)S(1)} async-done(((f32[128,1,128]{2,1,0:T(1,128)}), f32[128,1,128]{2,1,0:T(1,128)S(1)}, u32[]{:S(2)}, u32[]{:S(2)}) %all-to-all-start) | async-done | bytes 65568 | tf_op jit(solution)/shard_map/all_to_all | solution.py:422
  26.5 4.5 %all-to-all-start.1 = ((f32[128,1,128]{2,1,0:T(1,128)}), f32[128,1,128]{2,1,0:T(1,128)S(1)}, u32[]{:S(2)}, u32[]{:S(2)}) async-start(f32[128,1,128]{2,1,0:T(1,128)} %broadcast_in_dim.4), calls=%async_computation.1 | async-start | bytes 131072 | tf_op jit(solution)/shard_map/all_to_all | solution.py:425
  31.4 9.2 %all-to-all-done.1 = f32[128,1,128]{2,1,0:T(1,128)S(1)} async-done(((f32[128,1,128]{2,1,0:T(1,128)}), f32[128,1,128]{2,1,0:T(1,128)S(1)}, u32[]{:S(2)}, u32[]{:S(2)}) %all-to-all-start.1) | async-done | bytes 65568 | tf_op jit(solution)/shard_map/all_to_all | solution.py:425
  45.8 2.6 fusion.21.rotated
  48.4 4.4 %all-to-all-start.2 = ((f32[8,16,3072]{2,1,0:T(8,128)}), f32[8,16,3072]{2,1,0:T(8,128)S(1)}, u32[]{:S(2)}, u32[]{:S(2)}) async-start(f32[8,16,3072]{2,1,0:T(8,128)} %bitcast.12), calls=%async_computation.2 | async-start | bytes 3145728 | tf_op jit(solution)/shard_map/all_to_all | solution.py:481
  55.5 18.1 %all-to-all-done.2 = f32[8,16,3072]{2,1,0:T(8,128)S(1)} async-done(((f32[8,16,3072]{2,1,0:T(8,128)}), f32[8,16,3072]{2,1,0:T(8,128)S(1)}, u32[]{:S(2)}, u32[]{:S(2)}) %all-to-all-start.2) | async-done | bytes 1572896 | tf_op jit(solution)/shard_map/all_to_all | solution.py:481
  74.8 44.2 %shard_map.347 = (f32[3456,128]{1,0:T(8,128)}, f32[3456,128]{1,0:T(8,128)}) custom-call(s32[24576]{0:T(1024)} %broadcast_subtract_fusion.cells, f32[128,3072]{1,0:T(8,128)} %bitcast.126, bf16[192,96]{1,0:T(8,128)(2,1)} %constant.77.clone.zt, bf16[6,256,256]{2,1,0:T(8,128)(2,1)} %constant.78.clone.mh, bf16[6,256,256]{2,1,0:T(8,128)(2,1)} %constant.79.clone.ml, ...), custom_call_target="tpu_custom_call" | custom-call | tf_op jit(solution)/shard_map/pallas_call | solution.py:387
  118.9 28.5 %all_to_all.98 = f32[16,216,128]{2,1,0:T(8,128)} all-to-all(f32[16,216,128]{2,1,0:T(8,128)} %bitcast.128), channel_id=1, replica_groups=mesh['pw'=16,'band'=8] {'pw'}, dimensions={0} | all-to-all | bytes 3538944 | tf_op jit(solution)/shard_map/all_to_all | solution.py:502
  147.5 3.8 %all-to-all-start.5 = ((f32[16,216,128]{2,1,0:T(8,128)}), f32[16,216,128]{2,1,0:T(8,128)S(1)}, u32[]{:S(2)}, u32[]{:S(2)}) async-start(f32[16,216,128]{2,1,0:T(8,128)} %bitcast.28), calls=%async_computation.5 | async-start | bytes 3538944 | tf_op jit(solution)/shard_map/all_to_all | solution.py:502
  152.1 5.7 %shard_map.348 = (f32[3456,128]{1,0:T(8,128)}, f32[288,128]{1,0:T(8,128)}) custom-call(f32[3456,128]{1,0:T(8,128)} %bitcast.120, bf16[192,96]{1,0:T(8,128)(2,1)} %constant.80.clone.yt, bf16[768,128]{1,0:T(8,128)(2,1)} %constant.81.clone.pack0, bf16[768,128]{1,0:T(8,128)(2,1)} %constant.82.clone.pack1, f32[1,768]{1,0:T(1,128)} %reshape_tile.3.share), custom_call_target="tpu_custom_call" | custom-call | tf_op jit(solution)/shard_map/pallas_call | solution.py:387
  162.0 2.4 collective-permute-start.2
  164.4 3.6 %collective-permute-done.1 = f32[288,128]{1,0:T(8,128)S(1)} collective-permute-done((f32[288,128]{1,0:T(8,128)S(1)}, f32[288,128]{1,0:T(8,128)S(1)}, u32[]{:S(2)}, u32[]{:S(2)}) %collective-permute-start.1) | collective-permute-done | bytes 147488 | tf_op jit(solution)/shard_map/ppermute | solution.py:430
  168.0 2.4 collective-permute-done.3
  171.1 6.1 %shard_map.349.rest_0_ = f32[3456,128]{1,0:T(8,128)} custom-call(f32[288,128]{1,0:T(8,128)} %add_add_fusion.1.density, f32[288,128]{1,0:T(8,128)} %bitcast.132, f32[3456,128]{1,0:T(8,128)} %get-tuple-element.12.fields, bf16[192,96]{1,0:T(8,128)(2,1)} %constant.83.clone.yt, bf16[128,768]{1,0:T(8,128)(2,1)} %constant.84.clone.open0, ...), custom_call_target="tpu_custom_call" | custom-call | tf_op jit(solution)/shard_map/pallas_call | solution.py:387
  178.4 6.9 %all-to-all-start.4 = ((f32[16,216,128]{2,1,0:T(8,128)}), f32[16,216,128]{2,1,0:T(8,128)S(1)}, u32[]{:S(2)}, u32[]{:S(2)}) async-start(f32[16,216,128]{2,1,0:T(8,128)} %bitcast.119), calls=%async_computation.4 | async-start | bytes 3538944 | tf_op jit(solution)/shard_map/all_to_all | solution.py:527
  185.3 5.7 %shard_map.350 = (f32[3456,128]{1,0:T(8,128)}, f32[288,128]{1,0:T(8,128)}) custom-call(f32[3456,128]{1,0:T(8,128)} %bitcast.121, bf16[192,96]{1,0:T(8,128)(2,1)} %constant.80.clone.yt, bf16[768,128]{1,0:T(8,128)(2,1)} %constant.81.clone.pack0, bf16[768,128]{1,0:T(8,128)(2,1)} %constant.82.clone.pack1, f32[1,768]{1,0:T(1,128)} %reshape_tile.3.share, ...), custom_call_target="tpu_custom_call" | custom-call | tf_op jit(solution)/shard_map/pallas_call | solution.py:387
  199.3 2.4 collective-permute-done.5
  201.8 4.3 %collective-permute-done.7 = f32[288,128]{1,0:T(8,128)S(1)} collective-permute-done((f32[288,128]{1,0:T(8,128)S(1)}, f32[288,128]{1,0:T(8,128)S(1)}, u32[]{:S(2)}, u32[]{:S(2)}) %collective-permute-start.7) | collective-permute-done | bytes 147488 | tf_op jit(solution)/shard_map/ppermute | solution.py:430
  206.8 6.0 %shard_map.351 = f32[3456,128]{1,0:T(8,128)} custom-call(f32[288,128]{1,0:T(8,128)} %add_add_fusion.density, f32[288,128]{1,0:T(8,128)} %bitcast.130, f32[3456,128]{1,0:T(8,128)} %get-tuple-element.15.fields, bf16[192,96]{1,0:T(8,128)(2,1)} %constant.83.clone.yt, bf16[128,768]{1,0:T(8,128)(2,1)} %constant.84.clone.open0, bf16[128,768]{1,0:T(8,128)(2,1)} %constant.85.clone.open1), custom_call_target="tpu_custom_call" | custom-call | tf_op jit(solution)/shard_map/pallas_call | solution.py:387
  212.8 30.3 %all_to_all.99 = f32[16,216,128]{2,1,0:T(8,128)} all-to-all(f32[16,216,128]{2,1,0:T(8,128)} %bitcast.122), channel_id=1, replica_groups=mesh['pw'=16,'band'=8] {'pw'}, dimensions={0} | all-to-all | bytes 3538944 | tf_op jit(solution)/shard_map/all_to_all | solution.py:527
  243.2 41.3 %shard_map.352 = f32[128,3072]{1,0:T(8,128)} custom-call(s32[24576]{0:T(1024)} %broadcast_subtract_fusion.cells, f32[3456,128]{1,0:T(8,128)} %bitcast.123, f32[3456,128]{1,0:T(8,128)} %bitcast.124, bf16[192,96]{1,0:T(8,128)(2,1)} %constant.86.clone.zt, bf16[6,256,256]{2,1,0:T(8,128)(2,1)} %constant.87.clone.mh, bf16[6,256,256]{2,1,0:T(8,128)(2,1)} %constant.88.clone.ml), custom_call_target="tpu_custom_call" | custom-call | tf_op jit(solution)/shard_map/pallas_call | solution.py:387
  284.5 6.2 %all-to-all-start.7 = ((f32[8,16,3072]{2,1,0:T(8,128)}), f32[8,16,3072]{2,1,0:T(8,128)S(1)}, u32[]{:S(2)}, u32[]{:S(2)}) async-start(f32[8,16,3072]{2,1,0:T(8,128)} %bitcast.127), calls=%async_computation.7 | async-start | bytes 3145728 | tf_op jit(solution)/shard_map/all_to_all | solution.py:544
  293.3 18.2 %all-to-all-done.7 = f32[8,16,3072]{2,1,0:T(8,128)S(1)} async-done(((f32[8,16,3072]{2,1,0:T(8,128)}), f32[8,16,3072]{2,1,0:T(8,128)S(1)}, u32[]{:S(2)}, u32[]{:S(2)}) %all-to-all-start.7) | async-done | bytes 1572896 | tf_op jit(solution)/shard_map/all_to_all | solution.py:544
  312.7 4.1 %shard_map.353 = (f32[128,3072]{1,0:T(8,128)}, f32[128,128]{1,0:T(8,128)}) custom-call(f32[128,3072]{1,0:T(8,128)} %bitcast.125, f32[128,3072]{1,0:T(8,128)} %fusion.21.rotated, f32[128,3072]{1,0:T(8,128)} %coefs.3, f32[1,3072]{1,0:T(1,128)} %bitcast.141, f32[128,1]{1,0:T(8,128)} %copy.52.occupancy), custom_call_target="tpu_custom_call" | custom-call | tf_op jit(solution)/shard_map/pallas_call | solution.py:387
  316.7 4.4 %all-to-all-start.8 = ((f32[128,1,128]{2,1,0:T(1,128)}), f32[128,1,128]{2,1,0:T(1,128)S(1)}, u32[]{:S(2)}, u32[]{:S(2)}) async-start(f32[128,1,128]{2,1,0:T(1,128)} %bitcast.140), calls=%async_computation.8 | async-start | bytes 131072 | tf_op jit(solution)/shard_map/all_to_all | solution.py:422
  322.1 8.7 %all-to-all-done.8 = f32[128,1,128]{2,1,0:T(1,128)S(1)} async-done(((f32[128,1,128]{2,1,0:T(1,128)}), f32[128,1,128]{2,1,0:T(1,128)S(1)}, u32[]{:S(2)}, u32[]{:S(2)}) %all-to-all-start.8) | async-done | bytes 65568 | tf_op jit(solution)/shard_map/all_to_all | solution.py:422
  331.7 4.5 %all-to-all-start.9 = ((f32[128,1,128]{2,1,0:T(1,128)}), f32[128,1,128]{2,1,0:T(1,128)S(1)}, u32[]{:S(2)}, u32[]{:S(2)}) async-start(f32[128,1,128]{2,1,0:T(1,128)} %broadcast_in_dim.5), calls=%async_computation.9 | async-start | bytes 131072 | tf_op jit(solution)/shard_map/all_to_all | solution.py:425
  336.2 2.6 fusion.20.first
  338.9 6.9 %all-to-all-done.9 = f32[128,1,128]{2,1,0:T(1,128)S(1)} async-done(((f32[128,1,128]{2,1,0:T(1,128)}), f32[128,1,128]{2,1,0:T(1,128)S(1)}, u32[]{:S(2)}, u32[]{:S(2)}) %all-to-all-start.9) | async-done | bytes 65568 | tf_op jit(solution)/shard_map/all_to_all | solution.py:425
  346.4 6.5 %shard_map.354 = f32[128,3072]{1,0:T(8,128)} custom-call(f32[128,128]{1,0:T(8,128)} %bitcast.139, f32[128,128]{1,0:T(8,128)} %multiply_bitcast_fusion.s, f32[128,128]{1,0:T(8,128)} %copy-done.10, f32[128,128]{1,0:T(8,128)} %copy-done.20, f32[128,128]{1,0:T(8,128)} %copy-done.13, f32[128,128]{1,0:T(8,128)} %copy-done.21, f32[128,128]{1,0:T(8,128)} %get-tuple-element.18.z1.t1, ...), custom_call_target="tpu_custom_call" | custom-call | tf_op jit(solution)/shard_map/pallas_call | solution.py:387
  (131 shorter events, 33.6 us)
Async XLA Ops:
  0.6 15.9 %copy-start.27 = (f32[96,128,1]{1,0,2:T(8,128)S(1)}, f32[96,128,1]{1,0,2:T(8,128)}, u32[]{:S(2)}) copy-start(f32[96,128,1]{1,0,2:T(8,128)} %constant.95) | copy-start | bytes 147460
  0.6 15.6 %copy-start.23 = (f32[6,9216]{1,0:T(8,128)S(1)}, f32[6,9216]{1,0:T(8,128)}, u32[]{:S(2)}) copy-start(f32[6,9216]{1,0:T(8,128)} %param.41) | copy-start | bytes 663556
  0.7 15.7 %copy-start.24 = (f32[6,9216]{1,0:T(8,128)S(1)}, f32[6,9216]{1,0:T(8,128)}, u32[]{:S(2)}) copy-start(f32[6,9216]{1,0:T(8,128)} %param.40) | copy-start | bytes 663556
  4.7 12.4 %copy-start.29 = (f32[96,128,1]{1,0,2:T(8,128)S(1)}, f32[96,128,1]{1,0,2:T(8,128)}, u32[]{:S(2)}) copy-start(f32[96,128,1]{1,0,2:T(8,128)} %constant.96) | copy-start | bytes 147460
  4.7 13.6 %copy-start.26 = (f32[96,128,1]{1,0,2:T(8,128)S(1)}, f32[96,128,1]{1,0,2:T(8,128)}, u32[]{:S(2)}) copy-start(f32[96,128,1]{1,0,2:T(8,128)} %constant.97) | copy-start | bytes 147460
  4.7 21.0 %all-to-all-start = ((f32[128,1,128]{2,1,0:T(1,128)}), f32[128,1,128]{2,1,0:T(1,128)S(1)}, u32[]{:S(2)}, u32[]{:S(2)}) async-start(f32[128,1,128]{2,1,0:T(1,128)} %bitcast.7), calls=%async_computation | async-start | bytes 131072 | tf_op jit(solution)/shard_map/all_to_all | solution.py:422
  16.3 14.7 %copy-start.28 = (f32[96,128,1]{1,0,2:T(8,128)S(1)}, f32[96,128,1]{1,0,2:T(8,128)}, u32[]{:S(2)}) copy-start(f32[96,128,1]{1,0,2:T(8,128)} %constant.98) | copy-start | bytes 147460
  18.6 27.2 %copy-start = (f32[128,3072]{1,0:T(8,128)S(1)}, f32[128,3072]{1,0:T(8,128)}, u32[]{:S(2)}) copy-start(f32[128,3072]{1,0:T(8,128)} %coefs.3) | copy-start | bytes 4718596
  26.5 14.0 %all-to-all-start.1 = ((f32[128,1,128]{2,1,0:T(1,128)}), f32[128,1,128]{2,1,0:T(1,128)S(1)}, u32[]{:S(2)}, u32[]{:S(2)}) async-start(f32[128,1,128]{2,1,0:T(1,128)} %broadcast_in_dim.4), calls=%async_computation.1 | async-start | bytes 131072 | tf_op jit(solution)/shard_map/all_to_all | solution.py:425
  31.3 22.7 %copy-start.8 = (f32[128,6,48]{0,2,1:T(8,128)}, f32[128,6,48]{0,2,1:T(8,128)S(1)}, u32[]{:S(2)}) copy-start(f32[128,6,48]{0,2,1:T(8,128)S(1)} %convolution_add_fusion.2) | copy-start | bytes 442372
  48.4 25.1 %all-to-all-start.2 = ((f32[8,16,3072]{2,1,0:T(8,128)}), f32[8,16,3072]{2,1,0:T(8,128)S(1)}, u32[]{:S(2)}, u32[]{:S(2)}) async-start(f32[8,16,3072]{2,1,0:T(8,128)} %bitcast.12), calls=%async_computation.2 | async-start | bytes 3145728 | tf_op jit(solution)/shard_map/all_to_all | solution.py:481
  147.5 29.8 %all-to-all-start.5 = ((f32[16,216,128]{2,1,0:T(8,128)}), f32[16,216,128]{2,1,0:T(8,128)S(1)}, u32[]{:S(2)}, u32[]{:S(2)}) async-start(f32[16,216,128]{2,1,0:T(8,128)} %bitcast.28), calls=%async_computation.5 | async-start | bytes 3538944 | tf_op jit(solution)/shard_map/all_to_all | solution.py:502
  157.8 3.0 collective-permute-start
  161.7 6.3 %collective-permute-start.1 = (f32[288,128]{1,0:T(8,128)S(1)}, f32[288,128]{1,0:T(8,128)S(1)}, u32[]{:S(2)}, u32[]{:S(2)}) collective-permute-start(f32[288,128]{1,0:T(8,128)S(1)} %add.76), channel_id=1, source_target_pairs={{0,2},{1,3},{2,4},{3,5},{4,6},{5,7},{6,0},{7,1},{8,10},{9,11},{10,... | collective-permute-start | bytes 442376 | tf_op jit(solution)/shard_map/ppermute | solution.py:430
  162.0 6.0 %collective-permute-start.2 = (f32[288,128]{1,0:T(8,128)S(1)}, f32[288,128]{1,0:T(8,128)S(1)}, u32[]{:S(2)}, u32[]{:S(2)}) collective-permute-start(f32[288,128]{1,0:T(8,128)S(1)} %add.76), channel_id=1, source_target_pairs={{0,6},{1,7},{2,0},{3,1},{4,2},{5,3},{6,4},{7,5},{8,14},{9,15},{10,... | collective-permute-start | bytes 442376 | tf_op jit(solution)/shard_map/ppermute | solution.py:430
  164.4 6.0 %collective-permute-start.3 = (f32[288,128]{1,0:T(8,128)S(1)}, f32[288,128]{1,0:T(8,128)S(1)}, u32[]{:S(2)}, u32[]{:S(2)}) collective-permute-start(f32[288,128]{1,0:T(8,128)S(1)} %add.76), channel_id=1, source_target_pairs={{0,4},{1,5},{2,6},{3,7},{4,0},{5,1},{6,2},{7,3},{8,12},{9,13},{10,... | collective-permute-start | bytes 442376 | tf_op jit(solution)/shard_map/ppermute | solution.py:430
  178.4 34.4 %all-to-all-start.4 = ((f32[16,216,128]{2,1,0:T(8,128)}), f32[16,216,128]{2,1,0:T(8,128)S(1)}, u32[]{:S(2)}, u32[]{:S(2)}) async-start(f32[16,216,128]{2,1,0:T(8,128)} %bitcast.119), calls=%async_computation.4 | async-start | bytes 3538944 | tf_op jit(solution)/shard_map/all_to_all | solution.py:527
  185.3 20.8 %copy-start.9 = (f32[128,6,48]{0,2,1:T(8,128)S(1)}, f32[128,6,48]{0,2,1:T(8,128)}, u32[]{:S(2)}) copy-start(f32[128,6,48]{0,2,1:T(8,128)} %copy-done.8) | copy-start | bytes 442372
  191.0 3.4 collective-permute-start.4
  195.4 6.4 %collective-permute-start.5 = (f32[288,128]{1,0:T(8,128)S(1)}, f32[288,128]{1,0:T(8,128)S(1)}, u32[]{:S(2)}, u32[]{:S(2)}) collective-permute-start(f32[288,128]{1,0:T(8,128)S(1)} %add.81), channel_id=1, source_target_pairs={{0,2},{1,3},{2,4},{3,5},{4,6},{5,7},{6,0},{7,1},{8,10},{9,11},{10,... | collective-permute-start | bytes 442376 | tf_op jit(solution)/shard_map/ppermute | solution.py:430
  196.0 5.7 %collective-permute-start.6 = (f32[288,128]{1,0:T(8,128)S(1)}, f32[288,128]{1,0:T(8,128)S(1)}, u32[]{:S(2)}, u32[]{:S(2)}) collective-permute-start(f32[288,128]{1,0:T(8,128)S(1)} %add.81), channel_id=1, source_target_pairs={{0,6},{1,7},{2,0},{3,1},{4,2},{5,3},{6,4},{7,5},{8,14},{9,15},{10,... | collective-permute-start | bytes 442376 | tf_op jit(solution)/shard_map/ppermute | solution.py:430
  198.2 7.9 %collective-permute-start.7 = (f32[288,128]{1,0:T(8,128)S(1)}, f32[288,128]{1,0:T(8,128)S(1)}, u32[]{:S(2)}, u32[]{:S(2)}) collective-permute-start(f32[288,128]{1,0:T(8,128)S(1)} %add.81), channel_id=1, source_target_pairs={{0,4},{1,5},{2,6},{3,7},{4,0},{5,1},{6,2},{7,3},{8,12},{9,13},{10,... | collective-permute-start | bytes 442376 | tf_op jit(solution)/shard_map/ppermute | solution.py:430
  212.8 30.3 %copy-start.2 = (f32[16,216,128]{2,1,0:T(8,128)}, f32[16,216,128]{2,1,0:T(8,128)S(1)}, u32[]{:S(2)}) copy-start(f32[16,216,128]{2,1,0:T(8,128)S(1)} %all-to-all-done.4) | copy-start | bytes 5308420
  284.5 8.0 %copy-start.31 = (f32[128,96]{1,0:T(8,128)S(1)}, f32[128,96]{1,0:T(8,128)}, u32[]{:S(2)}) copy-start(f32[128,96]{1,0:T(8,128)} %constant.92.clone) | copy-start | bytes 147460
  284.5 8.2 %copy-start.6 = (f32[288,128]{1,0:T(8,128)S(1)}, f32[288,128]{1,0:T(8,128)}, u32[]{:S(2)}) copy-start(f32[288,128]{1,0:T(8,128)} %add_add_fusion.1.density) | copy-start | bytes 442372
  284.5 8.2 %copy-start.34 = (f32[128,96]{1,0:T(8,128)S(1)}, f32[128,96]{1,0:T(8,128)}, u32[]{:S(2)}) copy-start(f32[128,96]{1,0:T(8,128)} %constant.89.clone) | copy-start | bytes 147460
  284.5 8.5 %copy-start.33 = (f32[128,96]{1,0:T(8,128)S(1)}, f32[128,96]{1,0:T(8,128)}, u32[]{:S(2)}) copy-start(f32[128,96]{1,0:T(8,128)} %constant.91.clone) | copy-start | bytes 147460
  284.5 27.0 %all-to-all-start.7 = ((f32[8,16,3072]{2,1,0:T(8,128)}), f32[8,16,3072]{2,1,0:T(8,128)S(1)}, u32[]{:S(2)}, u32[]{:S(2)}) async-start(f32[8,16,3072]{2,1,0:T(8,128)} %bitcast.127), calls=%async_computation.7 | async-start | bytes 3145728 | tf_op jit(solution)/shard_map/all_to_all | solution.py:544
  316.7 19.5 %copy-start.7 = (f32[128,3072]{1,0:T(8,128)S(1)}, f32[128,3072]{1,0:T(8,128)}, u32[]{:S(2)}) copy-start(f32[128,3072]{1,0:T(8,128)} %get-tuple-element.17) | copy-start | bytes 4718596
  316.7 19.5 %copy-start.17 = (f32[128,128]{1,0:T(8,128)S(1)}, f32[128,128]{1,0:T(8,128)}, u32[]{:S(2)}) copy-start(f32[128,128]{1,0:T(8,128)} %copy-done.16) | copy-start | bytes 196612
  316.7 14.1 %all-to-all-start.8 = ((f32[128,1,128]{2,1,0:T(1,128)}), f32[128,1,128]{2,1,0:T(1,128)S(1)}, u32[]{:S(2)}, u32[]{:S(2)}) async-start(f32[128,1,128]{2,1,0:T(1,128)} %bitcast.140), calls=%async_computation.8 | async-start | bytes 131072 | tf_op jit(solution)/shard_map/all_to_all | solution.py:422
  331.7 14.0 %all-to-all-start.9 = ((f32[128,1,128]{2,1,0:T(1,128)}), f32[128,1,128]{2,1,0:T(1,128)S(1)}, u32[]{:S(2)}, u32[]{:S(2)}) async-start(f32[128,1,128]{2,1,0:T(1,128)} %broadcast_in_dim.5), calls=%async_computation.9 | async-start | bytes 131072 | tf_op jit(solution)/shard_map/all_to_all | solution.py:425
  (21 other events, 78.7 us)

commit v4 on v3

--- a/solution.py
+++ b/solution.py
@@ -18,6 +18,8 @@
 BD = 8
 LB = NB // BD
 GY = G // PW
+ORDER = (0, 1, 2, 6, 3, 7, 4, 5)
+HELD = BD // 2
 PARTS = 2
 BLOCKS = ((0, 6), (1, 11), (2, 10), (3, 9), (4, 8), (5, 7))
 PAIRS = len(BLOCKS) // PARTS
@@ -159,8 +161,7 @@
     return [group == s for s in range(BD)]
 
 
-def scatter_kernel(cells, recv, zt, mh, ml, *rest):
-    sent, (dense, turned, fields, bh, bl) = rest[-7:-5], rest[-5:]
+def clear_kernel(unread, dense):
     zero = jnp.zeros((256, LANES), f32)
 
     def clear(i, carry):
@@ -169,9 +170,16 @@
 
     lax.fori_loop(0, SLAB // 256, clear, 0)
 
+
+def place_kernel(first, cells, *rest):
+    blocks, (dense, turned) = rest[:HELD], rest[-2:]
+    empty = jnp.zeros((HELD * LB, LANES), f32)
+
     def turn(i, carry):
         at = pl.multiple_of(i * LANES, LANES)
-        turned[pl.ds(at, LANES), :] = recv[:, pl.ds(at, LANES)].T
+        rows = [block[:, pl.ds(at, LANES)] for block in blocks]
+        rows = [empty, *rows] if first else [*rows, empty]
+        turned[pl.ds(at, LANES), :] = jnp.concatenate(rows, axis=0).T
         return carry
 
     lax.fori_loop(0, KW // LANES, turn, 0)
@@ -181,12 +189,16 @@
         for j in range(16):
             k = i * 16 + j
             row = turned[pl.ds(k, 1), :]
-            for s in range(BD):
-                cell = cells[s * KW + k]
-                pltpu.store(dense.at[pl.ds(cell, 1), :], row, mask=masks[s])
+            for p in range(HELD):
+                pltpu.store(dense.at[pl.ds(cells[p * KW + k], 1), :], row, mask=masks[first + p])
         return carry
 
     lax.fori_loop(0, KW // 16, place, 0)
+
+
+def fold_kernel(cells, *rest):
+    given, zt, mh, ml, dense, sent0, sent1, turned, fields, high, low = rest[HELD:]
+    place_kernel(HELD, cells, *rest[:HELD], dense, turned)
     table = zt[...]
 
     def along_z(i, carry):
@@ -213,21 +225,20 @@
         c = cos12([e[0]] + [e[j] + e[12 - j] for j in range(1, 6)] + [e[6]])
         s = sin12([None] + [e[j] - e[12 - j] for j in range(1, 6)])
         for p in range(6):
-            high, low = split(jnp.concatenate([c[p], c[6] if p == 0 else s[p]], axis=1))
-            bh[p, pl.ds(at, 16), :] = high
-            bl[p, pl.ds(at, 16), :] = low
+            high[p, pl.ds(at, 16), :], low[p, pl.ds(at, 16), :] = split(
+                jnp.concatenate([c[p], c[6] if p == 0 else s[p]], axis=1)
+            )
         return carry
 
     lax.fori_loop(0, GY * G // 16, twelve, 0)
-
-    for p in range(6):
-        out = dot3((bh[p], bl[p]), (mh[p], ml[p]))
+    for p in range(2 * PAIRS):
+        out = dot3((high[p], low[p]), (mh[p], ml[p]))
+        sent = (sent0, sent1)[p // PAIRS]
         for side in range(2):
             for y in range(GY):
                 for z in range(GY):
-                    row = y * COLS + z * XB + p % PAIRS * 2 + side
                     at = y * G + z * PW
-                    sent[p // PAIRS][pl.ds(row, PW, stride=BLK), :] = out[
+                    sent[pl.ds(y * COLS + z * XB + p % PAIRS * 2 + side, PW, stride=BLK), :] = out[
                         at : at + PW, side * LANES : (side + 1) * LANES
                     ]
 
@@ -277,20 +288,19 @@
     lax.fori_loop(0, GY, along_y, 0)
 
 
-def gather_kernel(cells, recv0, recv1, zt, mh, ml, terms, dense, turned, uv, bh, bl):
+def spread_kernel(recv0, recv1, zt, mh, ml, dense, uv, bh, bl):
     table = zt[...]
-    recv = (recv0, recv1)
-    for p in range(6):
-        first = p % PAIRS * 2
-        starts = [y * COLS + z * XB + first for y in range(GY) for z in range(GY)]
-        data = [lines(recv[p // PAIRS], [row + side for row in starts]) for side in range(2)]
+    for p in range(2 * PAIRS):
+        recv = (recv0, recv1)[p // PAIRS]
+        starts = [y * COLS + z * XB + p % PAIRS * 2 for y in range(GY) for z in range(GY)]
+        data = [lines(recv, [row + side for row in starts]) for side in range(2)]
         uv[p] = dot3(split(jnp.concatenate(data, axis=1)), (mh[p], ml[p]))
 
     def twelve(i, carry):
         at = pl.multiple_of(i * 16, 16)
-        u = [uv[p, pl.ds(at, 16), :LANES] for p in range(6)] + [uv[0, pl.ds(at, 16), LANES:]]
-        v = [None] + [uv[p, pl.ds(at, 16), LANES:] for p in range(1, 6)]
-        c, s = cos12(u), sin12(v)
+        left = [uv[p, pl.ds(at, 16), :LANES] for p in range(6)]
+        right = [uv[p, pl.ds(at, 16), LANES:] for p in range(6)]
+        c, s = cos12(left + [right[0]]), sin12([None] + right[1:])
         x = [c[0]] + [c[j] + s[j] for j in range(1, 6)] + [c[6]] + [c[j] - s[j] for j in range(5, 0, -1)]
         for quad in range(3):
             high, low = split(jnp.concatenate(x[4 * quad : 4 * quad + 4], axis=1))
@@ -313,14 +323,18 @@
         return carry
 
     lax.fori_loop(0, GY * 3, along_z, 0)
+
+
+def pick_kernel(first, cells, dense, *rest):
+    terms, turned = rest[-1 - HELD : -1], rest[-1]
     masks = source_masks()
 
     def pick(i, carry):
         for j in range(16):
             k = i * 16 + j
             row = dense[pl.ds(cells[k], 1), :]
-            for s in range(1, BD):
-                row = jnp.where(masks[s], dense[pl.ds(cells[s * KW + k], 1), :], row)
+            for p in range(1, HELD):
+                row = jnp.where(masks[first + p], dense[pl.ds(cells[p * KW + k], 1), :], row)
             turned[pl.ds(k, 1), :] = row
         return carry
 
@@ -328,10 +342,22 @@
 
     def turn(i, carry):
         at = pl.multiple_of(i * LANES, LANES)
-        terms[:, pl.ds(at, LANES)] = turned[pl.ds(at, LANES), :].T
+        rows = turned[pl.ds(at, LANES), :].T
+        for p in range(HELD):
+            terms[p][:, pl.ds(at, LANES)] = rows[(first + p) * LB : (first + p + 1) * LB]
         return carry
 
     lax.fori_loop(0, KW // LANES, turn, 0)
+
+
+def rotate_kernel(order, weights, coefs, *rest):
+    blocks, rotated = rest[-1 - BD : -1], rest[-1]
+    turned = split(weights[...].T)
+    for at in range(0, KW, 512):
+        part = pl.ds(at, 512)
+        rotated[:, part] = dot3(turned, split(coefs[:, part]))
+    for p in range(BD):
+        blocks[p][...] = rotated[pl.ds(pl.multiple_of(order[p] * LB, LB), LB), :]
 
 
 def pullback_kernel(grads, s, y0, y1, y2, y3, z1, z2, z3, z4, t1, t2, t3, t4, coefs, first, out):
@@ -366,7 +392,11 @@
         out[:, part] = first[:, part] + dot3(both, split(coefs[:, part]))
 
 
-def products_kernel(terms, rotated, coefs, kinetic, occupancy, grads, sums):
+def products_kernel(order, *rest):
+    terms, rotated, (coefs, kinetic, occupancy, grads, sums) = rest[:BD], rest[BD : 2 * BD], rest[2 * BD :]
+    for p in range(BD):
+        rows = pl.ds(pl.multiple_of(order[p] * LB, LB), LB)
+        grads[rows, :] = occupancy[rows, :] * (kinetic[...] * rotated[p][...] + terms[p][...])
     added = jnp.zeros((NB, NB), f32)
 
     def dot_t(a, b):
@@ -374,14 +404,12 @@
 
     for at in range(0, KW, 512):
         part = pl.ds(at, 512)
-        value = occupancy[...] * (kinetic[:, part] * rotated[:, part] + terms[:, part])
-        grads[:, part] = value
-        a, b = split(coefs[:, part]), split(value)
+        a, b = split(coefs[:, part]), split(grads[:, part])
         added = added + (dot_t(a[0], b[0]) + (dot_t(a[0], b[1]) + dot_t(a[1], b[0])))
     sums[...] = added
 
 
-def call(kernel, out_shapes, scratch, scalars, *operands, unread=()):
+def call(kernel, out_shapes, scratch, scalars, *operands, unread=(), alias=None, room=58, micros=3):
     vmem = pl.BlockSpec(memory_space=pltpu.VMEM)
     smem = pl.BlockSpec(memory_space=pltpu.SMEM)
     return pl.pallas_call(
@@ -392,8 +420,18 @@
         + [pl.BlockSpec(memory_space=pl.ANY)] * len(unread),
         out_specs=jax.tree.map(lambda _: vmem, out_shapes),
         scratch_shapes=scratch,
-        compiler_params=pltpu.CompilerParams(vmem_limit_bytes=58 * 1024 * 1024),
+        input_output_aliases=alias or {},
+        cost_estimate=pl.CostEstimate(flops=0, bytes_accessed=micros * 3_500_000, transcendentals=0),
+        compiler_params=pltpu.CompilerParams(vmem_limit_bytes=room * 1024 * 1024),
     )(*operands, *unread)
+
+
+def kept(*shape):
+    return pltpu.VMEM(shape, f32)
+
+
+def held(values):
+    return pltpu.with_memory_space_constraint(values, pltpu.VMEM)
 
 
 def array(*shape):
@@ -466,38 +504,80 @@
     chosen = chosen.astype(np.float32)
     pack = packed[0].astype(ml_dtypes.bfloat16)
     unpack = np.swapaxes(pack, 1, 2)
-    unused = (1.0 - chosen.sum(axis=(1, 2))).astype(np.float32)
+    unused_lanes = (1.0 - chosen.sum(axis=(1, 2))).astype(np.float32)
     pw_pos = lax.axis_index("pw")
     band_pos = lax.axis_index("band")
     cells = cell_map - pw_pos * SLAB
+
+    order = jnp.bitwise_xor(band_pos, jnp.asarray(ORDER, jnp.int32))
+    cells = [lax.dynamic_slice_in_dim(cells, order[p] * KW, KW) for p in range(BD)]
+    cells = [jnp.concatenate(cells[:HELD]), jnp.concatenate(cells[HELD:])]
+
+    def meet(block, p):
+        if ORDER[p] == 0:
+            return block
+        return lax.ppermute(block, "band", [(i, i ^ ORDER[p]) for i in range(BD)])
+
+    intersection = total(matmul(coefficients, coefficients.T)) / NPW
+    weights, iterates = loewdin(intersection)
+    rotated = call(
+        rotate_kernel,
+        [array(LB, KW)] * BD,
+        [pltpu.VMEM((NB, KW), f32)],
+        1,
+        order,
+        weights,
+        coefficients,
+        unread=cells,
+        room=28,
+    )
+    near = [meet(rotated[p], p) for p in range(HELD)]
+    dense = call(clear_kernel, kept(SLAB, LANES), [], 0, unread=(rotated[0],), room=28)
+    *barred, dense = lax.optimization_barrier((*near, *rotated[HELD:], dense))
+    blocks = [*barred[:HELD], *(meet(barred[p], p) for p in range(HELD, BD))]
+    dense = call(
+        functools.partial(place_kernel, 0),
+        kept(SLAB, LANES),
+        [pltpu.VMEM((KW, LANES), f32)],
+        1,
+        cells[0],
+        *blocks[:HELD],
+        held(dense),
+        alias={1 + HELD: 0},
+        room=28,
+        micros=14,
+    )
+    halves_shape = (2 * PAIRS, GY * G, 2 * LANES)
+    unused, *sent = call(
+        fold_kernel,
+        (kept(SLAB, LANES), array(ROWS, LANES), array(ROWS, LANES)),
+        [
+            pltpu.VMEM((KW, LANES), f32),
+            pltpu.VMEM((12, GY * G, LANES), f32),
+            pltpu.VMEM(halves_shape, bf16),
+            pltpu.VMEM(halves_shape, bf16),
+        ],
+        1,
+        cells[1],
+        *blocks[HELD:],
+        held(dense),
+        table["z_out"],
+        *table["mix"],
+        alias={1 + HELD: 0},
+        room=28,
+        micros=29,
+    )
+    *sent, core_density, potential_ext, kinetic, occupancy = lax.optimization_barrier(
+        (*sent, core_density, potential_ext, kinetic, occupancy)
+    )
+    core = [to_sums(core_density, chosen[part]) + unused_lanes[part] for part in range(PARTS)]
+    external = [to_sums(potential_ext, chosen[part]) for part in range(PARTS)]
     share = lax.dynamic_slice_in_dim(occupancy / NB, band_pos * LB, LB)
     share = jnp.tile(share, XB * BD).reshape(1, WIDE)
-    core = [to_sums(core_density, chosen[part]) + unused[part] for part in range(PARTS)]
-    external = [to_sums(potential_ext, chosen[part]) for part in range(PARTS)]
-
-    intersection = total(matmul(coefficients, coefficients.T)) / NPW
-    weights, iterates = loewdin(intersection)
-    rotated = matmul(weights.T, coefficients)
-    block = lax.all_to_all(rotated, "band", split_axis=0, concat_axis=0, tiled=True)
-    sent = call(
-        scatter_kernel,
-        [array(ROWS, LANES)] * PARTS,
-        [
-            pltpu.VMEM((SLAB, LANES), f32),
-            pltpu.VMEM((KW, LANES), f32),
-            pltpu.VMEM((12, GY * G, LANES), f32),
-            pltpu.VMEM((6, GY * G, 2 * LANES), bf16),
-            pltpu.VMEM((6, GY * G, 2 * LANES), bf16),
-        ],
-        1,
-        cells,
-        block,
-        table["z_out"],
-        *table["mix"],
-        unread=(*core, *external),
-    )
+    kinetic_row = kinetic.reshape(1, KW)
+    occupancy_column = occupancy.reshape(NB, 1)
     exchange = functools.partial(lax.all_to_all, axis_name="pw", split_axis=0, concat_axis=0, tiled=True)
-    density, returned, after = [], [], []
+    density, returned, after = [], [], [*core, *external]
     for part in range(PARTS):
         received = exchange(sent[part])
         fields, sums = call(
@@ -525,34 +605,53 @@
         )
         after = [product]
         returned.append(exchange(product))
-    terms = call(
-        gather_kernel,
-        array(NB, KW),
+    dense = call(
+        spread_kernel,
+        kept(SLAB, LANES),
         [
-            pltpu.VMEM((SLAB, LANES), f32),
-            pltpu.VMEM((KW, LANES), f32),
             pltpu.VMEM((6, GY * G, 2 * LANES), f32),
             pltpu.VMEM((3, GY * G, 4 * LANES), bf16),
             pltpu.VMEM((3, GY * G, 4 * LANES), bf16),
         ],
-        1,
-        cells,
+        0,
         *returned,
         table["z_in"],
         *table["mix_t"],
-    )
-    row_term = lax.all_to_all(terms, "band", split_axis=0, concat_axis=0, tiled=True)
+        room=28,
+        micros=13,
+    )
+    terms, after = [None, None], ()
+    for side in (1, 0):
+        terms[side] = call(
+            functools.partial(pick_kernel, side * HELD),
+            [array(LB, KW)] * HELD,
+            [pltpu.VMEM((KW, LANES), f32)],
+            1,
+            cells[side],
+            held(dense),
+            unread=after,
+            room=28,
+            micros=14,
+        )
+        after = tuple(terms[side])
+    far = [meet(terms[1][p], HELD + p) for p in range(HELD)]
+    near = terms[0]
+    barred = lax.optimization_barrier((*near, *far))
+    near, far = barred[:HELD], barred[HELD:]
+    terms = [meet(near[p], p) for p in range(HELD)] + list(far)
     grad_rotated, partial = call(
         products_kernel,
         (array(NB, KW), array(NB, NB)),
         [],
-        0,
-        row_term,
-        rotated,
+        1,
+        order,
+        *terms,
+        *rotated,
         coefficients,
-        kinetic.reshape(1, KW),
-        occupancy.reshape(NB, 1),
-    )
+        kinetic_row,
+        occupancy_column,
+    )
+    *density, partial = lax.optimization_barrier((*density, partial))
     grad_weights = total(partial)
     first = matmul(weights, grad_rotated)
     grad_coef = call(

time: 354 us -> 349 us (0.986)
  blocking collectives: 58.9 us -> 30.1 us
  starting transfers between devices: 56.9 us -> 69 us
  Pallas kernels: 119 us -> 131 us
  between operations: 1.97 us -> 7.34 us
  waiting for transfers between devices: 83.5 us -> 78.4 us
    all_to_all x2 -> x0, waiting for transfers between devices: 36.3 us -> none  [the longest x1 18.2 us: shards(): lax.all_to_all(terms, 'band', split_axis=0, concat_axis=0, tiled=True)]
    all_to_all x1 -> x0, blocking collectives: 28.5 us -> none  [shards(): received = exchange(sent[part])]
    all_to_all x1 -> x2, waiting for transfers between devices: 0.01 us -> 27.2 us  [shards(): received = exchange(sent[part])]
    ppermute x0 -> x14, starting transfers between devices: none -> 17.6 us  [meet(): return lax.ppermute(block, 'band', [(i, i ^ ORDER[p]) for i in range(BD)])]
    pallas_call x8 -> x13, Pallas kernels: 119 us -> 131 us  [call(): pl.pallas_call(kernel, out_shape=out_shapes, in_specs=[smem] * scalars +...]
    all_to_all x2 -> x0, starting transfers between devices: 10.6 us -> none  [the longest x1 6.24 us: shards(): lax.all_to_all(terms, 'band', split_axis=0, concat_axis=0, tiled=True)]
    ppermute x0 -> x14, waiting for transfers between devices: none -> 9 us  [meet(): return lax.ppermute(block, 'band', [(i, i ^ ORDER[p]) for i in range(BD)])]
    all_to_all x2, waiting for transfers between devices: 15.9 us -> 8.09 us  [total(): lax.all_to_all(values, axes, split_axis=0, concat_axis=0, tiled=True)]
  transfers between devices with their start and end apart: 16 -> 29, of which waited for: 12 -> 17; matrix products, arithmetic and copies ran while one was open for 4% -> 5% of each run, Pallas kernels for 7% -> 16%
where the time goes in v4:
time: 349 us; the launch traced here: 348 us
  Pallas kernels  131 us (38%)
  waiting for transfers between devices  78.4 us (22%)
  starting transfers between devices  69 us (20%)
  blocking collectives  30.1 us (9%)
  matrix products  15.1 us (4%)
  local copies, waits for them, and re-layouts  10.7 us (3%)
  between operations  7.34 us (2%)
  other arithmetic  6.22 us (2%)
    pallas_call x13, Pallas kernels, call(): pl.pallas_call(kernel, out_shape=out_shapes, in_specs=[smem] * scalars +...  131 us
    all_to_all x1, blocking collectives, shards(): returned.append(exchange(product))  30.1 us
    all_to_all x2, waiting for transfers between devices, shards(): received = exchange(sent[part])  27.2 us
    all_to_all x2, waiting for transfers between devices, total(): return lax.all_to_all(copies, axes, split_axis=0, concat_axis=0, tiled=True)  18 us
    ppermute x14, starting transfers between devices, meet(): return lax.ppermute(block, 'band', [(i, i ^ ORDER[p]) for i in range(BD)])  17.6 us
    all_to_all x2, starting transfers between devices, total(): lax.all_to_all(values, axes, split_axis=0, concat_axis=0, tiled=True)  16.6 us
    dot_general x23, matrix products, matmul(): jnp.dot(left_side, right_side, precision=highest, preferred_element_type=...  15.1 us
    ppermute x6, waiting for transfers between devices, band_total(): lax.ppermute(values, 'band', [(i, (i + 2 * step) % BD) for i in range(BD)])  13.6 us
  transfers between devices with their start and end apart: 29, of which 17 were waited for; matrix products, arithmetic and copies ran while one was open for 5% of the time, Pallas kernels for 16%

profile of v4, /device:TPU:1, one launch (start us, length us, event | category | flops | bytes accessed | tf_op | source)
XLA Modules:
  0.0 348.2 jit_solution(8502388924540777059)
XLA Ops:
  0.7 4.0 %fusion.27 = f32[128,128]{1,0:T(8,128)} fusion(f32[128,3072]{1,0:T(8,128)} %coefs.3), kind=kOutput, calls=%fused_computation.57 | convolution fusion | flops 603979776 | bytes 1638400 | tf_op jit(solution)/shard_map/dot_general | solution.py:442
  4.7 11.5 %all-to-all-start = ((f32[128,1,128]{2,1,0:T(1,128)}), f32[128,1,128]{2,1,0:T(1,128)S(1)}, u32[]{:S(2)}, u32[]{:S(2)}) async-start(f32[128,1,128]{2,1,0:T(1,128)} %bitcast.5), calls=%async_computation | async-start | bytes 131072 | tf_op jit(solution)/shard_map/all_to_all | solution.py:460
  22.0 3.7 %all-to-all-done = f32[128,1,128]{2,1,0:T(1,128)S(1)} async-done(((f32[128,1,128]{2,1,0:T(1,128)}), f32[128,1,128]{2,1,0:T(1,128)S(1)}, u32[]{:S(2)}, u32[]{:S(2)}) %all-to-all-start) | async-done | bytes 65568 | tf_op jit(solution)/shard_map/all_to_all | solution.py:460
  26.5 6.1 %all-to-all-start.1 = ((f32[128,1,128]{2,1,0:T(1,128)}), f32[128,1,128]{2,1,0:T(1,128)S(1)}, u32[]{:S(2)}, u32[]{:S(2)}) async-start(f32[128,1,128]{2,1,0:T(1,128)} %broadcast_in_dim.4), calls=%async_computation.1 | async-start | bytes 131072 | tf_op jit(solution)/shard_map/all_to_all | solution.py:463
  32.7 9.5 %all-to-all-done.1 = f32[128,1,128]{2,1,0:T(1,128)S(1)} async-done(((f32[128,1,128]{2,1,0:T(1,128)}), f32[128,1,128]{2,1,0:T(1,128)S(1)}, u32[]{:S(2)}, u32[]{:S(2)}) %all-to-all-start.1) | async-done | bytes 65568 | tf_op jit(solution)/shard_map/all_to_all | solution.py:463
  53.2 3.1 collective-permute-done.1.rest_2_
  63.0 14.5 %shard_map.358.rest_4_ = f32[55296,128]{1,0:T(8,128)S(1)} custom-call(s32[12288]{0:T(1024)} %copy-done.2, f32[16,3072]{1,0:T(8,128)} %copy-done.1, f32[16,3072]{1,0:T(8,128)} %copy-done.28, f32[16,3072]{1,0:T(8,128)} %copy-done.30, f32[16,3072]{1,0:T(8,128)} %copy-done.32, f32[55296,128]{1,0:T(8,128)S(1)} %shard_map.357.rest_4_), custom_call_target="tpu_custom_call", output_to_operand_aliasing={{}: (5, {})} | custom-call | bytes 49000000 | tf_op jit(solution)/shard_map/pallas_call | solution.py:415
  79.0 31.4 %shard_map.359 = (f32[55296,128]{1,0:T(8,128)S(1)}, f32[3456,128]{1,0:T(8,128)}, f32[3456,128]{1,0:T(8,128)}) custom-call(s32[12288]{0:T(1024)} %copy-done.3, f32[16,3072]{1,0:T(8,128)} %copy-done.29, f32[16,3072]{1,0:T(8,128)} %copy-done.31, f32[16,3072]{1,0:T(8,128)} %copy-done.33, f32[16,3072]{1,0:T(8,128)} %copy-done.34, ...), custom_call_target="tpu_custom_call", output_to_operand_aliasing={{0}: (5, {})} | custom-call | bytes 101500000 | tf_op jit(solution)/shard_map/pallas_call | solution.py:415
  110.4 3.9 %all-to-all-start.2 = ((f32[16,216,128]{2,1,0:T(8,128)}), f32[16,216,128]{2,1,0:T(8,128)S(1)}, u32[]{:S(2)}, u32[]{:S(2)}) async-start(f32[16,216,128]{2,1,0:T(8,128)} %bitcast.121), calls=%async_computation.2 | async-start | bytes 3538944 | tf_op jit(solution)/shard_map/all_to_all | solution.py:582
  116.5 27.2 %all-to-all-done.2 = f32[16,216,128]{2,1,0:T(8,128)S(1)} async-done(((f32[16,216,128]{2,1,0:T(8,128)}), f32[16,216,128]{2,1,0:T(8,128)S(1)}, u32[]{:S(2)}, u32[]{:S(2)}) %all-to-all-start.2) | async-done | bytes 1769504 | tf_op jit(solution)/shard_map/all_to_all | solution.py:582
  144.8 3.9 %all-to-all-start.3 = ((f32[16,216,128]{2,1,0:T(8,128)}), f32[16,216,128]{2,1,0:T(8,128)S(1)}, u32[]{:S(2)}, u32[]{:S(2)}) async-start(f32[16,216,128]{2,1,0:T(8,128)} %bitcast.120), calls=%async_computation.3 | async-start | bytes 3538944 | tf_op jit(solution)/shard_map/all_to_all | solution.py:582
  151.9 5.8 %shard_map.360 = (f32[3456,128]{1,0:T(8,128)}, f32[288,128]{1,0:T(8,128)}) custom-call(f32[3456,128]{1,0:T(8,128)} %bitcast.117, bf16[192,96]{1,0:T(8,128)(2,1)} %constant.95.clone.yt, bf16[768,128]{1,0:T(8,128)(2,1)} %constant.96.clone.pack0, bf16[768,128]{1,0:T(8,128)(2,1)} %constant.97.clone.pack1, f32[1,768]{1,0:T(1,128)} %reshape_tile.3.share, ...), custom_call_target="tpu_custom_call" | custom-call | bytes 10500000 | tf_op jit(solution)/shard_map/pallas_call | solution.py:415
  164.0 3.2 collective-permute-done.10
  171.3 6.0 %shard_map.361.rest_0_ = f32[3456,128]{1,0:T(8,128)} custom-call(f32[288,128]{1,0:T(8,128)} %add_add_fusion.1.density, f32[288,128]{1,0:T(8,128)} %bitcast.125, f32[3456,128]{1,0:T(8,128)} %get-tuple-element.77.fields, bf16[192,96]{1,0:T(8,128)(2,1)} %constant.98.clone.yt, bf16[128,768]{1,0:T(8,128)(2,1)} %constant.99.clone.open0, ...), custom_call_target="tpu_custom_call" | custom-call | bytes 10500000 | tf_op jit(solution)/shard_map/pallas_call | solution.py:415
  178.5 6.7 %all-to-all-start.4 = ((f32[16,216,128]{2,1,0:T(8,128)}), f32[16,216,128]{2,1,0:T(8,128)}, u32[]{:S(2)}, u32[]{:S(2)}) async-start(f32[16,216,128]{2,1,0:T(8,128)} %bitcast.115), calls=%async_computation.4 | async-start | bytes 3538944 | tf_op jit(solution)/shard_map/all_to_all | solution.py:607
  185.2 5.7 %shard_map.362 = (f32[3456,128]{1,0:T(8,128)}, f32[288,128]{1,0:T(8,128)}) custom-call(f32[3456,128]{1,0:T(8,128)} %bitcast.116, bf16[192,96]{1,0:T(8,128)(2,1)} %constant.95.clone.yt, bf16[768,128]{1,0:T(8,128)(2,1)} %constant.96.clone.pack0, bf16[768,128]{1,0:T(8,128)(2,1)} %constant.97.clone.pack1, f32[1,768]{1,0:T(1,128)} %reshape_tile.3.share, ...), custom_call_target="tpu_custom_call" | custom-call | bytes 10500000 | tf_op jit(solution)/shard_map/pallas_call | solution.py:415
  197.7 3.8 %collective-permute-done.14 = f32[288,128]{1,0:T(8,128)S(1)} collective-permute-done((f32[288,128]{1,0:T(8,128)S(1)}, f32[288,128]{1,0:T(8,128)S(1)}, u32[]{:S(2)}, u32[]{:S(2)}) %collective-permute-start.14) | collective-permute-done | bytes 147488 | tf_op jit(solution)/shard_map/ppermute | solution.py:468
  205.5 6.0 %shard_map.363 = f32[3456,128]{1,0:T(8,128)} custom-call(f32[288,128]{1,0:T(8,128)} %add_add_fusion.density, f32[288,128]{1,0:T(8,128)} %bitcast.123, f32[3456,128]{1,0:T(8,128)} %get-tuple-element.79.fields, bf16[192,96]{1,0:T(8,128)(2,1)} %constant.98.clone.yt, bf16[128,768]{1,0:T(8,128)(2,1)} %constant.99.clone.open0, bf16[128,768]{1,0:T(8,128)(2,1)} %constant.100.clone.open1), custom_call_target="tpu_custom_call" | custom-call | bytes 10500000 | tf_op jit(solution)/shard_map/pallas_call | solution.py:415
  211.5 30.1 %all_to_all.76 = f32[16,216,128]{2,1,0:T(8,128)} all-to-all(f32[16,216,128]{2,1,0:T(8,128)} %bitcast.118), channel_id=1, replica_groups=mesh['pw'=16,'band'=8] {'pw'}, dimensions={0} | all-to-all | bytes 3538944 | tf_op jit(solution)/shard_map/all_to_all | solution.py:607
  241.7 17.4 %shard_map.364.dense = f32[55296,128]{1,0:T(8,128)S(1)} custom-call(f32[3456,128]{1,0:T(8,128)} %bitcast.31.recv0, f32[3456,128]{1,0:T(8,128)} %bitcast.119, bf16[192,96]{1,0:T(8,128)(2,1)} %constant.101.clone.zt, bf16[6,256,256]{2,1,0:T(8,128)(2,1)} %constant.102.clone.mh, bf16[6,256,256]{2,1,0:T(8,128)(2,1)} %constant.103.clone.ml), custom_call_target="tpu_custom_call" | custom-call | bytes 45500000 | tf_op jit(solution)/shard_map/pallas_call | solution.py:415
  259.1 15.3 %shard_map.365 = (f32[16,3072]{1,0:T(8,128)}, f32[16,3072]{1,0:T(8,128)}, f32[16,3072]{1,0:T(8,128)}, f32[16,3072]{1,0:T(8,128)}) custom-call(s32[12288]{0:T(1024)} %copy-done.3, f32[55296,128]{1,0:T(8,128)S(1)} %shard_map.364.dense), custom_call_target="tpu_custom_call" | custom-call | bytes 49000000 | tf_op jit(solution)/shard_map/pallas_call | solution.py:415
  274.4 3.6 %collective-permute-start.15 = (f32[16,3072]{1,0:T(8,128)}, f32[16,3072]{1,0:T(8,128)S(1)}, u32[]{:S(2)}, u32[]{:S(2)}) collective-permute-start(f32[16,3072]{1,0:T(8,128)} %get-tuple-element.80.rest_0_), channel_id=1, source_target_pairs={{0,3},{1,2},{2,1},{3,0},{4,7},{5,6},{6,5},{7,4},{8,11},{9,10},{10,... | collective-permute-start | bytes 589832 | tf_op jit(solution)/shard_map/ppermute | solution.py:519
  280.0 2.6 collective-permute-start.18
  282.6 15.0 %shard_map.366 = (f32[16,3072]{1,0:T(8,128)}, f32[16,3072]{1,0:T(8,128)}, f32[16,3072]{1,0:T(8,128)}, f32[16,3072]{1,0:T(8,128)}) custom-call(s32[12288]{0:T(1024)} %copy-done.2, f32[55296,128]{1,0:T(8,128)S(1)} %shard_map.364.dense, f32[16,3072]{1,0:T(8,128)} %get-tuple-element.80.rest_0_, f32[16,3072]{1,0:T(8,128)} %get-tuple-element.81.rest_1_, ...), custom_call_target="tpu_custom_call" | custom-call | bytes 49000000 | tf_op jit(solution)/shard_map/pallas_call | solution.py:415
  300.9 3.2 collective-permute-done.20.rest_2_
  306.3 4.4 %shard_map.367 = (f32[128,3072]{1,0:T(8,128)}, f32[128,128]{1,0:T(8,128)}) custom-call(s32[8]{0:T(128)} %copy-done.11, f32[16,3072]{1,0:T(8,128)} %get-tuple-element.88.rest_0_, f32[16,3072]{1,0:T(8,128)} %copy-done.39, f32[16,3072]{1,0:T(8,128)} %copy-done.40, f32[16,3072]{1,0:T(8,128)} %copy-done.41, f32[16,3072]{1,0:T(8,128)} %copy-done.35, ...), custom_call_target="tpu_custom_call" | custom-call | bytes 10500000 | tf_op jit(solution)/shard_map/pallas_call | solution.py:415
  310.7 5.1 %all-to-all-start.6 = ((f32[128,1,128]{2,1,0:T(1,128)}), f32[128,1,128]{2,1,0:T(1,128)S(1)}, u32[]{:S(2)}, u32[]{:S(2)}) async-start(f32[128,1,128]{2,1,0:T(1,128)} %bitcast.133), calls=%async_computation.6 | async-start | bytes 131072 | tf_op jit(solution)/shard_map/all_to_all | solution.py:460
  316.4 4.0 %fusion.31.first = f32[128,3072]{1,0:T(8,128)} fusion(f32[128,128]{1,0:T(8,128)S(1)} %get-tuple-element.122.weights, f32[128,3072]{1,0:T(8,128)} %get-tuple-element.99), kind=kOutput, calls=%fused_computation.61 | convolution fusion | flops 603979776 | bytes 3211264 | tf_op jit(solution)/shard_map/dot_general | solution.py:442
  321.0 4.4 %all-to-all-done.6 = f32[128,1,128]{2,1,0:T(1,128)S(1)} async-done(((f32[128,1,128]{2,1,0:T(1,128)}), f32[128,1,128]{2,1,0:T(1,128)S(1)}, u32[]{:S(2)}, u32[]{:S(2)}) %all-to-all-start.6) | async-done | bytes 65568 | tf_op jit(solution)/shard_map/all_to_all | solution.py:460
  326.2 5.4 %all-to-all-start.7 = ((f32[128,1,128]{2,1,0:T(1,128)}), f32[128,1,128]{2,1,0:T(1,128)S(1)}, u32[]{:S(2)}, u32[]{:S(2)}) async-start(f32[128,1,128]{2,1,0:T(1,128)} %broadcast_in_dim.5), calls=%async_computation.7 | async-start | bytes 131072 | tf_op jit(solution)/shard_map/all_to_all | solution.py:463
  332.6 8.5 %all-to-all-done.7 = f32[128,1,128]{2,1,0:T(1,128)S(1)} async-done(((f32[128,1,128]{2,1,0:T(1,128)}), f32[128,1,128]{2,1,0:T(1,128)S(1)}, u32[]{:S(2)}, u32[]{:S(2)}) %all-to-all-start.7) | async-done | bytes 65568 | tf_op jit(solution)/shard_map/all_to_all | solution.py:463
  341.8 6.5 %shard_map.368 = f32[128,3072]{1,0:T(8,128)} custom-call(f32[128,128]{1,0:T(8,128)} %bitcast.132, f32[128,128]{1,0:T(8,128)} %multiply_bitcast_fusion.s, f32[128,128]{1,0:T(8,128)} %copy-done.16, f32[128,128]{1,0:T(8,128)} %copy-done.22, f32[128,128]{1,0:T(8,128)} %copy-done.18, f32[128,128]{1,0:T(8,128)} %copy-done.23, ...), custom_call_target="tpu_custom_call" | custom-call | bytes 10500000 | tf_op jit(solution)/shard_map/pallas_call | solution.py:415
  (198 shorter events, 59.5 us)
Async XLA Ops:
  0.6 21.3 %copy-start.46 = (s32[24576]{0:T(1024)S(1)}, s32[24576]{0:T(1024)}, u32[]{:S(2)}) copy-start(s32[24576]{0:T(1024)} %param.40) | copy-start | bytes 294916
  4.7 42.1 %copy-start = (f32[128,3072]{1,0:T(8,128)S(1)}, f32[128,3072]{1,0:T(8,128)}, u32[]{:S(2)}) copy-start(f32[128,3072]{1,0:T(8,128)} %coefs.3) | copy-start | bytes 4718596
  4.7 21.0 %all-to-all-start = ((f32[128,1,128]{2,1,0:T(1,128)}), f32[128,1,128]{2,1,0:T(1,128)S(1)}, u32[]{:S(2)}, u32[]{:S(2)}) async-start(f32[128,1,128]{2,1,0:T(1,128)} %bitcast.5), calls=%async_computation | async-start | bytes 131072 | tf_op jit(solution)/shard_map/all_to_all | solution.py:460
  16.2 32.0 %copy-start.11 = (s32[8]{0:T(128)}, s32[8]{0:T(128)S(1)}, u32[]{:S(2)}) copy-start(s32[8]{0:T(128)S(1)} %broadcast_xor_fusion.order) | copy-start | bytes 100
  26.5 15.6 %all-to-all-start.1 = ((f32[128,1,128]{2,1,0:T(1,128)}), f32[128,1,128]{2,1,0:T(1,128)S(1)}, u32[]{:S(2)}, u32[]{:S(2)}) async-start(f32[128,1,128]{2,1,0:T(1,128)} %broadcast_in_dim.4), calls=%async_computation.1 | async-start | bytes 131072 | tf_op jit(solution)/shard_map/all_to_all | solution.py:463
  49.0 4.2 %collective-permute-start = (f32[16,3072]{1,0:T(8,128)S(1)}, f32[16,3072]{1,0:T(8,128)S(1)}, u32[]{:S(2)}, u32[]{:S(2)}) collective-permute-start(f32[16,3072]{1,0:T(8,128)S(1)} %get-tuple-element.53.rest_9_), channel_id=1, source_target_pairs={{0,1},{1,0},{2,3},{3,2},{4,5},{5,4},{6,7},{7,6},{8,9},{9,8},{10,11... | collective-permute-start | bytes 589832 | tf_op jit(solution)/shard_map/ppermute | solution.py:519
  49.8 6.5 %collective-permute-start.1 = (f32[16,3072]{1,0:T(8,128)S(1)}, f32[16,3072]{1,0:T(8,128)S(1)}, u32[]{:S(2)}, u32[]{:S(2)}) collective-permute-start(f32[16,3072]{1,0:T(8,128)S(1)} %get-tuple-element.54.rest_10_), channel_id=1, source_target_pairs={{0,2},{1,3},{2,0},{3,1},{4,6},{5,7},{6,4},{7,5},{8,10},{9,11},{10,... | collective-permute-start | bytes 589832 | tf_op jit(solution)/shard_map/ppermute | solution.py:519
  50.1 7.3 %collective-permute-start.2 = (f32[16,3072]{1,0:T(8,128)S(1)}, f32[16,3072]{1,0:T(8,128)S(1)}, u32[]{:S(2)}, u32[]{:S(2)}) collective-permute-start(f32[16,3072]{1,0:T(8,128)S(1)} %get-tuple-element.55.rest_11_), channel_id=1, source_target_pairs={{0,6},{1,7},{2,4},{3,5},{4,2},{5,3},{6,0},{7,1},{8,14},{9,15},{10,... | collective-permute-start | bytes 589832 | tf_op jit(solution)/shard_map/ppermute | solution.py:519
  57.5 20.0 %collective-permute-start.3 = (f32[16,3072]{1,0:T(8,128)S(1)}, f32[16,3072]{1,0:T(8,128)S(1)}, u32[]{:S(2)}, u32[]{:S(2)}) collective-permute-start(f32[16,3072]{1,0:T(8,128)S(1)} %get-tuple-element.60.rest_12_), channel_id=1, source_target_pairs={{0,3},{1,2},{2,1},{3,0},{4,7},{5,6},{6,5},{7,4},{8,11},{9,10},{10,... | collective-permute-start | bytes 589832 | tf_op jit(solution)/shard_map/ppermute | solution.py:519
  58.5 19.0 %collective-permute-start.4 = (f32[16,3072]{1,0:T(8,128)S(1)}, f32[16,3072]{1,0:T(8,128)S(1)}, u32[]{:S(2)}, u32[]{:S(2)}) collective-permute-start(f32[16,3072]{1,0:T(8,128)S(1)} %get-tuple-element.61.rest_13_), channel_id=1, source_target_pairs={{0,7},{1,6},{2,5},{3,4},{4,3},{5,2},{6,1},{7,0},{8,15},{9,14},{10,... | collective-permute-start | bytes 589832 | tf_op jit(solution)/shard_map/ppermute | solution.py:519
  59.6 18.0 %collective-permute-start.5 = (f32[16,3072]{1,0:T(8,128)S(1)}, f32[16,3072]{1,0:T(8,128)S(1)}, u32[]{:S(2)}, u32[]{:S(2)}) collective-permute-start(f32[16,3072]{1,0:T(8,128)S(1)} %get-tuple-element.62.rest_14_), channel_id=1, source_target_pairs={{0,4},{1,5},{2,6},{3,7},{4,0},{5,1},{6,2},{7,3},{8,12},{9,13},{10,... | collective-permute-start | bytes 589832 | tf_op jit(solution)/shard_map/ppermute | solution.py:519
  61.0 16.5 %collective-permute-start.6 = (f32[16,3072]{1,0:T(8,128)S(1)}, f32[16,3072]{1,0:T(8,128)S(1)}, u32[]{:S(2)}, u32[]{:S(2)}) collective-permute-start(f32[16,3072]{1,0:T(8,128)S(1)} %get-tuple-element.63.rest_15_), channel_id=1, source_target_pairs={{0,5},{1,4},{2,7},{3,6},{4,1},{5,0},{6,3},{7,2},{8,13},{9,12},{10,... | collective-permute-start | bytes 589832 | tf_op jit(solution)/shard_map/ppermute | solution.py:519
  110.4 33.2 %all-to-all-start.2 = ((f32[16,216,128]{2,1,0:T(8,128)}), f32[16,216,128]{2,1,0:T(8,128)S(1)}, u32[]{:S(2)}, u32[]{:S(2)}) async-start(f32[16,216,128]{2,1,0:T(8,128)} %bitcast.121), calls=%async_computation.2 | async-start | bytes 3538944 | tf_op jit(solution)/shard_map/all_to_all | solution.py:582
  144.8 32.4 %all-to-all-start.3 = ((f32[16,216,128]{2,1,0:T(8,128)}), f32[16,216,128]{2,1,0:T(8,128)S(1)}, u32[]{:S(2)}, u32[]{:S(2)}) async-start(f32[16,216,128]{2,1,0:T(8,128)} %bitcast.120), calls=%async_computation.3 | async-start | bytes 3538944 | tf_op jit(solution)/shard_map/all_to_all | solution.py:582
  157.7 2.0 collective-permute-start.7
  160.6 6.7 %collective-permute-start.10 = (f32[288,128]{1,0:T(8,128)S(1)}, f32[288,128]{1,0:T(8,128)S(1)}, u32[]{:S(2)}, u32[]{:S(2)}) collective-permute-start(f32[288,128]{1,0:T(8,128)S(1)} %add.108), channel_id=1, source_target_pairs={{0,4},{1,5},{2,6},{3,7},{4,0},{5,1},{6,2},{7,3},{8,12},{9,13},{10,... | collective-permute-start | bytes 442376 | tf_op jit(solution)/shard_map/ppermute | solution.py:468
  162.2 7.5 %collective-permute-start.9 = (f32[288,128]{1,0:T(8,128)S(1)}, f32[288,128]{1,0:T(8,128)S(1)}, u32[]{:S(2)}, u32[]{:S(2)}) collective-permute-start(f32[288,128]{1,0:T(8,128)S(1)} %add.108), channel_id=1, source_target_pairs={{0,6},{1,7},{2,0},{3,1},{4,2},{5,3},{6,4},{7,5},{8,14},{9,15},{10,... | collective-permute-start | bytes 442376 | tf_op jit(solution)/shard_map/ppermute | solution.py:468
  164.0 6.5 %collective-permute-start.8 = (f32[288,128]{1,0:T(8,128)S(1)}, f32[288,128]{1,0:T(8,128)S(1)}, u32[]{:S(2)}, u32[]{:S(2)}) collective-permute-start(f32[288,128]{1,0:T(8,128)S(1)} %add.108), channel_id=1, source_target_pairs={{0,2},{1,3},{2,4},{3,5},{4,6},{5,7},{6,0},{7,1},{8,10},{9,11},{10,... | collective-permute-start | bytes 442376 | tf_op jit(solution)/shard_map/ppermute | solution.py:468
  178.5 33.1 %all-to-all-start.4 = ((f32[16,216,128]{2,1,0:T(8,128)}), f32[16,216,128]{2,1,0:T(8,128)}, u32[]{:S(2)}, u32[]{:S(2)}) async-start(f32[16,216,128]{2,1,0:T(8,128)} %bitcast.115), calls=%async_computation.4 | async-start | bytes 3538944 | tf_op jit(solution)/shard_map/all_to_all | solution.py:607
  190.9 2.9 collective-permute-start.11
  194.8 6.8 %collective-permute-start.14 = (f32[288,128]{1,0:T(8,128)S(1)}, f32[288,128]{1,0:T(8,128)S(1)}, u32[]{:S(2)}, u32[]{:S(2)}) collective-permute-start(f32[288,128]{1,0:T(8,128)S(1)} %add.113), channel_id=1, source_target_pairs={{0,4},{1,5},{2,6},{3,7},{4,0},{5,1},{6,2},{7,3},{8,12},{9,13},{10,... | collective-permute-start | bytes 442376 | tf_op jit(solution)/shard_map/ppermute | solution.py:468
  196.1 7.6 %collective-permute-start.13 = (f32[288,128]{1,0:T(8,128)S(1)}, f32[288,128]{1,0:T(8,128)S(1)}, u32[]{:S(2)}, u32[]{:S(2)}) collective-permute-start(f32[288,128]{1,0:T(8,128)S(1)} %add.113), channel_id=1, source_target_pairs={{0,6},{1,7},{2,0},{3,1},{4,2},{5,3},{6,4},{7,5},{8,14},{9,15},{10,... | collective-permute-start | bytes 442376 | tf_op jit(solution)/shard_map/ppermute | solution.py:468
  197.7 7.1 %collective-permute-start.12 = (f32[288,128]{1,0:T(8,128)S(1)}, f32[288,128]{1,0:T(8,128)S(1)}, u32[]{:S(2)}, u32[]{:S(2)}) collective-permute-start(f32[288,128]{1,0:T(8,128)S(1)} %add.113), channel_id=1, source_target_pairs={{0,2},{1,3},{2,4},{3,5},{4,6},{5,7},{6,0},{7,1},{8,10},{9,11},{10,... | collective-permute-start | bytes 442376 | tf_op jit(solution)/shard_map/ppermute | solution.py:468
  274.4 23.2 %collective-permute-start.15 = (f32[16,3072]{1,0:T(8,128)}, f32[16,3072]{1,0:T(8,128)S(1)}, u32[]{:S(2)}, u32[]{:S(2)}) collective-permute-start(f32[16,3072]{1,0:T(8,128)} %get-tuple-element.80.rest_0_), channel_id=1, source_target_pairs={{0,3},{1,2},{2,1},{3,0},{4,7},{5,6},{6,5},{7,4},{8,11},{9,10},{10,... | collective-permute-start | bytes 589832 | tf_op jit(solution)/shard_map/ppermute | solution.py:519
  278.0 19.5 %collective-permute-start.16 = (f32[16,3072]{1,0:T(8,128)}, f32[16,3072]{1,0:T(8,128)S(1)}, u32[]{:S(2)}, u32[]{:S(2)}) collective-permute-start(f32[16,3072]{1,0:T(8,128)} %get-tuple-element.81.rest_1_), channel_id=1, source_target_pairs={{0,7},{1,6},{2,5},{3,4},{4,3},{5,2},{6,1},{7,0},{8,15},{9,14},{10,... | collective-permute-start | bytes 589832 | tf_op jit(solution)/shard_map/ppermute | solution.py:519
  278.9 18.7 %collective-permute-start.17 = (f32[16,3072]{1,0:T(8,128)}, f32[16,3072]{1,0:T(8,128)S(1)}, u32[]{:S(2)}, u32[]{:S(2)}) collective-permute-start(f32[16,3072]{1,0:T(8,128)} %get-tuple-element.82.rest_2_), channel_id=1, source_target_pairs={{0,4},{1,5},{2,6},{3,7},{4,0},{5,1},{6,2},{7,3},{8,12},{9,13},{10,... | collective-permute-start | bytes 589832 | tf_op jit(solution)/shard_map/ppermute | solution.py:519
  280.0 17.6 %collective-permute-start.18 = (f32[16,3072]{1,0:T(8,128)}, f32[16,3072]{1,0:T(8,128)S(1)}, u32[]{:S(2)}, u32[]{:S(2)}) collective-permute-start(f32[16,3072]{1,0:T(8,128)} %get-tuple-element.83.rest_3_), channel_id=1, source_target_pairs={{0,5},{1,4},{2,7},{3,6},{4,1},{5,0},{6,3},{7,2},{8,13},{9,12},{10,... | collective-permute-start | bytes 589832 | tf_op jit(solution)/shard_map/ppermute | solution.py:519
  297.6 3.3 collective-permute-start.19
  297.7 6.4 %collective-permute-start.20 = (f32[16,3072]{1,0:T(8,128)}, f32[16,3072]{1,0:T(8,128)S(1)}, u32[]{:S(2)}, u32[]{:S(2)}) collective-permute-start(f32[16,3072]{1,0:T(8,128)} %get-tuple-element.90), channel_id=1, source_target_pairs={{0,2},{1,3},{2,0},{3,1},{4,6},{5,7},{6,4},{7,5},{8,10},{9,11},{10,... | collective-permute-start | bytes 589832 | tf_op jit(solution)/shard_map/ppermute | solution.py:519
  298.5 7.2 %collective-permute-start.21 = (f32[16,3072]{1,0:T(8,128)}, f32[16,3072]{1,0:T(8,128)S(1)}, u32[]{:S(2)}, u32[]{:S(2)}) collective-permute-start(f32[16,3072]{1,0:T(8,128)} %get-tuple-element.91), channel_id=1, source_target_pairs={{0,6},{1,7},{2,4},{3,5},{4,2},{5,3},{6,0},{7,1},{8,14},{9,15},{10,... | collective-permute-start | bytes 589832 | tf_op jit(solution)/shard_map/ppermute | solution.py:519
  310.7 14.7 %all-to-all-start.6 = ((f32[128,1,128]{2,1,0:T(1,128)}), f32[128,1,128]{2,1,0:T(1,128)S(1)}, u32[]{:S(2)}, u32[]{:S(2)}) async-start(f32[128,1,128]{2,1,0:T(1,128)} %bitcast.133), calls=%async_computation.6 | async-start | bytes 131072 | tf_op jit(solution)/shard_map/all_to_all | solution.py:460
  326.2 14.9 %all-to-all-start.7 = ((f32[128,1,128]{2,1,0:T(1,128)}), f32[128,1,128]{2,1,0:T(1,128)S(1)}, u32[]{:S(2)}, u32[]{:S(2)}) async-start(f32[128,1,128]{2,1,0:T(1,128)} %broadcast_in_dim.5), calls=%async_computation.7 | async-start | bytes 131072 | tf_op jit(solution)/shard_map/all_to_all | solution.py:463
  (51 other events, 312.1 us)

commit v5 on v4

--- a/solution.py
+++ b/solution.py
@@ -20,6 +20,7 @@
 GY = G // PW
 ORDER = (0, 1, 2, 6, 3, 7, 4, 5)
 HELD = BD // 2
+FIRST = NPW // (PW * BD) // 2
 PARTS = 2
 BLOCKS = ((0, 6), (1, 11), (2, 10), (3, 9), (4, 8), (5, 7))
 PAIRS = len(BLOCKS) // PARTS
@@ -171,34 +172,34 @@
     lax.fori_loop(0, SLAB // 256, clear, 0)
 
 
-def place_kernel(first, cells, *rest):
+def place_kernel(cells, *rest):
     blocks, (dense, turned) = rest[:HELD], rest[-2:]
-    empty = jnp.zeros((HELD * LB, LANES), f32)
 
     def turn(i, carry):
         at = pl.multiple_of(i * LANES, LANES)
-        rows = [block[:, pl.ds(at, LANES)] for block in blocks]
-        rows = [empty, *rows] if first else [*rows, empty]
+        rows = [block[:, pl.ds(half * FIRST + at, LANES)] for half in range(2) for block in blocks]
         turned[pl.ds(at, LANES), :] = jnp.concatenate(rows, axis=0).T
         return carry
 
-    lax.fori_loop(0, KW // LANES, turn, 0)
+    lax.fori_loop(0, FIRST // LANES, turn, 0)
     masks = source_masks()
 
     def place(i, carry):
         for j in range(16):
             k = i * 16 + j
             row = turned[pl.ds(k, 1), :]
-            for p in range(HELD):
-                pltpu.store(dense.at[pl.ds(cells[p * KW + k], 1), :], row, mask=masks[first + p])
-        return carry
-
-    lax.fori_loop(0, KW // 16, place, 0)
+            for group in range(BD):
+                half, p = group // HELD, group % HELD
+                cell = cells[p * KW + half * FIRST + k]
+                pltpu.store(dense.at[pl.ds(cell, 1), :], row, mask=masks[group])
+        return carry
+
+    lax.fori_loop(0, FIRST // 16, place, 0)
 
 
 def fold_kernel(cells, *rest):
     given, zt, mh, ml, dense, sent0, sent1, turned, fields, high, low = rest[HELD:]
-    place_kernel(HELD, cells, *rest[:HELD], dense, turned)
+    place_kernel(cells, *rest[:HELD], dense, turned)
     table = zt[...]
 
     def along_z(i, carry):
@@ -325,29 +326,32 @@
     lax.fori_loop(0, GY * 3, along_z, 0)
 
 
-def pick_kernel(first, cells, dense, *rest):
+def pick_kernel(cells, dense, *rest):
     terms, turned = rest[-1 - HELD : -1], rest[-1]
     masks = source_masks()
 
     def pick(i, carry):
         for j in range(16):
             k = i * 16 + j
-            row = dense[pl.ds(cells[k], 1), :]
-            for p in range(1, HELD):
-                row = jnp.where(masks[first + p], dense[pl.ds(cells[p * KW + k], 1), :], row)
+            row = None
+            for group in range(BD):
+                half, p = group // HELD, group % HELD
+                value = dense[pl.ds(cells[p * KW + half * FIRST + k], 1), :]
+                row = value if row is None else jnp.where(masks[group], value, row)
             turned[pl.ds(k, 1), :] = row
         return carry
 
-    lax.fori_loop(0, KW // 16, pick, 0)
+    lax.fori_loop(0, FIRST // 16, pick, 0)
 
     def turn(i, carry):
         at = pl.multiple_of(i * LANES, LANES)
         rows = turned[pl.ds(at, LANES), :].T
-        for p in range(HELD):
-            terms[p][:, pl.ds(at, LANES)] = rows[(first + p) * LB : (first + p + 1) * LB]
-        return carry
-
-    lax.fori_loop(0, KW // LANES, turn, 0)
+        for group in range(BD):
+            half, p = group // HELD, group % HELD
+            terms[p][:, pl.ds(half * FIRST + at, LANES)] = rows[group * LB : (group + 1) * LB]
+        return carry
+
+    lax.fori_loop(0, FIRST // LANES, turn, 0)
 
 
 def rotate_kernel(order, weights, coefs, *rest):
@@ -455,12 +459,13 @@
     return zs[-1] / jnp.sqrt(frob_norm), (*ys, *zs, *ts)
 
 
-def total(values):
+def total(values, beside=()):
     axes = ("pw", "band")
     pieces = lax.all_to_all(values, axes, split_axis=0, concat_axis=0, tiled=True)
     row = jnp.sum(pieces, axis=0, keepdims=True)
+    row, *beside = lax.optimization_barrier((row, *beside))
     copies = jnp.broadcast_to(row, values.shape)
-    return lax.all_to_all(copies, axes, split_axis=0, concat_axis=0, tiled=True)
+    return lax.all_to_all(copies, axes, split_axis=0, concat_axis=0, tiled=True), beside
 
 
 def band_total(values):
@@ -518,7 +523,10 @@
             return block
         return lax.ppermute(block, "band", [(i, i ^ ORDER[p]) for i in range(BD)])
 
-    intersection = total(matmul(coefficients, coefficients.T)) / NPW
+    intersection, planes = total(matmul(coefficients, coefficients.T), (core_density, potential_ext))
+    intersection = intersection / NPW
+    core = [to_sums(planes[0], chosen[part]) + unused_lanes[part] for part in range(PARTS)]
+    external = [to_sums(planes[1], chosen[part]) for part in range(PARTS)]
     weights, iterates = loewdin(intersection)
     rotated = call(
         rotate_kernel,
@@ -528,7 +536,7 @@
         order,
         weights,
         coefficients,
-        unread=cells,
+        unread=(*cells, *core, *external),
         room=28,
     )
     near = [meet(rotated[p], p) for p in range(HELD)]
@@ -536,9 +544,9 @@
     *barred, dense = lax.optimization_barrier((*near, *rotated[HELD:], dense))
     blocks = [*barred[:HELD], *(meet(barred[p], p) for p in range(HELD, BD))]
     dense = call(
-        functools.partial(place_kernel, 0),
+        place_kernel,
         kept(SLAB, LANES),
-        [pltpu.VMEM((KW, LANES), f32)],
+        [pltpu.VMEM((FIRST, LANES), f32)],
         1,
         cells[0],
         *blocks[:HELD],
@@ -552,7 +560,7 @@
         fold_kernel,
         (kept(SLAB, LANES), array(ROWS, LANES), array(ROWS, LANES)),
         [
-            pltpu.VMEM((KW, LANES), f32),
+            pltpu.VMEM((FIRST, LANES), f32),
             pltpu.VMEM((12, GY * G, LANES), f32),
             pltpu.VMEM(halves_shape, bf16),
             pltpu.VMEM(halves_shape, bf16),
@@ -567,17 +575,13 @@
         room=28,
         micros=29,
     )
-    *sent, core_density, potential_ext, kinetic, occupancy = lax.optimization_barrier(
-        (*sent, core_density, potential_ext, kinetic, occupancy)
-    )
-    core = [to_sums(core_density, chosen[part]) + unused_lanes[part] for part in range(PARTS)]
-    external = [to_sums(potential_ext, chosen[part]) for part in range(PARTS)]
+    *sent, kinetic, occupancy = lax.optimization_barrier((*sent, kinetic, occupancy))
     share = lax.dynamic_slice_in_dim(occupancy / NB, band_pos * LB, LB)
     share = jnp.tile(share, XB * BD).reshape(1, WIDE)
     kinetic_row = kinetic.reshape(1, KW)
     occupancy_column = occupancy.reshape(NB, 1)
     exchange = functools.partial(lax.all_to_all, axis_name="pw", split_axis=0, concat_axis=0, tiled=True)
-    density, returned, after = [], [], [*core, *external]
+    density, returned, after = [], [], []
     for part in range(PARTS):
         received = exchange(sent[part])
         fields, sums = call(
@@ -623,9 +627,9 @@
     terms, after = [None, None], ()
     for side in (1, 0):
         terms[side] = call(
-            functools.partial(pick_kernel, side * HELD),
+            pick_kernel,
             [array(LB, KW)] * HELD,
-            [pltpu.VMEM((KW, LANES), f32)],
+            [pltpu.VMEM((FIRST, LANES), f32)],
             1,
             cells[side],
             held(dense),
@@ -652,7 +656,7 @@
         occupancy_column,
     )
     *density, partial = lax.optimization_barrier((*density, partial))
-    grad_weights = total(partial)
+    grad_weights, unneeded = total(partial)
     first = matmul(weights, grad_rotated)
     grad_coef = call(
         pullback_kernel, array(NB, KW), [], 0, grad_weights, intersection, *iterates, coefficients, first

time: 349 us -> 339 us (0.971)
  blocking collectives: 30.1 us -> 59.4 us
  waiting for transfers between devices: 78.4 us -> 49.7 us
  Pallas kernels: 131 us -> 126 us
    all_to_all x0 -> x1, blocking collectives: none -> 29.3 us  [shards(): received = exchange(sent[part])]
    all_to_all x2 -> x1, waiting for transfers between devices: 27.2 us -> 0.01 us  [shards(): received = exchange(sent[part])]
    pallas_call x13, Pallas kernels: 131 us -> 126 us  [call(): pl.pallas_call(kernel, out_shape=out_shapes, in_specs=[smem] * scalars +...]
    all_to_all x2 -> x1, starting transfers between devices: 7.75 us -> 4.02 us  [shards(): received = exchange(sent[part])]
  transfers between devices with their start and end apart: 29 -> 28, of which waited for: 17 -> 16; matrix products, arithmetic and copies ran while one was open for 5% -> 4% of each run, Pallas kernels for 16% -> 15%
where the time goes in v5:
time: 339 us; the launch traced here: 337 us
  Pallas kernels  126 us (37%)
  starting transfers between devices  66.2 us (20%)
  blocking collectives  59.4 us (18%)
  waiting for transfers between devices  49.7 us (15%)
  matrix products  13.8 us (4%)
  local copies, waits for them, and re-layouts  9.53 us (3%)
  between operations  7.35 us (2%)
  other arithmetic  5.52 us (2%)
    pallas_call x13, Pallas kernels, call(): pl.pallas_call(kernel, out_shape=out_shapes, in_specs=[smem] * scalars +...  126 us
    all_to_all x1, blocking collectives, shards(): returned.append(exchange(product))  30.1 us
    all_to_all x1, blocking collectives, shards(): received = exchange(sent[part])  29.3 us
    ppermute x14, starting transfers between devices, meet(): return lax.ppermute(block, 'band', [(i, i ^ ORDER[p]) for i in range(BD)])  17.2 us
    all_to_all x2, waiting for transfers between devices, total(): lax.all_to_all(copies, axes, split_axis=0, concat_axis=0, tiled=True)  16.9 us
    all_to_all x2, starting transfers between devices, total(): lax.all_to_all(values, axes, split_axis=0, concat_axis=0, tiled=True)  16.1 us
    dot_general x23, matrix products, matmul(): jnp.dot(left_side, right_side, precision=highest, preferred_element_type=...  13.8 us
    ppermute x6, waiting for transfers between devices, band_total(): lax.ppermute(values, 'band', [(i, (i + 2 * step) % BD) for i in range(BD)])  12.4 us
  transfers between devices with their start and end apart: 28, of which 16 were waited for; matrix products, arithmetic and copies ran while one was open for 4% of the time, Pallas kernels for 15%

profile of v5, /device:TPU:1, one launch (start us, length us, event | category | flops | bytes accessed | tf_op | source)
XLA Modules:
  0.0 337.4 jit_solution(10902462029176234764)
XLA Ops:
  0.7 4.0 %fusion.27 = f32[128,128]{1,0:T(8,128)} fusion(f32[128,3072]{1,0:T(8,128)} %coefs.3), kind=kOutput, calls=%fused_computation.57 | convolution fusion | flops 603979776 | bytes 1638400 | tf_op jit(solution)/shard_map/dot_general | solution.py:446
  4.7 11.5 %all-to-all-start = ((f32[128,1,128]{2,1,0:T(1,128)}), f32[128,1,128]{2,1,0:T(1,128)S(1)}, u32[]{:S(2)}, u32[]{:S(2)}) async-start(f32[128,1,128]{2,1,0:T(1,128)} %bitcast.1), calls=%async_computation | async-start | bytes 131072 | tf_op jit(solution)/shard_map/all_to_all | solution.py:464
  22.1 3.7 %all-to-all-done = f32[128,1,128]{2,1,0:T(1,128)S(1)} async-done(((f32[128,1,128]{2,1,0:T(1,128)}), f32[128,1,128]{2,1,0:T(1,128)S(1)}, u32[]{:S(2)}, u32[]{:S(2)}) %all-to-all-start) | async-done | bytes 65568 | tf_op jit(solution)/shard_map/all_to_all | solution.py:464
  28.0 6.1 %all-to-all-start.1 = ((f32[128,1,128]{2,1,0:T(1,128)}), f32[128,1,128]{2,1,0:T(1,128)S(1)}, u32[]{:S(2)}, u32[]{:S(2)}) async-start(f32[128,1,128]{2,1,0:T(1,128)} %broadcast_in_dim.9), calls=%async_computation.1 | async-start | bytes 131072 | tf_op jit(solution)/shard_map/all_to_all | solution.py:468
  35.3 8.3 %all-to-all-done.1 = f32[128,1,128]{2,1,0:T(1,128)S(1)} async-done(((f32[128,1,128]{2,1,0:T(1,128)}), f32[128,1,128]{2,1,0:T(1,128)S(1)}, u32[]{:S(2)}, u32[]{:S(2)}) %all-to-all-start.1) | async-done | bytes 65568 | tf_op jit(solution)/shard_map/all_to_all | solution.py:468
  54.7 3.1 collective-permute-done.1.rest_2_
  64.5 12.9 %shard_map.358.rest_4_ = f32[55296,128]{1,0:T(8,128)S(1)} custom-call(s32[12288]{0:T(1024)} %copy-done.4, f32[16,3072]{1,0:T(8,128)} %copy-done.1, f32[16,3072]{1,0:T(8,128)} %copy-done.29, f32[16,3072]{1,0:T(8,128)} %copy-done.31, f32[16,3072]{1,0:T(8,128)} %copy-done.33, f32[55296,128]{1,0:T(8,128)S(1)} %shard_map.357.rest_4_), custom_call_target="tpu_custom_call", output_to_operand_aliasing={{}: (5, {})} | custom-call | bytes 49000000 | tf_op jit(solution)/shard_map/pallas_call | solution.py:419
  78.9 30.4 %shard_map.359 = (f32[55296,128]{1,0:T(8,128)S(1)}, f32[3456,128]{1,0:T(8,128)}, f32[3456,128]{1,0:T(8,128)}) custom-call(s32[12288]{0:T(1024)} %copy-done.5, f32[16,3072]{1,0:T(8,128)} %copy-done.30, f32[16,3072]{1,0:T(8,128)} %copy-done.32, f32[16,3072]{1,0:T(8,128)} %copy-done.34, f32[16,3072]{1,0:T(8,128)} %copy-done.35, ...), custom_call_target="tpu_custom_call", output_to_operand_aliasing={{0}: (5, {})} | custom-call | bytes 101500000 | tf_op jit(solution)/shard_map/pallas_call | solution.py:419
  109.3 29.3 %all_to_all.76 = f32[16,216,128]{2,1,0:T(8,128)} all-to-all(f32[16,216,128]{2,1,0:T(8,128)} %bitcast.129), channel_id=1, replica_groups=mesh['pw'=16,'band'=8] {'pw'}, dimensions={0} | all-to-all | bytes 3538944 | tf_op jit(solution)/shard_map/all_to_all | solution.py:586
  138.6 4.0 %all-to-all-start.3 = ((f32[16,216,128]{2,1,0:T(8,128)}), f32[16,216,128]{2,1,0:T(8,128)S(1)}, u32[]{:S(2)}, u32[]{:S(2)}) async-start(f32[16,216,128]{2,1,0:T(8,128)} %bitcast.128), calls=%async_computation.3 | async-start | bytes 3538944 | tf_op jit(solution)/shard_map/all_to_all | solution.py:586
  143.4 5.7 %shard_map.360 = (f32[3456,128]{1,0:T(8,128)}, f32[288,128]{1,0:T(8,128)}) custom-call(f32[3456,128]{1,0:T(8,128)} %bitcast.124, bf16[192,96]{1,0:T(8,128)(2,1)} %constant.95.clone.yt, bf16[768,128]{1,0:T(8,128)(2,1)} %constant.96.clone.pack0, bf16[768,128]{1,0:T(8,128)(2,1)} %constant.97.clone.pack1, f32[1,768]{1,0:T(1,128)} %reshape_tile.3.share), custom_call_target="tpu_custom_call" | custom-call | bytes 10500000 | tf_op jit(solution)/shard_map/pallas_call | solution.py:419
  153.9 2.6 collective-permute-start.9
  158.9 2.5 collective-permute-done.9
  162.9 6.0 %shard_map.361.rest_0_ = f32[3456,128]{1,0:T(8,128)} custom-call(f32[288,128]{1,0:T(8,128)} %add_add_fusion.1.density, f32[288,128]{1,0:T(8,128)} %bitcast.122, f32[3456,128]{1,0:T(8,128)} %get-tuple-element.79.fields, bf16[192,96]{1,0:T(8,128)(2,1)} %constant.98.clone.yt, bf16[128,768]{1,0:T(8,128)(2,1)} %constant.99.clone.open0, ...), custom_call_target="tpu_custom_call" | custom-call | bytes 10500000 | tf_op jit(solution)/shard_map/pallas_call | solution.py:419
  170.2 6.7 %all-to-all-start.4 = ((f32[16,216,128]{2,1,0:T(8,128)}), f32[16,216,128]{2,1,0:T(8,128)}, u32[]{:S(2)}, u32[]{:S(2)}) async-start(f32[16,216,128]{2,1,0:T(8,128)} %bitcast.123), calls=%async_computation.4 | async-start | bytes 3538944 | tf_op jit(solution)/shard_map/all_to_all | solution.py:611
  176.9 5.7 %shard_map.362 = (f32[3456,128]{1,0:T(8,128)}, f32[288,128]{1,0:T(8,128)}) custom-call(f32[3456,128]{1,0:T(8,128)} %bitcast.125, bf16[192,96]{1,0:T(8,128)(2,1)} %constant.95.clone.yt, bf16[768,128]{1,0:T(8,128)(2,1)} %constant.96.clone.pack0, bf16[768,128]{1,0:T(8,128)(2,1)} %constant.97.clone.pack1, f32[1,768]{1,0:T(1,128)} %reshape_tile.3.share, ...), custom_call_target="tpu_custom_call" | custom-call | bytes 10500000 | tf_op jit(solution)/shard_map/pallas_call | solution.py:419
  190.2 3.5 %collective-permute-done.14 = f32[288,128]{1,0:T(8,128)S(1)} collective-permute-done((f32[288,128]{1,0:T(8,128)S(1)}, f32[288,128]{1,0:T(8,128)S(1)}, u32[]{:S(2)}, u32[]{:S(2)}) %collective-permute-start.14) | collective-permute-done | bytes 147488 | tf_op jit(solution)/shard_map/ppermute | solution.py:473
  197.6 6.0 %shard_map.363 = f32[3456,128]{1,0:T(8,128)} custom-call(f32[288,128]{1,0:T(8,128)} %add_add_fusion.density, f32[288,128]{1,0:T(8,128)} %bitcast.120, f32[3456,128]{1,0:T(8,128)} %get-tuple-element.81.fields, bf16[192,96]{1,0:T(8,128)(2,1)} %constant.98.clone.yt, bf16[128,768]{1,0:T(8,128)(2,1)} %constant.99.clone.open0, bf16[128,768]{1,0:T(8,128)(2,1)} %constant.100.clone.open1), custom_call_target="tpu_custom_call" | custom-call | bytes 10500000 | tf_op jit(solution)/shard_map/pallas_call | solution.py:419
  203.6 30.1 %all_to_all.77 = f32[16,216,128]{2,1,0:T(8,128)} all-to-all(f32[16,216,128]{2,1,0:T(8,128)} %bitcast.126), channel_id=1, replica_groups=mesh['pw'=16,'band'=8] {'pw'}, dimensions={0} | all-to-all | bytes 3538944 | tf_op jit(solution)/shard_map/all_to_all | solution.py:611
  233.8 17.4 %shard_map.364.dense = f32[55296,128]{1,0:T(8,128)S(1)} custom-call(f32[3456,128]{1,0:T(8,128)} %bitcast.33.recv0, f32[3456,128]{1,0:T(8,128)} %bitcast.127, bf16[192,96]{1,0:T(8,128)(2,1)} %constant.101.clone.zt, bf16[6,256,256]{2,1,0:T(8,128)(2,1)} %constant.102.clone.mh, bf16[6,256,256]{2,1,0:T(8,128)(2,1)} %constant.103.clone.ml), custom_call_target="tpu_custom_call" | custom-call | bytes 45500000 | tf_op jit(solution)/shard_map/pallas_call | solution.py:419
  251.2 13.7 %shard_map.365 = (f32[16,3072]{1,0:T(8,128)}, f32[16,3072]{1,0:T(8,128)}, f32[16,3072]{1,0:T(8,128)}, f32[16,3072]{1,0:T(8,128)}) custom-call(s32[12288]{0:T(1024)} %copy-done.5, f32[55296,128]{1,0:T(8,128)S(1)} %shard_map.364.dense), custom_call_target="tpu_custom_call" | custom-call | bytes 49000000 | tf_op jit(solution)/shard_map/pallas_call | solution.py:419
  264.8 3.1 collective-permute-start.15
  270.1 3.4 %collective-permute-start.18 = (f32[16,3072]{1,0:T(8,128)}, f32[16,3072]{1,0:T(8,128)S(1)}, u32[]{:S(2)}, u32[]{:S(2)}) collective-permute-start(f32[16,3072]{1,0:T(8,128)} %get-tuple-element.85.rest_3_), channel_id=1, source_target_pairs={{0,5},{1,4},{2,7},{3,6},{4,1},{5,0},{6,3},{7,2},{8,13},{9,12},{10,... | collective-permute-start | bytes 589832 | tf_op jit(solution)/shard_map/ppermute | solution.py:524
  273.6 13.7 %shard_map.366 = (f32[16,3072]{1,0:T(8,128)}, f32[16,3072]{1,0:T(8,128)}, f32[16,3072]{1,0:T(8,128)}, f32[16,3072]{1,0:T(8,128)}) custom-call(s32[12288]{0:T(1024)} %copy-done.4, f32[55296,128]{1,0:T(8,128)S(1)} %shard_map.364.dense, f32[16,3072]{1,0:T(8,128)} %get-tuple-element.82.rest_0_, f32[16,3072]{1,0:T(8,128)} %get-tuple-element.83.rest_1_, ...), custom_call_target="tpu_custom_call" | custom-call | bytes 49000000 | tf_op jit(solution)/shard_map/pallas_call | solution.py:419
  289.7 4.1 %collective-permute-done.20.rest_2_ = f32[16,3072]{1,0:T(8,128)S(1)} collective-permute-done((f32[16,3072]{1,0:T(8,128)}, f32[16,3072]{1,0:T(8,128)S(1)}, u32[]{:S(2)}, u32[]{:S(2)}) %collective-permute-start.20) | collective-permute-done | bytes 196640 | tf_op jit(solution)/shard_map/ppermute | solution.py:524
  295.8 4.4 %shard_map.367 = (f32[128,3072]{1,0:T(8,128)}, f32[128,128]{1,0:T(8,128)}) custom-call(s32[8]{0:T(128)} %copy-done.13, f32[16,3072]{1,0:T(8,128)} %get-tuple-element.90.rest_0_, f32[16,3072]{1,0:T(8,128)} %copy-done.40, f32[16,3072]{1,0:T(8,128)} %copy-done.41, f32[16,3072]{1,0:T(8,128)} %copy-done.42, f32[16,3072]{1,0:T(8,128)} %copy-done.36, ...), custom_call_target="tpu_custom_call" | custom-call | bytes 10500000 | tf_op jit(solution)/shard_map/pallas_call | solution.py:419
  300.2 4.6 %all-to-all-start.6 = ((f32[128,1,128]{2,1,0:T(1,128)}), f32[128,1,128]{2,1,0:T(1,128)S(1)}, u32[]{:S(2)}, u32[]{:S(2)}) async-start(f32[128,1,128]{2,1,0:T(1,128)} %bitcast.137), calls=%async_computation.6 | async-start | bytes 131072 | tf_op jit(solution)/shard_map/all_to_all | solution.py:464
  305.5 4.0 %fusion.31.first = f32[128,3072]{1,0:T(8,128)} fusion(f32[128,128]{1,0:T(8,128)S(1)} %get-tuple-element.124.weights, f32[128,3072]{1,0:T(8,128)} %get-tuple-element.101), kind=kOutput, calls=%fused_computation.61 | convolution fusion | flops 603979776 | bytes 3211264 | tf_op jit(solution)/shard_map/dot_general | solution.py:446
  310.1 4.5 %all-to-all-done.6 = f32[128,1,128]{2,1,0:T(1,128)S(1)} async-done(((f32[128,1,128]{2,1,0:T(1,128)}), f32[128,1,128]{2,1,0:T(1,128)S(1)}, u32[]{:S(2)}, u32[]{:S(2)}) %all-to-all-start.6) | async-done | bytes 65568 | tf_op jit(solution)/shard_map/all_to_all | solution.py:464
  315.4 5.4 %all-to-all-start.7 = ((f32[128,1,128]{2,1,0:T(1,128)}), f32[128,1,128]{2,1,0:T(1,128)S(1)}, u32[]{:S(2)}, u32[]{:S(2)}) async-start(f32[128,1,128]{2,1,0:T(1,128)} %broadcast_in_dim.21), calls=%async_computation.7 | async-start | bytes 131072 | tf_op jit(solution)/shard_map/all_to_all | solution.py:468
  321.8 8.5 %all-to-all-done.7 = f32[128,1,128]{2,1,0:T(1,128)S(1)} async-done(((f32[128,1,128]{2,1,0:T(1,128)}), f32[128,1,128]{2,1,0:T(1,128)S(1)}, u32[]{:S(2)}, u32[]{:S(2)}) %all-to-all-start.7) | async-done | bytes 65568 | tf_op jit(solution)/shard_map/all_to_all | solution.py:468
  331.0 6.5 %shard_map.368 = f32[128,3072]{1,0:T(8,128)} custom-call(f32[128,128]{1,0:T(8,128)} %bitcast.136, f32[128,128]{1,0:T(8,128)} %multiply_bitcast_fusion.s, f32[128,128]{1,0:T(8,128)} %copy-done.17, f32[128,128]{1,0:T(8,128)} %copy-done.23, f32[128,128]{1,0:T(8,128)} %copy-done.19, f32[128,128]{1,0:T(8,128)} %copy-done.24, ...), custom_call_target="tpu_custom_call" | custom-call | bytes 10500000 | tf_op jit(solution)/shard_map/pallas_call | solution.py:419
  (199 shorter events, 54.3 us)
Async XLA Ops:
  0.7 25.7 %copy-start.43 = (f32[96,128,1]{1,0,2:T(8,128)S(1)}, f32[96,128,1]{1,0,2:T(8,128)}, u32[]{:S(2)}) copy-start(f32[96,128,1]{1,0,2:T(8,128)} %constant.110) | copy-start | bytes 147460
  4.7 21.0 %all-to-all-start = ((f32[128,1,128]{2,1,0:T(1,128)}), f32[128,1,128]{2,1,0:T(1,128)S(1)}, u32[]{:S(2)}, u32[]{:S(2)}) async-start(f32[128,1,128]{2,1,0:T(1,128)} %bitcast.1), calls=%async_computation | async-start | bytes 131072 | tf_op jit(solution)/shard_map/all_to_all | solution.py:464
  16.2 32.0 %copy-start.13 = (s32[8]{0:T(128)}, s32[8]{0:T(128)S(1)}, u32[]{:S(2)}) copy-start(s32[8]{0:T(128)S(1)} %broadcast_xor_fusion.order) | copy-start | bytes 100
  22.0 26.2 %copy-start.4 = (s32[12288]{0:T(1024)}, s32[12288]{0:T(1024)S(1)}, u32[]{:S(2)}) copy-start(s32[12288]{0:T(1024)S(1)} %get-tuple-element.127.rest_0_.cells) | copy-start | bytes 147460
  22.0 26.2 %copy-start.5 = (s32[12288]{0:T(1024)}, s32[12288]{0:T(1024)S(1)}, u32[]{:S(2)}) copy-start(s32[12288]{0:T(1024)S(1)} %get-tuple-element.126.rest_1_.cells) | copy-start | bytes 147460
  28.0 15.6 %all-to-all-start.1 = ((f32[128,1,128]{2,1,0:T(1,128)}), f32[128,1,128]{2,1,0:T(1,128)S(1)}, u32[]{:S(2)}, u32[]{:S(2)}) async-start(f32[128,1,128]{2,1,0:T(1,128)} %broadcast_in_dim.9), calls=%async_computation.1 | async-start | bytes 131072 | tf_op jit(solution)/shard_map/all_to_all | solution.py:468
  50.5 4.2 %collective-permute-start = (f32[16,3072]{1,0:T(8,128)S(1)}, f32[16,3072]{1,0:T(8,128)S(1)}, u32[]{:S(2)}, u32[]{:S(2)}) collective-permute-start(f32[16,3072]{1,0:T(8,128)S(1)} %get-tuple-element.57.rest_9_), channel_id=1, source_target_pairs={{0,1},{1,0},{2,3},{3,2},{4,5},{5,4},{6,7},{7,6},{8,9},{9,8},{10,11... | collective-permute-start | bytes 589832 | tf_op jit(solution)/shard_map/ppermute | solution.py:524
  51.3 6.5 %collective-permute-start.1 = (f32[16,3072]{1,0:T(8,128)S(1)}, f32[16,3072]{1,0:T(8,128)S(1)}, u32[]{:S(2)}, u32[]{:S(2)}) collective-permute-start(f32[16,3072]{1,0:T(8,128)S(1)} %get-tuple-element.58.rest_10_), channel_id=1, source_target_pairs={{0,2},{1,3},{2,0},{3,1},{4,6},{5,7},{6,4},{7,5},{8,10},{9,11},{10,... | collective-permute-start | bytes 589832 | tf_op jit(solution)/shard_map/ppermute | solution.py:524
  51.6 7.3 %collective-permute-start.2 = (f32[16,3072]{1,0:T(8,128)S(1)}, f32[16,3072]{1,0:T(8,128)S(1)}, u32[]{:S(2)}, u32[]{:S(2)}) collective-permute-start(f32[16,3072]{1,0:T(8,128)S(1)} %get-tuple-element.59.rest_11_), channel_id=1, source_target_pairs={{0,6},{1,7},{2,4},{3,5},{4,2},{5,3},{6,0},{7,1},{8,14},{9,15},{10,... | collective-permute-start | bytes 589832 | tf_op jit(solution)/shard_map/ppermute | solution.py:524
  59.0 18.4 %collective-permute-start.3 = (f32[16,3072]{1,0:T(8,128)S(1)}, f32[16,3072]{1,0:T(8,128)S(1)}, u32[]{:S(2)}, u32[]{:S(2)}) collective-permute-start(f32[16,3072]{1,0:T(8,128)S(1)} %get-tuple-element.64.rest_12_), channel_id=1, source_target_pairs={{0,3},{1,2},{2,1},{3,0},{4,7},{5,6},{6,5},{7,4},{8,11},{9,10},{10,... | collective-permute-start | bytes 589832 | tf_op jit(solution)/shard_map/ppermute | solution.py:524
  60.0 17.4 %collective-permute-start.4 = (f32[16,3072]{1,0:T(8,128)S(1)}, f32[16,3072]{1,0:T(8,128)S(1)}, u32[]{:S(2)}, u32[]{:S(2)}) collective-permute-start(f32[16,3072]{1,0:T(8,128)S(1)} %get-tuple-element.65.rest_13_), channel_id=1, source_target_pairs={{0,7},{1,6},{2,5},{3,4},{4,3},{5,2},{6,1},{7,0},{8,15},{9,14},{10,... | collective-permute-start | bytes 589832 | tf_op jit(solution)/shard_map/ppermute | solution.py:524
  61.1 16.4 %collective-permute-start.5 = (f32[16,3072]{1,0:T(8,128)S(1)}, f32[16,3072]{1,0:T(8,128)S(1)}, u32[]{:S(2)}, u32[]{:S(2)}) collective-permute-start(f32[16,3072]{1,0:T(8,128)S(1)} %get-tuple-element.66.rest_14_), channel_id=1, source_target_pairs={{0,4},{1,5},{2,6},{3,7},{4,0},{5,1},{6,2},{7,3},{8,12},{9,13},{10,... | collective-permute-start | bytes 589832 | tf_op jit(solution)/shard_map/ppermute | solution.py:524
  62.5 14.9 %collective-permute-start.6 = (f32[16,3072]{1,0:T(8,128)S(1)}, f32[16,3072]{1,0:T(8,128)S(1)}, u32[]{:S(2)}, u32[]{:S(2)}) collective-permute-start(f32[16,3072]{1,0:T(8,128)S(1)} %get-tuple-element.67.rest_15_), channel_id=1, source_target_pairs={{0,5},{1,4},{2,7},{3,6},{4,1},{5,0},{6,3},{7,2},{8,13},{9,12},{10,... | collective-permute-start | bytes 589832 | tf_op jit(solution)/shard_map/ppermute | solution.py:524
  138.6 30.3 %all-to-all-start.3 = ((f32[16,216,128]{2,1,0:T(8,128)}), f32[16,216,128]{2,1,0:T(8,128)S(1)}, u32[]{:S(2)}, u32[]{:S(2)}) async-start(f32[16,216,128]{2,1,0:T(8,128)} %bitcast.128), calls=%async_computation.3 | async-start | bytes 3538944 | tf_op jit(solution)/shard_map/all_to_all | solution.py:586
  149.1 2.3 collective-permute-start.7
  152.3 6.6 %collective-permute-start.10 = (f32[288,128]{1,0:T(8,128)S(1)}, f32[288,128]{1,0:T(8,128)S(1)}, u32[]{:S(2)}, u32[]{:S(2)}) collective-permute-start(f32[288,128]{1,0:T(8,128)S(1)} %add.108), channel_id=1, source_target_pairs={{0,4},{1,5},{2,6},{3,7},{4,0},{5,1},{6,2},{7,3},{8,12},{9,13},{10,... | collective-permute-start | bytes 442376 | tf_op jit(solution)/shard_map/ppermute | solution.py:473
  153.9 7.5 %collective-permute-start.9 = (f32[288,128]{1,0:T(8,128)S(1)}, f32[288,128]{1,0:T(8,128)S(1)}, u32[]{:S(2)}, u32[]{:S(2)}) collective-permute-start(f32[288,128]{1,0:T(8,128)S(1)} %add.108), channel_id=1, source_target_pairs={{0,6},{1,7},{2,0},{3,1},{4,2},{5,3},{6,4},{7,5},{8,14},{9,15},{10,... | collective-permute-start | bytes 442376 | tf_op jit(solution)/shard_map/ppermute | solution.py:473
  156.6 5.6 %collective-permute-start.8 = (f32[288,128]{1,0:T(8,128)S(1)}, f32[288,128]{1,0:T(8,128)S(1)}, u32[]{:S(2)}, u32[]{:S(2)}) collective-permute-start(f32[288,128]{1,0:T(8,128)S(1)} %add.108), channel_id=1, source_target_pairs={{0,2},{1,3},{2,4},{3,5},{4,6},{5,7},{6,0},{7,1},{8,10},{9,11},{10,... | collective-permute-start | bytes 442376 | tf_op jit(solution)/shard_map/ppermute | solution.py:473
  170.2 33.5 %all-to-all-start.4 = ((f32[16,216,128]{2,1,0:T(8,128)}), f32[16,216,128]{2,1,0:T(8,128)}, u32[]{:S(2)}, u32[]{:S(2)}) async-start(f32[16,216,128]{2,1,0:T(8,128)} %bitcast.123), calls=%async_computation.4 | async-start | bytes 3538944 | tf_op jit(solution)/shard_map/all_to_all | solution.py:611
  182.6 3.3 collective-permute-start.11
  186.9 6.8 %collective-permute-start.14 = (f32[288,128]{1,0:T(8,128)S(1)}, f32[288,128]{1,0:T(8,128)S(1)}, u32[]{:S(2)}, u32[]{:S(2)}) collective-permute-start(f32[288,128]{1,0:T(8,128)S(1)} %add.113), channel_id=1, source_target_pairs={{0,4},{1,5},{2,6},{3,7},{4,0},{5,1},{6,2},{7,3},{8,12},{9,13},{10,... | collective-permute-start | bytes 442376 | tf_op jit(solution)/shard_map/ppermute | solution.py:473
  188.7 6.7 %collective-permute-start.13 = (f32[288,128]{1,0:T(8,128)S(1)}, f32[288,128]{1,0:T(8,128)S(1)}, u32[]{:S(2)}, u32[]{:S(2)}) collective-permute-start(f32[288,128]{1,0:T(8,128)S(1)} %add.113), channel_id=1, source_target_pairs={{0,6},{1,7},{2,0},{3,1},{4,2},{5,3},{6,4},{7,5},{8,14},{9,15},{10,... | collective-permute-start | bytes 442376 | tf_op jit(solution)/shard_map/ppermute | solution.py:473
  189.7 7.2 %collective-permute-start.12 = (f32[288,128]{1,0:T(8,128)S(1)}, f32[288,128]{1,0:T(8,128)S(1)}, u32[]{:S(2)}, u32[]{:S(2)}) collective-permute-start(f32[288,128]{1,0:T(8,128)S(1)} %add.113), channel_id=1, source_target_pairs={{0,2},{1,3},{2,4},{3,5},{4,6},{5,7},{6,0},{7,1},{8,10},{9,11},{10,... | collective-permute-start | bytes 442376 | tf_op jit(solution)/shard_map/ppermute | solution.py:473
  264.8 22.4 %collective-permute-start.15 = (f32[16,3072]{1,0:T(8,128)}, f32[16,3072]{1,0:T(8,128)S(1)}, u32[]{:S(2)}, u32[]{:S(2)}) collective-permute-start(f32[16,3072]{1,0:T(8,128)} %get-tuple-element.82.rest_0_), channel_id=1, source_target_pairs={{0,3},{1,2},{2,1},{3,0},{4,7},{5,6},{6,5},{7,4},{8,11},{9,10},{10,... | collective-permute-start | bytes 589832 | tf_op jit(solution)/shard_map/ppermute | solution.py:524
  268.0 19.3 %collective-permute-start.16 = (f32[16,3072]{1,0:T(8,128)}, f32[16,3072]{1,0:T(8,128)S(1)}, u32[]{:S(2)}, u32[]{:S(2)}) collective-permute-start(f32[16,3072]{1,0:T(8,128)} %get-tuple-element.83.rest_1_), channel_id=1, source_target_pairs={{0,7},{1,6},{2,5},{3,4},{4,3},{5,2},{6,1},{7,0},{8,15},{9,14},{10,... | collective-permute-start | bytes 589832 | tf_op jit(solution)/shard_map/ppermute | solution.py:524
  268.9 18.4 %collective-permute-start.17 = (f32[16,3072]{1,0:T(8,128)}, f32[16,3072]{1,0:T(8,128)S(1)}, u32[]{:S(2)}, u32[]{:S(2)}) collective-permute-start(f32[16,3072]{1,0:T(8,128)} %get-tuple-element.84.rest_2_), channel_id=1, source_target_pairs={{0,4},{1,5},{2,6},{3,7},{4,0},{5,1},{6,2},{7,3},{8,12},{9,13},{10,... | collective-permute-start | bytes 589832 | tf_op jit(solution)/shard_map/ppermute | solution.py:524
  270.1 17.2 %collective-permute-start.18 = (f32[16,3072]{1,0:T(8,128)}, f32[16,3072]{1,0:T(8,128)S(1)}, u32[]{:S(2)}, u32[]{:S(2)}) collective-permute-start(f32[16,3072]{1,0:T(8,128)} %get-tuple-element.85.rest_3_), channel_id=1, source_target_pairs={{0,5},{1,4},{2,7},{3,6},{4,1},{5,0},{6,3},{7,2},{8,13},{9,12},{10,... | collective-permute-start | bytes 589832 | tf_op jit(solution)/shard_map/ppermute | solution.py:524
  287.3 2.3 collective-permute-start.19
  287.4 6.4 %collective-permute-start.20 = (f32[16,3072]{1,0:T(8,128)}, f32[16,3072]{1,0:T(8,128)S(1)}, u32[]{:S(2)}, u32[]{:S(2)}) collective-permute-start(f32[16,3072]{1,0:T(8,128)} %get-tuple-element.92), channel_id=1, source_target_pairs={{0,2},{1,3},{2,0},{3,1},{4,6},{5,7},{6,4},{7,5},{8,10},{9,11},{10,... | collective-permute-start | bytes 589832 | tf_op jit(solution)/shard_map/ppermute | solution.py:524
  287.5 7.6 %collective-permute-start.21 = (f32[16,3072]{1,0:T(8,128)}, f32[16,3072]{1,0:T(8,128)S(1)}, u32[]{:S(2)}, u32[]{:S(2)}) collective-permute-start(f32[16,3072]{1,0:T(8,128)} %get-tuple-element.93), channel_id=1, source_target_pairs={{0,6},{1,7},{2,4},{3,5},{4,2},{5,3},{6,0},{7,1},{8,14},{9,15},{10,... | collective-permute-start | bytes 589832 | tf_op jit(solution)/shard_map/ppermute | solution.py:524
  300.2 14.4 %all-to-all-start.6 = ((f32[128,1,128]{2,1,0:T(1,128)}), f32[128,1,128]{2,1,0:T(1,128)S(1)}, u32[]{:S(2)}, u32[]{:S(2)}) async-start(f32[128,1,128]{2,1,0:T(1,128)} %bitcast.137), calls=%async_computation.6 | async-start | bytes 131072 | tf_op jit(solution)/shard_map/all_to_all | solution.py:464
  315.4 14.9 %all-to-all-start.7 = ((f32[128,1,128]{2,1,0:T(1,128)}), f32[128,1,128]{2,1,0:T(1,128)S(1)}, u32[]{:S(2)}, u32[]{:S(2)}) async-start(f32[128,1,128]{2,1,0:T(1,128)} %broadcast_in_dim.21), calls=%async_computation.7 | async-start | bytes 131072 | tf_op jit(solution)/shard_map/all_to_all | solution.py:468
  (51 other events, 403.7 us)

commit v6 on v5

--- a/solution.py
+++ b/solution.py
@@ -244,10 +244,17 @@
                     ]
 
 
-def density_kernel(recv, yt, pack0, pack1, share, *rest):
+def lane_of(shape, dim, half):
+    wide = lax.broadcasted_iota(jnp.int32, shape, dim) // LB
+    lane = lax.broadcasted_iota(jnp.int32, shape, 1 - dim)
+    return jnp.where(wide + 64 * half == lane, 1.0, 0.0).astype(bf16)
+
+
+def density_kernel(recv, yt, share, *rest):
     fields, sums = rest[-2:]
     table = yt[...]
     weight = share[...]
+    first, second = [lane_of((WIDE, LANES), 0, half) for half in range(2)]
 
     def along_y(z, carry):
         data = [lines(recv, [y * COLS + z * XB + i for y in range(GY)]) for i in range(XB)]
@@ -256,7 +263,6 @@
             at = pl.multiple_of((z * XB + i) * G, G)
             fields[pl.ds(at, G), :] = out[:, i * LANES : (i + 1) * LANES]
         high, low = split(weight * out * out)
-        first, second = pack0[...], pack1[...]
         added = dot(high[:HALF], first) + dot(low[:HALF], first)
         added = added + (dot(high[HALF:], second) + dot(low[HALF:], second))
         sums[pl.ds(pl.multiple_of(z * HALF, HALF), HALF), :] = added
@@ -265,8 +271,9 @@
     lax.fori_loop(0, GY, along_y, 0)
 
 
-def potential_kernel(density, external, fields, yt, open0, open1, sent):
+def potential_kernel(density, external, fields, yt, sent):
     table = yt[...]
+    first, second = [lane_of((LANES, WIDE), 1, half) for half in range(2)]
 
     def along_y(z, carry):
         at = pl.multiple_of(z * HALF, HALF)
@@ -274,7 +281,6 @@
         root = jnp.exp(jnp.log(dens) * (1.0 / 3.0))
         root = root - (root - dens / (root * root)) * (1.0 / 3.0)
         high, low = split(external[pl.ds(at, HALF), :] - slater * root)
-        first, second = open0[...], open1[...]
         spread = [dot(high, first) + dot(low, first), dot(high, second) + dot(low, second)]
         value = [fields[pl.ds(pl.multiple_of((z * XB + i) * G, G), G), :] for i in range(XB)]
         product = jnp.concatenate(spread, axis=0) * jnp.concatenate(value, axis=1)
@@ -396,16 +402,26 @@
         out[:, part] = first[:, part] + dot3(both, split(coefs[:, part]))
 
 
+def dot_t(a, b):
+    return lax.dot_general(a, b, (((1,), (1,)), ((), ())), preferred_element_type=f32)
+
+
+def gram_kernel(coefs, out):
+    equal = jnp.zeros((NB, NB), f32)
+    mixed = jnp.zeros((NB, NB), f32)
+    for at in range(0, KW, 512):
+        high, low = split(coefs[:, pl.ds(at, 512)])
+        equal = equal + dot_t(high, high)
+        mixed = mixed + dot_t(high, low)
+    out[...] = equal + (mixed + mixed.T)
+
+
 def products_kernel(order, *rest):
     terms, rotated, (coefs, kinetic, occupancy, grads, sums) = rest[:BD], rest[BD : 2 * BD], rest[2 * BD :]
     for p in range(BD):
         rows = pl.ds(pl.multiple_of(order[p] * LB, LB), LB)
         grads[rows, :] = occupancy[rows, :] * (kinetic[...] * rotated[p][...] + terms[p][...])
     added = jnp.zeros((NB, NB), f32)
-
-    def dot_t(a, b):
-        return lax.dot_general(a, b, (((1,), (1,)), ((), ())), preferred_element_type=f32)
-
     for at in range(0, KW, 512):
         part = pl.ds(at, 512)
         a, b = split(coefs[:, part]), split(grads[:, part])
@@ -475,18 +491,14 @@
 
 
 def packings():
-    chosen = np.zeros((PARTS, 2, G, LANES))
-    packed = np.zeros((PARTS, 2, WIDE, LANES))
+    chosen = np.zeros((PARTS, 2, G, LANES), np.float32)
     for part in range(PARTS):
         blocks = [m for pair in BLOCKS[part * PAIRS : (part + 1) * PAIRS] for m in pair]
         for half in range(2):
             for i, m in enumerate(blocks):
                 for q in range(BD):
-                    lane = half * 64 + i * BD + q
-                    chosen[part, half, m + 12 * q, lane] = 1
-                    row = i * LANES + q * LB
-                    packed[part, half, row : row + LB, lane] = 1
-    return chosen, packed
+                    chosen[part, half, m + 12 * q, half * 64 + i * BD + q] = 1
+    return chosen
 
 
 def to_sums(planes, chosen):
@@ -505,10 +517,7 @@
 
 def shards(coefficients, occupancy, kinetic, cell_map, potential_ext, core_density):
     table = tables()
-    chosen, packed = packings()
-    chosen = chosen.astype(np.float32)
-    pack = packed[0].astype(ml_dtypes.bfloat16)
-    unpack = np.swapaxes(pack, 1, 2)
+    chosen = packings()
     unused_lanes = (1.0 - chosen.sum(axis=(1, 2))).astype(np.float32)
     pw_pos = lax.axis_index("pw")
     band_pos = lax.axis_index("band")
@@ -523,7 +532,7 @@
             return block
         return lax.ppermute(block, "band", [(i, i ^ ORDER[p]) for i in range(BD)])
 
-    intersection, planes = total(matmul(coefficients, coefficients.T), (core_density, potential_ext))
+    intersection, planes = total(call(gram_kernel, array(NB, NB), [], 0, coefficients), (core_density, potential_ext))
     intersection = intersection / NPW
     core = [to_sums(planes[0], chosen[part]) + unused_lanes[part] for part in range(PARTS)]
     external = [to_sums(planes[1], chosen[part]) for part in range(PARTS)]
@@ -591,9 +600,10 @@
             0,
             received,
             table["y_out"],
-            *pack,
             share,
             unread=after,
+            room=28,
+            micros=6,
         )
         density.append(core[part] + band_total(sums))
         product = call(
@@ -605,7 +615,8 @@
             external[part],
             fields,
             table["y_in"],
-            *unpack,
+            room=28,
+            micros=6,
         )
         after = [product]
         returned.append(exchange(product))

time: 339 us -> 331 us (0.976)
  Pallas kernels: 126 us -> 118 us
  matrix products: 13.8 us -> 9.7 us
  starting transfers between devices: 66.2 us -> 70.3 us
  waiting for transfers between devices: 49.7 us -> 53.3 us
    pallas_call x13 -> x14, Pallas kernels: 126 us -> 118 us  [call(): pl.pallas_call(kernel, out_shape=out_shapes, in_specs=[smem] * scalars +...]
    dot_general x23 -> x22, matrix products: 13.8 us -> 9.7 us  [matmul(): jnp.dot(left_side, right_side, precision=highest, preferred_element_type=...]
    ppermute x14, starting transfers between devices: 17.2 us -> 20.7 us  [meet(): return lax.ppermute(block, 'band', [(i, i ^ ORDER[p]) for i in range(BD)])]
  transfers between devices with their start and end apart: 28 -> 28, of which waited for: 16 -> 18; matrix products, arithmetic and copies ran while one was open for 4% -> 3% of each run, Pallas kernels for 15% -> 13%
where the time goes in v6:
time: 331 us; the launch traced here: 330 us
  Pallas kernels  118 us (36%)
  starting transfers between devices  70.3 us (21%)
  blocking collectives  58.4 us (18%)
  waiting for transfers between devices  53.3 us (16%)
  local copies, waits for them, and re-layouts  10 us (3%)
  matrix products  9.7 us (3%)
  between operations  7.48 us (2%)
    pallas_call x14, Pallas kernels, call(): pl.pallas_call(kernel, out_shape=out_shapes, in_specs=[smem] * scalars +...  118 us
    all_to_all x1, blocking collectives, shards(): returned.append(exchange(product))  29.9 us
    all_to_all x1, blocking collectives, shards(): received = exchange(sent[part])  28.5 us
    ppermute x14, starting transfers between devices, meet(): return lax.ppermute(block, 'band', [(i, i ^ ORDER[p]) for i in range(BD)])  20.7 us
    all_to_all x2, waiting for transfers between devices, total(): lax.all_to_all(copies, axes, split_axis=0, concat_axis=0, tiled=True)  16.8 us
    all_to_all x2, starting transfers between devices, total(): lax.all_to_all(values, axes, split_axis=0, concat_axis=0, tiled=True)  16 us
    ppermute x6, waiting for transfers between devices, band_total(): lax.ppermute(values, 'band', [(i, (i + 2 * step) % BD) for i in range(BD)])  11.7 us
    all_to_all x2, starting transfers between devices, total(): lax.all_to_all(copies, axes, split_axis=0, concat_axis=0, tiled=True)  11.4 us
  transfers between devices with their start and end apart: 28, of which 18 were waited for; matrix products, arithmetic and copies ran while one was open for 3% of the time, Pallas kernels for 13%

profile of v6, /device:TPU:1, one launch (start us, length us, event | category | flops | bytes accessed | tf_op | source)
XLA Modules:
  0.0 330.0 jit_solution(12193611403199743885)
XLA Ops:
  3.5 11.5 %all-to-all-start = ((f32[128,1,128]{2,1,0:T(1,128)}), f32[128,1,128]{2,1,0:T(1,128)S(1)}, u32[]{:S(2)}, u32[]{:S(2)}) async-start(f32[128,1,128]{2,1,0:T(1,128)} %bitcast.134), calls=%async_computation | async-start | bytes 131072 | tf_op jit(solution)/shard_map/all_to_all | solution.py:480
  20.8 3.7 %all-to-all-done = f32[128,1,128]{2,1,0:T(1,128)S(1)} async-done(((f32[128,1,128]{2,1,0:T(1,128)}), f32[128,1,128]{2,1,0:T(1,128)S(1)}, u32[]{:S(2)}, u32[]{:S(2)}) %all-to-all-start) | async-done | bytes 65568 | tf_op jit(solution)/shard_map/all_to_all | solution.py:480
  26.7 6.1 %all-to-all-start.1 = ((f32[128,1,128]{2,1,0:T(1,128)}), f32[128,1,128]{2,1,0:T(1,128)S(1)}, u32[]{:S(2)}, u32[]{:S(2)}) async-start(f32[128,1,128]{2,1,0:T(1,128)} %broadcast_in_dim.9), calls=%async_computation.1 | async-start | bytes 131072 | tf_op jit(solution)/shard_map/all_to_all | solution.py:484
  34.1 8.3 %all-to-all-done.1 = f32[128,1,128]{2,1,0:T(1,128)S(1)} async-done(((f32[128,1,128]{2,1,0:T(1,128)}), f32[128,1,128]{2,1,0:T(1,128)S(1)}, u32[]{:S(2)}, u32[]{:S(2)}) %all-to-all-start.1) | async-done | bytes 65568 | tf_op jit(solution)/shard_map/all_to_all | solution.py:484
  53.5 3.1 collective-permute-done.1.rest_2_
  63.2 12.9 %shard_map.287.rest_4_ = f32[55296,128]{1,0:T(8,128)S(1)} custom-call(s32[12288]{0:T(1024)} %copy-done.6, f32[16,3072]{1,0:T(8,128)} %copy-done.1, f32[16,3072]{1,0:T(8,128)} %copy-done.40, f32[16,3072]{1,0:T(8,128)} %copy-done.42, f32[16,3072]{1,0:T(8,128)} %copy-done.44, f32[55296,128]{1,0:T(8,128)S(1)} %shard_map.286.rest_4_), custom_call_target="tpu_custom_call", output_to_operand_aliasing={{}: (5, {})} | custom-call | bytes 49000000 | tf_op jit(solution)/shard_map/pallas_call | solution.py:435
  77.6 29.8 %shard_map.288 = (f32[55296,128]{1,0:T(8,128)S(1)}, f32[3456,128]{1,0:T(8,128)}, f32[3456,128]{1,0:T(8,128)}) custom-call(s32[12288]{0:T(1024)} %copy-done.7, f32[16,3072]{1,0:T(8,128)} %copy-done.41, f32[16,3072]{1,0:T(8,128)} %copy-done.43, f32[16,3072]{1,0:T(8,128)} %copy-done.45, f32[16,3072]{1,0:T(8,128)} %copy-done.46, ...), custom_call_target="tpu_custom_call", output_to_operand_aliasing={{0}: (5, {})} | custom-call | bytes 101500000 | tf_op jit(solution)/shard_map/pallas_call | solution.py:435
  107.5 28.5 %all_to_all.76 = f32[16,216,128]{2,1,0:T(8,128)S(1)} all-to-all(f32[16,216,128]{2,1,0:T(8,128)} %bitcast.126), channel_id=1, replica_groups=mesh['pw'=16,'band'=8] {'pw'}, dimensions={0} | all-to-all | bytes 3538944 | tf_op jit(solution)/shard_map/all_to_all | solution.py:595
  136.0 3.8 %all-to-all-start.3 = ((f32[16,216,128]{2,1,0:T(8,128)}), f32[16,216,128]{2,1,0:T(8,128)S(1)}, u32[]{:S(2)}, u32[]{:S(2)}) async-start(f32[16,216,128]{2,1,0:T(8,128)} %bitcast.125), calls=%async_computation.3 | async-start | bytes 3538944 | tf_op jit(solution)/shard_map/all_to_all | solution.py:595
  142.3 3.1 shard_map.289
  151.5 2.8 collective-permute-done.10
  154.3 2.9 collective-permute-done.9
  157.7 4.4 %shard_map.290.rest_0_ = f32[3456,128]{1,0:T(8,128)} custom-call(f32[288,128]{1,0:T(8,128)S(1)} %add_add_fusion.1.density, f32[288,128]{1,0:T(8,128)S(1)} %bitcast.123, f32[3456,128]{1,0:T(8,128)S(1)} %get-tuple-element.79.fields, bf16[192,96]{1,0:T(8,128)(2,1)S(1)} %copy-done.10), custom_call_target="tpu_custom_call" | custom-call | bytes 21000000 | tf_op jit(solution)/shard_map/pallas_call | solution.py:435
  162.1 3.2 all-to-all-done.3
  165.3 4.8 %all-to-all-start.4 = ((f32[16,216,128]{2,1,0:T(8,128)}), f32[16,216,128]{2,1,0:T(8,128)}, u32[]{:S(2)}, u32[]{:S(2)}) async-start(f32[16,216,128]{2,1,0:T(8,128)} %bitcast.32), calls=%async_computation.4 | async-start | bytes 3538944 | tf_op jit(solution)/shard_map/all_to_all | solution.py:622
  170.1 3.1 shard_map.291
  176.5 4.6 %collective-permute-start.14 = (f32[288,128]{1,0:T(8,128)S(1)}, f32[288,128]{1,0:T(8,128)S(1)}, u32[]{:S(2)}, u32[]{:S(2)}) collective-permute-start(f32[288,128]{1,0:T(8,128)S(1)} %add.113), channel_id=1, source_target_pairs={{0,4},{1,5},{2,6},{3,7},{4,0},{5,1},{6,2},{7,3},{8,12},{9,13},{10,... | collective-permute-start | bytes 442376 | tf_op jit(solution)/shard_map/ppermute | solution.py:489
  188.2 3.2 shard_map.292
  192.7 29.9 %all_to_all.77 = f32[16,216,128]{2,1,0:T(8,128)} all-to-all(f32[16,216,128]{2,1,0:T(8,128)S(1)} %bitcast.119), channel_id=1, replica_groups=mesh['pw'=16,'band'=8] {'pw'}, dimensions={0} | all-to-all | bytes 3538944 | tf_op jit(solution)/shard_map/all_to_all | solution.py:622
  222.5 17.4 %shard_map.293.dense = f32[55296,128]{1,0:T(8,128)S(1)} custom-call(f32[3456,128]{1,0:T(8,128)} %bitcast.33.recv0, f32[3456,128]{1,0:T(8,128)} %bitcast.124, bf16[192,96]{1,0:T(8,128)(2,1)} %constant.89.clone.zt, bf16[6,256,256]{2,1,0:T(8,128)(2,1)} %constant.90.clone.mh, bf16[6,256,256]{2,1,0:T(8,128)(2,1)} %constant.91.clone.ml), custom_call_target="tpu_custom_call" | custom-call | bytes 45500000 | tf_op jit(solution)/shard_map/pallas_call | solution.py:435
  239.9 13.7 %shard_map.294 = (f32[16,3072]{1,0:T(8,128)}, f32[16,3072]{1,0:T(8,128)}, f32[16,3072]{1,0:T(8,128)}, f32[16,3072]{1,0:T(8,128)}) custom-call(s32[12288]{0:T(1024)} %copy-done.7, f32[55296,128]{1,0:T(8,128)S(1)} %shard_map.293.dense), custom_call_target="tpu_custom_call" | custom-call | bytes 49000000 | tf_op jit(solution)/shard_map/pallas_call | solution.py:435
  253.6 4.4 %collective-permute-start.15 = (f32[16,3072]{1,0:T(8,128)}, f32[16,3072]{1,0:T(8,128)S(1)}, u32[]{:S(2)}, u32[]{:S(2)}) collective-permute-start(f32[16,3072]{1,0:T(8,128)} %get-tuple-element.82.rest_0_), channel_id=1, source_target_pairs={{0,3},{1,2},{2,1},{3,0},{4,7},{5,6},{6,5},{7,4},{8,11},{9,10},{10,... | collective-permute-start | bytes 589832 | tf_op jit(solution)/shard_map/ppermute | solution.py:533
  260.7 5.5 %collective-permute-start.18 = (f32[16,3072]{1,0:T(8,128)}, f32[16,3072]{1,0:T(8,128)S(1)}, u32[]{:S(2)}, u32[]{:S(2)}) collective-permute-start(f32[16,3072]{1,0:T(8,128)} %get-tuple-element.85.rest_3_), channel_id=1, source_target_pairs={{0,5},{1,4},{2,7},{3,6},{4,1},{5,0},{6,3},{7,2},{8,13},{9,12},{10,... | collective-permute-start | bytes 589832 | tf_op jit(solution)/shard_map/ppermute | solution.py:533
  266.2 13.7 %shard_map.295 = (f32[16,3072]{1,0:T(8,128)}, f32[16,3072]{1,0:T(8,128)}, f32[16,3072]{1,0:T(8,128)}, f32[16,3072]{1,0:T(8,128)}) custom-call(s32[12288]{0:T(1024)} %copy-done.6, f32[55296,128]{1,0:T(8,128)S(1)} %shard_map.293.dense, f32[16,3072]{1,0:T(8,128)} %get-tuple-element.82.rest_0_, f32[16,3072]{1,0:T(8,128)} %get-tuple-element.83.rest_1_, ...), custom_call_target="tpu_custom_call" | custom-call | bytes 49000000 | tf_op jit(solution)/shard_map/pallas_call | solution.py:435
  282.0 4.4 %collective-permute-done.20.rest_2_ = f32[16,3072]{1,0:T(8,128)S(1)} collective-permute-done((f32[16,3072]{1,0:T(8,128)}, f32[16,3072]{1,0:T(8,128)S(1)}, u32[]{:S(2)}, u32[]{:S(2)}) %collective-permute-start.20) | collective-permute-done | bytes 196640 | tf_op jit(solution)/shard_map/ppermute | solution.py:533
  288.5 4.4 %shard_map.296 = (f32[128,3072]{1,0:T(8,128)}, f32[128,128]{1,0:T(8,128)}) custom-call(s32[8]{0:T(128)} %copy-done.21, f32[16,3072]{1,0:T(8,128)} %get-tuple-element.90.rest_0_, f32[16,3072]{1,0:T(8,128)} %copy-done.51, f32[16,3072]{1,0:T(8,128)} %copy-done.52, f32[16,3072]{1,0:T(8,128)} %copy-done.53, f32[16,3072]{1,0:T(8,128)} %copy-done.47, ...), custom_call_target="tpu_custom_call" | custom-call | bytes 10500000 | tf_op jit(solution)/shard_map/pallas_call | solution.py:435
  292.9 4.5 %all-to-all-start.6 = ((f32[128,1,128]{2,1,0:T(1,128)}), f32[128,1,128]{2,1,0:T(1,128)S(1)}, u32[]{:S(2)}, u32[]{:S(2)}) async-start(f32[128,1,128]{2,1,0:T(1,128)} %bitcast.135), calls=%async_computation.6 | async-start | bytes 131072 | tf_op jit(solution)/shard_map/all_to_all | solution.py:480
  298.1 4.0 %fusion.30.first = f32[128,3072]{1,0:T(8,128)} fusion(f32[128,128]{1,0:T(8,128)S(1)} %copy-done.9, f32[128,3072]{1,0:T(8,128)} %get-tuple-element.101), kind=kOutput, calls=%fused_computation.60 | convolution fusion | flops 603979776 | bytes 3211264 | tf_op jit(solution)/shard_map/dot_general | solution.py:462
  302.7 4.6 %all-to-all-done.6 = f32[128,1,128]{2,1,0:T(1,128)S(1)} async-done(((f32[128,1,128]{2,1,0:T(1,128)}), f32[128,1,128]{2,1,0:T(1,128)S(1)}, u32[]{:S(2)}, u32[]{:S(2)}) %all-to-all-start.6) | async-done | bytes 65568 | tf_op jit(solution)/shard_map/all_to_all | solution.py:480
  308.0 5.4 %all-to-all-start.7 = ((f32[128,1,128]{2,1,0:T(1,128)}), f32[128,1,128]{2,1,0:T(1,128)S(1)}, u32[]{:S(2)}, u32[]{:S(2)}) async-start(f32[128,1,128]{2,1,0:T(1,128)} %broadcast_in_dim.21), calls=%async_computation.7 | async-start | bytes 131072 | tf_op jit(solution)/shard_map/all_to_all | solution.py:484
  314.4 8.5 %all-to-all-done.7 = f32[128,1,128]{2,1,0:T(1,128)S(1)} async-done(((f32[128,1,128]{2,1,0:T(1,128)}), f32[128,1,128]{2,1,0:T(1,128)S(1)}, u32[]{:S(2)}, u32[]{:S(2)}) %all-to-all-start.7) | async-done | bytes 65568 | tf_op jit(solution)/shard_map/all_to_all | solution.py:484
  323.6 6.5 %shard_map.297 = f32[128,3072]{1,0:T(8,128)} custom-call(f32[128,128]{1,0:T(8,128)} %bitcast.133, f32[128,128]{1,0:T(8,128)} %multiply_bitcast_fusion.s, f32[128,128]{1,0:T(8,128)} %copy-done.26, f32[128,128]{1,0:T(8,128)} %copy-done.34, f32[128,128]{1,0:T(8,128)} %copy-done.28, f32[128,128]{1,0:T(8,128)} %copy-done.35, ...), custom_call_target="tpu_custom_call" | custom-call | bytes 10500000 | tf_op jit(solution)/shard_map/pallas_call | solution.py:435
  (221 shorter events, 56.1 us)
Async XLA Ops:
  0.7 24.7 %copy-start.38 = (f32[6,9216]{1,0:T(8,128)S(1)}, f32[6,9216]{1,0:T(8,128)}, u32[]{:S(2)}) copy-start(f32[6,9216]{1,0:T(8,128)} %param.33) | copy-start | bytes 663556
  3.5 21.0 %all-to-all-start = ((f32[128,1,128]{2,1,0:T(1,128)}), f32[128,1,128]{2,1,0:T(1,128)S(1)}, u32[]{:S(2)}, u32[]{:S(2)}) async-start(f32[128,1,128]{2,1,0:T(1,128)} %bitcast.134), calls=%async_computation | async-start | bytes 131072 | tf_op jit(solution)/shard_map/all_to_all | solution.py:480
  15.0 32.0 %copy-start.21 = (s32[8]{0:T(128)}, s32[8]{0:T(128)S(1)}, u32[]{:S(2)}) copy-start(s32[8]{0:T(128)S(1)} %broadcast_xor_fusion.order) | copy-start | bytes 100
  20.8 26.2 %copy-start.6 = (s32[12288]{0:T(1024)}, s32[12288]{0:T(1024)S(1)}, u32[]{:S(2)}) copy-start(s32[12288]{0:T(1024)S(1)} %get-tuple-element.127.rest_0_.cells) | copy-start | bytes 147460
  20.8 26.2 %copy-start.7 = (s32[12288]{0:T(1024)}, s32[12288]{0:T(1024)S(1)}, u32[]{:S(2)}) copy-start(s32[12288]{0:T(1024)S(1)} %get-tuple-element.126.rest_1_.cells) | copy-start | bytes 147460
  26.7 15.6 %all-to-all-start.1 = ((f32[128,1,128]{2,1,0:T(1,128)}), f32[128,1,128]{2,1,0:T(1,128)S(1)}, u32[]{:S(2)}, u32[]{:S(2)}) async-start(f32[128,1,128]{2,1,0:T(1,128)} %broadcast_in_dim.9), calls=%async_computation.1 | async-start | bytes 131072 | tf_op jit(solution)/shard_map/all_to_all | solution.py:484
  49.3 4.2 %collective-permute-start = (f32[16,3072]{1,0:T(8,128)S(1)}, f32[16,3072]{1,0:T(8,128)S(1)}, u32[]{:S(2)}, u32[]{:S(2)}) collective-permute-start(f32[16,3072]{1,0:T(8,128)S(1)} %get-tuple-element.57.rest_9_), channel_id=1, source_target_pairs={{0,1},{1,0},{2,3},{3,2},{4,5},{5,4},{6,7},{7,6},{8,9},{9,8},{10,11... | collective-permute-start | bytes 589832 | tf_op jit(solution)/shard_map/ppermute | solution.py:533
  50.1 6.5 %collective-permute-start.1 = (f32[16,3072]{1,0:T(8,128)S(1)}, f32[16,3072]{1,0:T(8,128)S(1)}, u32[]{:S(2)}, u32[]{:S(2)}) collective-permute-start(f32[16,3072]{1,0:T(8,128)S(1)} %get-tuple-element.58.rest_10_), channel_id=1, source_target_pairs={{0,2},{1,3},{2,0},{3,1},{4,6},{5,7},{6,4},{7,5},{8,10},{9,11},{10,... | collective-permute-start | bytes 589832 | tf_op jit(solution)/shard_map/ppermute | solution.py:533
  50.4 7.3 %collective-permute-start.2 = (f32[16,3072]{1,0:T(8,128)S(1)}, f32[16,3072]{1,0:T(8,128)S(1)}, u32[]{:S(2)}, u32[]{:S(2)}) collective-permute-start(f32[16,3072]{1,0:T(8,128)S(1)} %get-tuple-element.59.rest_11_), channel_id=1, source_target_pairs={{0,6},{1,7},{2,4},{3,5},{4,2},{5,3},{6,0},{7,1},{8,14},{9,15},{10,... | collective-permute-start | bytes 589832 | tf_op jit(solution)/shard_map/ppermute | solution.py:533
  57.8 18.4 %collective-permute-start.3 = (f32[16,3072]{1,0:T(8,128)S(1)}, f32[16,3072]{1,0:T(8,128)S(1)}, u32[]{:S(2)}, u32[]{:S(2)}) collective-permute-start(f32[16,3072]{1,0:T(8,128)S(1)} %get-tuple-element.64.rest_12_), channel_id=1, source_target_pairs={{0,3},{1,2},{2,1},{3,0},{4,7},{5,6},{6,5},{7,4},{8,11},{9,10},{10,... | collective-permute-start | bytes 589832 | tf_op jit(solution)/shard_map/ppermute | solution.py:533
  58.8 17.4 %collective-permute-start.4 = (f32[16,3072]{1,0:T(8,128)S(1)}, f32[16,3072]{1,0:T(8,128)S(1)}, u32[]{:S(2)}, u32[]{:S(2)}) collective-permute-start(f32[16,3072]{1,0:T(8,128)S(1)} %get-tuple-element.65.rest_13_), channel_id=1, source_target_pairs={{0,7},{1,6},{2,5},{3,4},{4,3},{5,2},{6,1},{7,0},{8,15},{9,14},{10,... | collective-permute-start | bytes 589832 | tf_op jit(solution)/shard_map/ppermute | solution.py:533
  59.8 16.4 %collective-permute-start.5 = (f32[16,3072]{1,0:T(8,128)S(1)}, f32[16,3072]{1,0:T(8,128)S(1)}, u32[]{:S(2)}, u32[]{:S(2)}) collective-permute-start(f32[16,3072]{1,0:T(8,128)S(1)} %get-tuple-element.66.rest_14_), channel_id=1, source_target_pairs={{0,4},{1,5},{2,6},{3,7},{4,0},{5,1},{6,2},{7,3},{8,12},{9,13},{10,... | collective-permute-start | bytes 589832 | tf_op jit(solution)/shard_map/ppermute | solution.py:533
  61.3 14.9 %collective-permute-start.6 = (f32[16,3072]{1,0:T(8,128)S(1)}, f32[16,3072]{1,0:T(8,128)S(1)}, u32[]{:S(2)}, u32[]{:S(2)}) collective-permute-start(f32[16,3072]{1,0:T(8,128)S(1)} %get-tuple-element.67.rest_15_), channel_id=1, source_target_pairs={{0,5},{1,4},{2,7},{3,6},{4,1},{5,0},{6,3},{7,2},{8,13},{9,12},{10,... | collective-permute-start | bytes 589832 | tf_op jit(solution)/shard_map/ppermute | solution.py:533
  136.0 29.3 %all-to-all-start.3 = ((f32[16,216,128]{2,1,0:T(8,128)}), f32[16,216,128]{2,1,0:T(8,128)S(1)}, u32[]{:S(2)}, u32[]{:S(2)}) async-start(f32[16,216,128]{2,1,0:T(8,128)} %bitcast.125), calls=%async_computation.3 | async-start | bytes 3538944 | tf_op jit(solution)/shard_map/all_to_all | solution.py:595
  145.3 2.1 collective-permute-start.7
  147.5 6.8 %collective-permute-start.10 = (f32[288,128]{1,0:T(8,128)S(1)}, f32[288,128]{1,0:T(8,128)S(1)}, u32[]{:S(2)}, u32[]{:S(2)}) collective-permute-start(f32[288,128]{1,0:T(8,128)S(1)} %add.108), channel_id=1, source_target_pairs={{0,4},{1,5},{2,6},{3,7},{4,0},{5,1},{6,2},{7,3},{8,12},{9,13},{10,... | collective-permute-start | bytes 442376 | tf_op jit(solution)/shard_map/ppermute | solution.py:489
  149.5 7.7 %collective-permute-start.9 = (f32[288,128]{1,0:T(8,128)S(1)}, f32[288,128]{1,0:T(8,128)S(1)}, u32[]{:S(2)}, u32[]{:S(2)}) collective-permute-start(f32[288,128]{1,0:T(8,128)S(1)} %add.108), channel_id=1, source_target_pairs={{0,6},{1,7},{2,0},{3,1},{4,2},{5,3},{6,4},{7,5},{8,14},{9,15},{10,... | collective-permute-start | bytes 442376 | tf_op jit(solution)/shard_map/ppermute | solution.py:489
  151.5 6.1 %collective-permute-start.8 = (f32[288,128]{1,0:T(8,128)S(1)}, f32[288,128]{1,0:T(8,128)S(1)}, u32[]{:S(2)}, u32[]{:S(2)}) collective-permute-start(f32[288,128]{1,0:T(8,128)S(1)} %add.108), channel_id=1, source_target_pairs={{0,2},{1,3},{2,4},{3,5},{4,6},{5,7},{6,0},{7,1},{8,10},{9,11},{10,... | collective-permute-start | bytes 442376 | tf_op jit(solution)/shard_map/ppermute | solution.py:489
  165.3 27.4 %all-to-all-start.4 = ((f32[16,216,128]{2,1,0:T(8,128)}), f32[16,216,128]{2,1,0:T(8,128)}, u32[]{:S(2)}, u32[]{:S(2)}) async-start(f32[16,216,128]{2,1,0:T(8,128)} %bitcast.32), calls=%async_computation.4 | async-start | bytes 3538944 | tf_op jit(solution)/shard_map/all_to_all | solution.py:622
  173.2 3.3 collective-permute-start.11
  176.5 8.6 %collective-permute-start.14 = (f32[288,128]{1,0:T(8,128)S(1)}, f32[288,128]{1,0:T(8,128)S(1)}, u32[]{:S(2)}, u32[]{:S(2)}) collective-permute-start(f32[288,128]{1,0:T(8,128)S(1)} %add.113), channel_id=1, source_target_pairs={{0,4},{1,5},{2,6},{3,7},{4,0},{5,1},{6,2},{7,3},{8,12},{9,13},{10,... | collective-permute-start | bytes 442376 | tf_op jit(solution)/shard_map/ppermute | solution.py:489
  181.1 4.9 %collective-permute-start.13 = (f32[288,128]{1,0:T(8,128)S(1)}, f32[288,128]{1,0:T(8,128)S(1)}, u32[]{:S(2)}, u32[]{:S(2)}) collective-permute-start(f32[288,128]{1,0:T(8,128)S(1)} %add.113), channel_id=1, source_target_pairs={{0,6},{1,7},{2,0},{3,1},{4,2},{5,3},{6,4},{7,5},{8,14},{9,15},{10,... | collective-permute-start | bytes 442376 | tf_op jit(solution)/shard_map/ppermute | solution.py:489
  181.1 7.0 %collective-permute-start.12 = (f32[288,128]{1,0:T(8,128)S(1)}, f32[288,128]{1,0:T(8,128)S(1)}, u32[]{:S(2)}, u32[]{:S(2)}) collective-permute-start(f32[288,128]{1,0:T(8,128)S(1)} %add.113), channel_id=1, source_target_pairs={{0,2},{1,3},{2,4},{3,5},{4,6},{5,7},{6,0},{7,1},{8,10},{9,11},{10,... | collective-permute-start | bytes 442376 | tf_op jit(solution)/shard_map/ppermute | solution.py:489
  253.6 26.3 %collective-permute-start.15 = (f32[16,3072]{1,0:T(8,128)}, f32[16,3072]{1,0:T(8,128)S(1)}, u32[]{:S(2)}, u32[]{:S(2)}) collective-permute-start(f32[16,3072]{1,0:T(8,128)} %get-tuple-element.82.rest_0_), channel_id=1, source_target_pairs={{0,3},{1,2},{2,1},{3,0},{4,7},{5,6},{6,5},{7,4},{8,11},{9,10},{10,... | collective-permute-start | bytes 589832 | tf_op jit(solution)/shard_map/ppermute | solution.py:533
  258.0 21.9 %collective-permute-start.16 = (f32[16,3072]{1,0:T(8,128)}, f32[16,3072]{1,0:T(8,128)S(1)}, u32[]{:S(2)}, u32[]{:S(2)}) collective-permute-start(f32[16,3072]{1,0:T(8,128)} %get-tuple-element.83.rest_1_), channel_id=1, source_target_pairs={{0,7},{1,6},{2,5},{3,4},{4,3},{5,2},{6,1},{7,0},{8,15},{9,14},{10,... | collective-permute-start | bytes 589832 | tf_op jit(solution)/shard_map/ppermute | solution.py:533
  260.7 19.3 %collective-permute-start.17 = (f32[16,3072]{1,0:T(8,128)}, f32[16,3072]{1,0:T(8,128)S(1)}, u32[]{:S(2)}, u32[]{:S(2)}) collective-permute-start(f32[16,3072]{1,0:T(8,128)} %get-tuple-element.84.rest_2_), channel_id=1, source_target_pairs={{0,4},{1,5},{2,6},{3,7},{4,0},{5,1},{6,2},{7,3},{8,12},{9,13},{10,... | collective-permute-start | bytes 589832 | tf_op jit(solution)/shard_map/ppermute | solution.py:533
  260.7 19.3 %collective-permute-start.18 = (f32[16,3072]{1,0:T(8,128)}, f32[16,3072]{1,0:T(8,128)S(1)}, u32[]{:S(2)}, u32[]{:S(2)}) collective-permute-start(f32[16,3072]{1,0:T(8,128)} %get-tuple-element.85.rest_3_), channel_id=1, source_target_pairs={{0,5},{1,4},{2,7},{3,6},{4,1},{5,0},{6,3},{7,2},{8,13},{9,12},{10,... | collective-permute-start | bytes 589832 | tf_op jit(solution)/shard_map/ppermute | solution.py:533
  280.0 2.0 collective-permute-start.19
  280.1 6.4 %collective-permute-start.20 = (f32[16,3072]{1,0:T(8,128)}, f32[16,3072]{1,0:T(8,128)S(1)}, u32[]{:S(2)}, u32[]{:S(2)}) collective-permute-start(f32[16,3072]{1,0:T(8,128)} %get-tuple-element.92), channel_id=1, source_target_pairs={{0,2},{1,3},{2,0},{3,1},{4,6},{5,7},{6,4},{7,5},{8,10},{9,11},{10,... | collective-permute-start | bytes 589832 | tf_op jit(solution)/shard_map/ppermute | solution.py:533
  280.2 7.7 %collective-permute-start.21 = (f32[16,3072]{1,0:T(8,128)}, f32[16,3072]{1,0:T(8,128)S(1)}, u32[]{:S(2)}, u32[]{:S(2)}) collective-permute-start(f32[16,3072]{1,0:T(8,128)} %get-tuple-element.93), channel_id=1, source_target_pairs={{0,6},{1,7},{2,4},{3,5},{4,2},{5,3},{6,0},{7,1},{8,14},{9,15},{10,... | collective-permute-start | bytes 589832 | tf_op jit(solution)/shard_map/ppermute | solution.py:533
  292.9 14.3 %all-to-all-start.6 = ((f32[128,1,128]{2,1,0:T(1,128)}), f32[128,1,128]{2,1,0:T(1,128)S(1)}, u32[]{:S(2)}, u32[]{:S(2)}) async-start(f32[128,1,128]{2,1,0:T(1,128)} %bitcast.135), calls=%async_computation.6 | async-start | bytes 131072 | tf_op jit(solution)/shard_map/all_to_all | solution.py:480
  308.0 14.9 %all-to-all-start.7 = ((f32[128,1,128]{2,1,0:T(1,128)}), f32[128,1,128]{2,1,0:T(1,128)S(1)}, u32[]{:S(2)}, u32[]{:S(2)}) async-start(f32[128,1,128]{2,1,0:T(1,128)} %broadcast_in_dim.21), calls=%async_computation.7 | async-start | bytes 131072 | tf_op jit(solution)/shard_map/all_to_all | solution.py:484
  (62 other events, 541.4 us)

commit v7 on v6

--- a/solution.py
+++ b/solution.py
@@ -185,8 +185,8 @@
     masks = source_masks()
 
     def place(i, carry):
-        for j in range(16):
-            k = i * 16 + j
+        for j in range(64):
+            k = i * 64 + j
             row = turned[pl.ds(k, 1), :]
             for group in range(BD):
                 half, p = group // HELD, group % HELD
@@ -194,7 +194,7 @@
                 pltpu.store(dense.at[pl.ds(cell, 1), :], row, mask=masks[group])
         return carry
 
-    lax.fori_loop(0, FIRST // 16, place, 0)
+    lax.fori_loop(0, FIRST // 64, place, 0)
 
 
 def fold_kernel(cells, *rest):
@@ -337,8 +337,8 @@
     masks = source_masks()
 
     def pick(i, carry):
-        for j in range(16):
-            k = i * 16 + j
+        for j in range(64):
+            k = i * 64 + j
             row = None
             for group in range(BD):
                 half, p = group // HELD, group % HELD
@@ -347,7 +347,7 @@
             turned[pl.ds(k, 1), :] = row
         return carry
 
-    lax.fori_loop(0, FIRST // 16, pick, 0)
+    lax.fori_loop(0, FIRST // 64, pick, 0)
 
     def turn(i, carry):
         at = pl.multiple_of(i * LANES, LANES)
@@ -372,7 +372,7 @@
 
 def pullback_kernel(grads, s, y0, y1, y2, y3, z1, z2, z3, z4, t1, t2, t3, t4, coefs, first, out):
     def mul(a, b):
-        return jnp.dot(a[...], b[...], precision=highest, preferred_element_type=f32)
+        return dot3(split(a[...]), split(b[...]))
 
     y, z, t = (y0, y1, y2, y3), (None, z1, z2, z3, z4), (None, t1, t2, t3, t4)
     values = s[...]

time: 331 us -> 330 us (level)
  no operation moved by 1% of the time
where the time goes in v7:
time: 330 us; the launch traced here: 329 us
  Pallas kernels  117 us (35%)
  starting transfers between devices  73.4 us (22%)
  blocking collectives  58.2 us (18%)
  waiting for transfers between devices  50.9 us (15%)
  local copies, waits for them, and re-layouts  10 us (3%)
  matrix products  9.71 us (3%)
  between operations  7.48 us (2%)
    pallas_call x14, Pallas kernels, call(): pl.pallas_call(kernel, out_shape=out_shapes, in_specs=[smem] * scalars +...  117 us
    all_to_all x1, blocking collectives, shards(): returned.append(exchange(product))  29.7 us
    all_to_all x1, blocking collectives, shards(): received = exchange(sent[part])  28.5 us
    ppermute x14, starting transfers between devices, meet(): return lax.ppermute(block, 'band', [(i, i ^ ORDER[p]) for i in range(BD)])  22.1 us
    all_to_all x2, waiting for transfers between devices, total(): lax.all_to_all(copies, axes, split_axis=0, concat_axis=0, tiled=True)  16.8 us
    all_to_all x2, starting transfers between devices, total(): lax.all_to_all(values, axes, split_axis=0, concat_axis=0, tiled=True)  16.8 us
    all_to_all x2, starting transfers between devices, total(): lax.all_to_all(copies, axes, split_axis=0, concat_axis=0, tiled=True)  11.4 us
    ppermute x6, waiting for transfers between devices, band_total(): lax.ppermute(values, 'band', [(i, (i + 2 * step) % BD) for i in range(BD)])  11.4 us
  transfers between devices with their start and end apart: 28, of which 18 were waited for; matrix products, arithmetic and copies ran while one was open for 3% of the time, Pallas kernels for 13%

profile of v7, /device:TPU:1, one launch (start us, length us, event | category | flops | bytes accessed | tf_op | source)
XLA Modules:
  0.0 328.8 jit_solution(15688987857827548952)
XLA Ops:
  0.7 2.8 shard_map.284
  3.5 11.5 %all-to-all-start = ((f32[128,1,128]{2,1,0:T(1,128)}), f32[128,1,128]{2,1,0:T(1,128)S(1)}, u32[]{:S(2)}, u32[]{:S(2)}) async-start(f32[128,1,128]{2,1,0:T(1,128)} %bitcast.134), calls=%async_computation | async-start | bytes 131072 | tf_op jit(solution)/shard_map/all_to_all | solution.py:480
  20.8 3.7 %all-to-all-done = f32[128,1,128]{2,1,0:T(1,128)S(1)} async-done(((f32[128,1,128]{2,1,0:T(1,128)}), f32[128,1,128]{2,1,0:T(1,128)S(1)}, u32[]{:S(2)}, u32[]{:S(2)}) %all-to-all-start) | async-done | bytes 65568 | tf_op jit(solution)/shard_map/all_to_all | solution.py:480
  26.7 6.1 %all-to-all-start.1 = ((f32[128,1,128]{2,1,0:T(1,128)}), f32[128,1,128]{2,1,0:T(1,128)S(1)}, u32[]{:S(2)}, u32[]{:S(2)}) async-start(f32[128,1,128]{2,1,0:T(1,128)} %broadcast_in_dim.9), calls=%async_computation.1 | async-start | bytes 131072 | tf_op jit(solution)/shard_map/all_to_all | solution.py:484
  34.1 8.3 %all-to-all-done.1 = f32[128,1,128]{2,1,0:T(1,128)S(1)} async-done(((f32[128,1,128]{2,1,0:T(1,128)}), f32[128,1,128]{2,1,0:T(1,128)S(1)}, u32[]{:S(2)}, u32[]{:S(2)}) %all-to-all-start.1) | async-done | bytes 65568 | tf_op jit(solution)/shard_map/all_to_all | solution.py:484
  53.5 3.1 collective-permute-done.1.rest_2_
  63.2 12.6 %shard_map.287.rest_4_ = f32[55296,128]{1,0:T(8,128)S(1)} custom-call(s32[12288]{0:T(1024)} %copy-done.6, f32[16,3072]{1,0:T(8,128)} %copy-done.1, f32[16,3072]{1,0:T(8,128)} %copy-done.40, f32[16,3072]{1,0:T(8,128)} %copy-done.42, f32[16,3072]{1,0:T(8,128)} %copy-done.44, f32[55296,128]{1,0:T(8,128)S(1)} %shard_map.286.rest_4_), custom_call_target="tpu_custom_call", output_to_operand_aliasing={{}: (5, {})} | custom-call | bytes 49000000 | tf_op jit(solution)/shard_map/pallas_call | solution.py:435
  77.3 29.5 %shard_map.288 = (f32[55296,128]{1,0:T(8,128)S(1)}, f32[3456,128]{1,0:T(8,128)}, f32[3456,128]{1,0:T(8,128)}) custom-call(s32[12288]{0:T(1024)} %copy-done.7, f32[16,3072]{1,0:T(8,128)} %copy-done.41, f32[16,3072]{1,0:T(8,128)} %copy-done.43, f32[16,3072]{1,0:T(8,128)} %copy-done.45, f32[16,3072]{1,0:T(8,128)} %copy-done.46, ...), custom_call_target="tpu_custom_call", output_to_operand_aliasing={{0}: (5, {})} | custom-call | bytes 101500000 | tf_op jit(solution)/shard_map/pallas_call | solution.py:435
  106.9 28.5 %all_to_all.76 = f32[16,216,128]{2,1,0:T(8,128)S(1)} all-to-all(f32[16,216,128]{2,1,0:T(8,128)} %bitcast.126), channel_id=1, replica_groups=mesh['pw'=16,'band'=8] {'pw'}, dimensions={0} | all-to-all | bytes 3538944 | tf_op jit(solution)/shard_map/all_to_all | solution.py:595
  135.4 4.0 %all-to-all-start.3 = ((f32[16,216,128]{2,1,0:T(8,128)}), f32[16,216,128]{2,1,0:T(8,128)S(1)}, u32[]{:S(2)}, u32[]{:S(2)}) async-start(f32[16,216,128]{2,1,0:T(8,128)} %bitcast.125), calls=%async_computation.3 | async-start | bytes 3538944 | tf_op jit(solution)/shard_map/all_to_all | solution.py:595
  141.8 3.1 shard_map.289
  157.1 4.4 %shard_map.290.rest_0_ = f32[3456,128]{1,0:T(8,128)} custom-call(f32[288,128]{1,0:T(8,128)S(1)} %add_add_fusion.1.density, f32[288,128]{1,0:T(8,128)S(1)} %bitcast.123, f32[3456,128]{1,0:T(8,128)S(1)} %get-tuple-element.79.fields, bf16[192,96]{1,0:T(8,128)(2,1)S(1)} %copy-done.10), custom_call_target="tpu_custom_call" | custom-call | bytes 21000000 | tf_op jit(solution)/shard_map/pallas_call | solution.py:435
  161.5 3.2 all-to-all-done.3
  164.7 4.8 %all-to-all-start.4 = ((f32[16,216,128]{2,1,0:T(8,128)}), f32[16,216,128]{2,1,0:T(8,128)}, u32[]{:S(2)}, u32[]{:S(2)}) async-start(f32[16,216,128]{2,1,0:T(8,128)} %bitcast.32), calls=%async_computation.4 | async-start | bytes 3538944 | tf_op jit(solution)/shard_map/all_to_all | solution.py:622
  169.5 3.1 shard_map.291
  175.9 4.4 %collective-permute-start.14 = (f32[288,128]{1,0:T(8,128)S(1)}, f32[288,128]{1,0:T(8,128)S(1)}, u32[]{:S(2)}, u32[]{:S(2)}) collective-permute-start(f32[288,128]{1,0:T(8,128)S(1)} %add.113), channel_id=1, source_target_pairs={{0,4},{1,5},{2,6},{3,7},{4,0},{5,1},{6,2},{7,3},{8,12},{9,13},{10,... | collective-permute-start | bytes 442376 | tf_op jit(solution)/shard_map/ppermute | solution.py:489
  184.3 2.9 collective-permute-done.13
  188.2 3.2 shard_map.292
  192.1 29.7 %all_to_all.77 = f32[16,216,128]{2,1,0:T(8,128)} all-to-all(f32[16,216,128]{2,1,0:T(8,128)S(1)} %bitcast.119), channel_id=1, replica_groups=mesh['pw'=16,'band'=8] {'pw'}, dimensions={0} | all-to-all | bytes 3538944 | tf_op jit(solution)/shard_map/all_to_all | solution.py:622
  221.7 17.4 %shard_map.293.dense = f32[55296,128]{1,0:T(8,128)S(1)} custom-call(f32[3456,128]{1,0:T(8,128)} %bitcast.33.recv0, f32[3456,128]{1,0:T(8,128)} %bitcast.124, bf16[192,96]{1,0:T(8,128)(2,1)} %constant.89.clone.zt, bf16[6,256,256]{2,1,0:T(8,128)(2,1)} %constant.90.clone.mh, bf16[6,256,256]{2,1,0:T(8,128)(2,1)} %constant.91.clone.ml), custom_call_target="tpu_custom_call" | custom-call | bytes 45500000 | tf_op jit(solution)/shard_map/pallas_call | solution.py:435
  239.1 13.3 %shard_map.294 = (f32[16,3072]{1,0:T(8,128)}, f32[16,3072]{1,0:T(8,128)}, f32[16,3072]{1,0:T(8,128)}, f32[16,3072]{1,0:T(8,128)}) custom-call(s32[12288]{0:T(1024)} %copy-done.7, f32[55296,128]{1,0:T(8,128)S(1)} %shard_map.293.dense), custom_call_target="tpu_custom_call" | custom-call | bytes 49000000 | tf_op jit(solution)/shard_map/pallas_call | solution.py:435
  252.5 8.2 %collective-permute-start.15 = (f32[16,3072]{1,0:T(8,128)}, f32[16,3072]{1,0:T(8,128)S(1)}, u32[]{:S(2)}, u32[]{:S(2)}) collective-permute-start(f32[16,3072]{1,0:T(8,128)} %get-tuple-element.82.rest_0_), channel_id=1, source_target_pairs={{0,3},{1,2},{2,1},{3,0},{4,7},{5,6},{6,5},{7,4},{8,11},{9,10},{10,... | collective-permute-start | bytes 589832 | tf_op jit(solution)/shard_map/ppermute | solution.py:533
  262.4 2.7 collective-permute-start.18
  265.1 13.4 %shard_map.295 = (f32[16,3072]{1,0:T(8,128)}, f32[16,3072]{1,0:T(8,128)}, f32[16,3072]{1,0:T(8,128)}, f32[16,3072]{1,0:T(8,128)}) custom-call(s32[12288]{0:T(1024)} %copy-done.6, f32[55296,128]{1,0:T(8,128)S(1)} %shard_map.293.dense, f32[16,3072]{1,0:T(8,128)} %get-tuple-element.82.rest_0_, f32[16,3072]{1,0:T(8,128)} %get-tuple-element.83.rest_1_, ...), custom_call_target="tpu_custom_call" | custom-call | bytes 49000000 | tf_op jit(solution)/shard_map/pallas_call | solution.py:435
  281.9 3.1 collective-permute-done.20.rest_2_
  287.1 4.4 %shard_map.296 = (f32[128,3072]{1,0:T(8,128)}, f32[128,128]{1,0:T(8,128)}) custom-call(s32[8]{0:T(128)} %copy-done.21, f32[16,3072]{1,0:T(8,128)} %get-tuple-element.90.rest_0_, f32[16,3072]{1,0:T(8,128)} %copy-done.51, f32[16,3072]{1,0:T(8,128)} %copy-done.52, f32[16,3072]{1,0:T(8,128)} %copy-done.53, f32[16,3072]{1,0:T(8,128)} %copy-done.47, ...), custom_call_target="tpu_custom_call" | custom-call | bytes 10500000 | tf_op jit(solution)/shard_map/pallas_call | solution.py:435
  291.5 5.3 %all-to-all-start.6 = ((f32[128,1,128]{2,1,0:T(1,128)}), f32[128,1,128]{2,1,0:T(1,128)S(1)}, u32[]{:S(2)}, u32[]{:S(2)}) async-start(f32[128,1,128]{2,1,0:T(1,128)} %bitcast.135), calls=%async_computation.6 | async-start | bytes 131072 | tf_op jit(solution)/shard_map/all_to_all | solution.py:480
  297.4 4.0 %fusion.30.first = f32[128,3072]{1,0:T(8,128)} fusion(f32[128,128]{1,0:T(8,128)S(1)} %copy-done.9, f32[128,3072]{1,0:T(8,128)} %get-tuple-element.101), kind=kOutput, calls=%fused_computation.60 | convolution fusion | flops 603979776 | bytes 3211264 | tf_op jit(solution)/shard_map/dot_general | solution.py:462
  302.0 4.4 %all-to-all-done.6 = f32[128,1,128]{2,1,0:T(1,128)S(1)} async-done(((f32[128,1,128]{2,1,0:T(1,128)}), f32[128,1,128]{2,1,0:T(1,128)S(1)}, u32[]{:S(2)}, u32[]{:S(2)}) %all-to-all-start.6) | async-done | bytes 65568 | tf_op jit(solution)/shard_map/all_to_all | solution.py:480
  307.2 5.4 %all-to-all-start.7 = ((f32[128,1,128]{2,1,0:T(1,128)}), f32[128,1,128]{2,1,0:T(1,128)S(1)}, u32[]{:S(2)}, u32[]{:S(2)}) async-start(f32[128,1,128]{2,1,0:T(1,128)} %broadcast_in_dim.21), calls=%async_computation.7 | async-start | bytes 131072 | tf_op jit(solution)/shard_map/all_to_all | solution.py:484
  313.6 8.5 %all-to-all-done.7 = f32[128,1,128]{2,1,0:T(1,128)S(1)} async-done(((f32[128,1,128]{2,1,0:T(1,128)}), f32[128,1,128]{2,1,0:T(1,128)S(1)}, u32[]{:S(2)}, u32[]{:S(2)}) %all-to-all-start.7) | async-done | bytes 65568 | tf_op jit(solution)/shard_map/all_to_all | solution.py:484
  322.8 6.0 %shard_map.297 = f32[128,3072]{1,0:T(8,128)} custom-call(f32[128,128]{1,0:T(8,128)} %bitcast.133, f32[128,128]{1,0:T(8,128)} %multiply_bitcast_fusion.s, f32[128,128]{1,0:T(8,128)} %copy-done.26, f32[128,128]{1,0:T(8,128)} %copy-done.34, f32[128,128]{1,0:T(8,128)} %copy-done.28, f32[128,128]{1,0:T(8,128)} %copy-done.35, ...), custom_call_target="tpu_custom_call" | custom-call | bytes 10500000 | tf_op jit(solution)/shard_map/pallas_call | solution.py:435
  (221 shorter events, 56.5 us)
Async XLA Ops:
  0.7 24.7 %copy-start.38 = (f32[6,9216]{1,0:T(8,128)S(1)}, f32[6,9216]{1,0:T(8,128)}, u32[]{:S(2)}) copy-start(f32[6,9216]{1,0:T(8,128)} %param.33) | copy-start | bytes 663556
  3.5 21.0 %all-to-all-start = ((f32[128,1,128]{2,1,0:T(1,128)}), f32[128,1,128]{2,1,0:T(1,128)S(1)}, u32[]{:S(2)}, u32[]{:S(2)}) async-start(f32[128,1,128]{2,1,0:T(1,128)} %bitcast.134), calls=%async_computation | async-start | bytes 131072 | tf_op jit(solution)/shard_map/all_to_all | solution.py:480
  15.0 32.0 %copy-start.21 = (s32[8]{0:T(128)}, s32[8]{0:T(128)S(1)}, u32[]{:S(2)}) copy-start(s32[8]{0:T(128)S(1)} %broadcast_xor_fusion.order) | copy-start | bytes 100
  20.8 26.2 %copy-start.6 = (s32[12288]{0:T(1024)}, s32[12288]{0:T(1024)S(1)}, u32[]{:S(2)}) copy-start(s32[12288]{0:T(1024)S(1)} %get-tuple-element.127.rest_0_.cells) | copy-start | bytes 147460
  20.8 26.2 %copy-start.7 = (s32[12288]{0:T(1024)}, s32[12288]{0:T(1024)S(1)}, u32[]{:S(2)}) copy-start(s32[12288]{0:T(1024)S(1)} %get-tuple-element.126.rest_1_.cells) | copy-start | bytes 147460
  26.7 15.6 %all-to-all-start.1 = ((f32[128,1,128]{2,1,0:T(1,128)}), f32[128,1,128]{2,1,0:T(1,128)S(1)}, u32[]{:S(2)}, u32[]{:S(2)}) async-start(f32[128,1,128]{2,1,0:T(1,128)} %broadcast_in_dim.9), calls=%async_computation.1 | async-start | bytes 131072 | tf_op jit(solution)/shard_map/all_to_all | solution.py:484
  49.3 4.2 %collective-permute-start = (f32[16,3072]{1,0:T(8,128)S(1)}, f32[16,3072]{1,0:T(8,128)S(1)}, u32[]{:S(2)}, u32[]{:S(2)}) collective-permute-start(f32[16,3072]{1,0:T(8,128)S(1)} %get-tuple-element.57.rest_9_), channel_id=1, source_target_pairs={{0,1},{1,0},{2,3},{3,2},{4,5},{5,4},{6,7},{7,6},{8,9},{9,8},{10,11... | collective-permute-start | bytes 589832 | tf_op jit(solution)/shard_map/ppermute | solution.py:533
  50.1 6.5 %collective-permute-start.1 = (f32[16,3072]{1,0:T(8,128)S(1)}, f32[16,3072]{1,0:T(8,128)S(1)}, u32[]{:S(2)}, u32[]{:S(2)}) collective-permute-start(f32[16,3072]{1,0:T(8,128)S(1)} %get-tuple-element.58.rest_10_), channel_id=1, source_target_pairs={{0,2},{1,3},{2,0},{3,1},{4,6},{5,7},{6,4},{7,5},{8,10},{9,11},{10,... | collective-permute-start | bytes 589832 | tf_op jit(solution)/shard_map/ppermute | solution.py:533
  50.4 7.3 %collective-permute-start.2 = (f32[16,3072]{1,0:T(8,128)S(1)}, f32[16,3072]{1,0:T(8,128)S(1)}, u32[]{:S(2)}, u32[]{:S(2)}) collective-permute-start(f32[16,3072]{1,0:T(8,128)S(1)} %get-tuple-element.59.rest_11_), channel_id=1, source_target_pairs={{0,6},{1,7},{2,4},{3,5},{4,2},{5,3},{6,0},{7,1},{8,14},{9,15},{10,... | collective-permute-start | bytes 589832 | tf_op jit(solution)/shard_map/ppermute | solution.py:533
  57.8 18.1 %collective-permute-start.3 = (f32[16,3072]{1,0:T(8,128)S(1)}, f32[16,3072]{1,0:T(8,128)S(1)}, u32[]{:S(2)}, u32[]{:S(2)}) collective-permute-start(f32[16,3072]{1,0:T(8,128)S(1)} %get-tuple-element.64.rest_12_), channel_id=1, source_target_pairs={{0,3},{1,2},{2,1},{3,0},{4,7},{5,6},{6,5},{7,4},{8,11},{9,10},{10,... | collective-permute-start | bytes 589832 | tf_op jit(solution)/shard_map/ppermute | solution.py:533
  58.8 17.1 %collective-permute-start.4 = (f32[16,3072]{1,0:T(8,128)S(1)}, f32[16,3072]{1,0:T(8,128)S(1)}, u32[]{:S(2)}, u32[]{:S(2)}) collective-permute-start(f32[16,3072]{1,0:T(8,128)S(1)} %get-tuple-element.65.rest_13_), channel_id=1, source_target_pairs={{0,7},{1,6},{2,5},{3,4},{4,3},{5,2},{6,1},{7,0},{8,15},{9,14},{10,... | collective-permute-start | bytes 589832 | tf_op jit(solution)/shard_map/ppermute | solution.py:533
  59.8 16.1 %collective-permute-start.5 = (f32[16,3072]{1,0:T(8,128)S(1)}, f32[16,3072]{1,0:T(8,128)S(1)}, u32[]{:S(2)}, u32[]{:S(2)}) collective-permute-start(f32[16,3072]{1,0:T(8,128)S(1)} %get-tuple-element.66.rest_14_), channel_id=1, source_target_pairs={{0,4},{1,5},{2,6},{3,7},{4,0},{5,1},{6,2},{7,3},{8,12},{9,13},{10,... | collective-permute-start | bytes 589832 | tf_op jit(solution)/shard_map/ppermute | solution.py:533
  61.3 14.6 %collective-permute-start.6 = (f32[16,3072]{1,0:T(8,128)S(1)}, f32[16,3072]{1,0:T(8,128)S(1)}, u32[]{:S(2)}, u32[]{:S(2)}) collective-permute-start(f32[16,3072]{1,0:T(8,128)S(1)} %get-tuple-element.67.rest_15_), channel_id=1, source_target_pairs={{0,5},{1,4},{2,7},{3,6},{4,1},{5,0},{6,3},{7,2},{8,13},{9,12},{10,... | collective-permute-start | bytes 589832 | tf_op jit(solution)/shard_map/ppermute | solution.py:533
  135.4 29.3 %all-to-all-start.3 = ((f32[16,216,128]{2,1,0:T(8,128)}), f32[16,216,128]{2,1,0:T(8,128)S(1)}, u32[]{:S(2)}, u32[]{:S(2)}) async-start(f32[16,216,128]{2,1,0:T(8,128)} %bitcast.125), calls=%async_computation.3 | async-start | bytes 3538944 | tf_op jit(solution)/shard_map/all_to_all | solution.py:595
  144.9 2.1 collective-permute-start.7
  147.1 6.7 %collective-permute-start.10 = (f32[288,128]{1,0:T(8,128)S(1)}, f32[288,128]{1,0:T(8,128)S(1)}, u32[]{:S(2)}, u32[]{:S(2)}) collective-permute-start(f32[288,128]{1,0:T(8,128)S(1)} %add.108), channel_id=1, source_target_pairs={{0,4},{1,5},{2,6},{3,7},{4,0},{5,1},{6,2},{7,3},{8,12},{9,13},{10,... | collective-permute-start | bytes 442376 | tf_op jit(solution)/shard_map/ppermute | solution.py:489
  148.7 7.5 %collective-permute-start.9 = (f32[288,128]{1,0:T(8,128)S(1)}, f32[288,128]{1,0:T(8,128)S(1)}, u32[]{:S(2)}, u32[]{:S(2)}) collective-permute-start(f32[288,128]{1,0:T(8,128)S(1)} %add.108), channel_id=1, source_target_pairs={{0,6},{1,7},{2,0},{3,1},{4,2},{5,3},{6,4},{7,5},{8,14},{9,15},{10,... | collective-permute-start | bytes 442376 | tf_op jit(solution)/shard_map/ppermute | solution.py:489
  151.4 5.6 %collective-permute-start.8 = (f32[288,128]{1,0:T(8,128)S(1)}, f32[288,128]{1,0:T(8,128)S(1)}, u32[]{:S(2)}, u32[]{:S(2)}) collective-permute-start(f32[288,128]{1,0:T(8,128)S(1)} %add.108), channel_id=1, source_target_pairs={{0,2},{1,3},{2,4},{3,5},{4,6},{5,7},{6,0},{7,1},{8,10},{9,11},{10,... | collective-permute-start | bytes 442376 | tf_op jit(solution)/shard_map/ppermute | solution.py:489
  164.7 27.4 %all-to-all-start.4 = ((f32[16,216,128]{2,1,0:T(8,128)}), f32[16,216,128]{2,1,0:T(8,128)}, u32[]{:S(2)}, u32[]{:S(2)}) async-start(f32[16,216,128]{2,1,0:T(8,128)} %bitcast.32), calls=%async_computation.4 | async-start | bytes 3538944 | tf_op jit(solution)/shard_map/all_to_all | solution.py:622
  172.6 3.3 collective-permute-start.11
  175.9 8.5 %collective-permute-start.14 = (f32[288,128]{1,0:T(8,128)S(1)}, f32[288,128]{1,0:T(8,128)S(1)}, u32[]{:S(2)}, u32[]{:S(2)}) collective-permute-start(f32[288,128]{1,0:T(8,128)S(1)} %add.113), channel_id=1, source_target_pairs={{0,4},{1,5},{2,6},{3,7},{4,0},{5,1},{6,2},{7,3},{8,12},{9,13},{10,... | collective-permute-start | bytes 442376 | tf_op jit(solution)/shard_map/ppermute | solution.py:489
  180.3 6.9 %collective-permute-start.13 = (f32[288,128]{1,0:T(8,128)S(1)}, f32[288,128]{1,0:T(8,128)S(1)}, u32[]{:S(2)}, u32[]{:S(2)}) collective-permute-start(f32[288,128]{1,0:T(8,128)S(1)} %add.113), channel_id=1, source_target_pairs={{0,6},{1,7},{2,0},{3,1},{4,2},{5,3},{6,4},{7,5},{8,14},{9,15},{10,... | collective-permute-start | bytes 442376 | tf_op jit(solution)/shard_map/ppermute | solution.py:489
  182.4 5.7 %collective-permute-start.12 = (f32[288,128]{1,0:T(8,128)S(1)}, f32[288,128]{1,0:T(8,128)S(1)}, u32[]{:S(2)}, u32[]{:S(2)}) collective-permute-start(f32[288,128]{1,0:T(8,128)S(1)} %add.113), channel_id=1, source_target_pairs={{0,2},{1,3},{2,4},{3,5},{4,6},{5,7},{6,0},{7,1},{8,10},{9,11},{10,... | collective-permute-start | bytes 442376 | tf_op jit(solution)/shard_map/ppermute | solution.py:489
  252.5 26.0 %collective-permute-start.15 = (f32[16,3072]{1,0:T(8,128)}, f32[16,3072]{1,0:T(8,128)S(1)}, u32[]{:S(2)}, u32[]{:S(2)}) collective-permute-start(f32[16,3072]{1,0:T(8,128)} %get-tuple-element.82.rest_0_), channel_id=1, source_target_pairs={{0,3},{1,2},{2,1},{3,0},{4,7},{5,6},{6,5},{7,4},{8,11},{9,10},{10,... | collective-permute-start | bytes 589832 | tf_op jit(solution)/shard_map/ppermute | solution.py:533
  260.6 17.9 %collective-permute-start.16 = (f32[16,3072]{1,0:T(8,128)}, f32[16,3072]{1,0:T(8,128)S(1)}, u32[]{:S(2)}, u32[]{:S(2)}) collective-permute-start(f32[16,3072]{1,0:T(8,128)} %get-tuple-element.83.rest_1_), channel_id=1, source_target_pairs={{0,7},{1,6},{2,5},{3,4},{4,3},{5,2},{6,1},{7,0},{8,15},{9,14},{10,... | collective-permute-start | bytes 589832 | tf_op jit(solution)/shard_map/ppermute | solution.py:533
  260.6 17.9 %collective-permute-start.17 = (f32[16,3072]{1,0:T(8,128)}, f32[16,3072]{1,0:T(8,128)S(1)}, u32[]{:S(2)}, u32[]{:S(2)}) collective-permute-start(f32[16,3072]{1,0:T(8,128)} %get-tuple-element.84.rest_2_), channel_id=1, source_target_pairs={{0,4},{1,5},{2,6},{3,7},{4,0},{5,1},{6,2},{7,3},{8,12},{9,13},{10,... | collective-permute-start | bytes 589832 | tf_op jit(solution)/shard_map/ppermute | solution.py:533
  262.4 16.1 %collective-permute-start.18 = (f32[16,3072]{1,0:T(8,128)}, f32[16,3072]{1,0:T(8,128)S(1)}, u32[]{:S(2)}, u32[]{:S(2)}) collective-permute-start(f32[16,3072]{1,0:T(8,128)} %get-tuple-element.85.rest_3_), channel_id=1, source_target_pairs={{0,5},{1,4},{2,7},{3,6},{4,1},{5,0},{6,3},{7,2},{8,13},{9,12},{10,... | collective-permute-start | bytes 589832 | tf_op jit(solution)/shard_map/ppermute | solution.py:533
  278.6 3.4 %collective-permute-start.19 = (f32[16,3072]{1,0:T(8,128)}, f32[16,3072]{1,0:T(8,128)S(1)}, u32[]{:S(2)}, u32[]{:S(2)}) collective-permute-start(f32[16,3072]{1,0:T(8,128)} %get-tuple-element.91), channel_id=1, source_target_pairs={{0,1},{1,0},{2,3},{3,2},{4,5},{5,4},{6,7},{7,6},{8,9},{9,8},{10,11... | collective-permute-start | bytes 589832 | tf_op jit(solution)/shard_map/ppermute | solution.py:533
  278.7 6.4 %collective-permute-start.20 = (f32[16,3072]{1,0:T(8,128)}, f32[16,3072]{1,0:T(8,128)S(1)}, u32[]{:S(2)}, u32[]{:S(2)}) collective-permute-start(f32[16,3072]{1,0:T(8,128)} %get-tuple-element.92), channel_id=1, source_target_pairs={{0,2},{1,3},{2,0},{3,1},{4,6},{5,7},{6,4},{7,5},{8,10},{9,11},{10,... | collective-permute-start | bytes 589832 | tf_op jit(solution)/shard_map/ppermute | solution.py:533
  278.7 7.7 %collective-permute-start.21 = (f32[16,3072]{1,0:T(8,128)}, f32[16,3072]{1,0:T(8,128)S(1)}, u32[]{:S(2)}, u32[]{:S(2)}) collective-permute-start(f32[16,3072]{1,0:T(8,128)} %get-tuple-element.93), channel_id=1, source_target_pairs={{0,6},{1,7},{2,4},{3,5},{4,2},{5,3},{6,0},{7,1},{8,14},{9,15},{10,... | collective-permute-start | bytes 589832 | tf_op jit(solution)/shard_map/ppermute | solution.py:533
  291.5 14.9 %all-to-all-start.6 = ((f32[128,1,128]{2,1,0:T(1,128)}), f32[128,1,128]{2,1,0:T(1,128)S(1)}, u32[]{:S(2)}, u32[]{:S(2)}) async-start(f32[128,1,128]{2,1,0:T(1,128)} %bitcast.135), calls=%async_computation.6 | async-start | bytes 131072 | tf_op jit(solution)/shard_map/all_to_all | solution.py:480
  307.2 14.9 %all-to-all-start.7 = ((f32[128,1,128]{2,1,0:T(1,128)}), f32[128,1,128]{2,1,0:T(1,128)S(1)}, u32[]{:S(2)}, u32[]{:S(2)}) async-start(f32[128,1,128]{2,1,0:T(1,128)} %broadcast_in_dim.21), calls=%async_computation.7 | async-start | bytes 131072 | tf_op jit(solution)/shard_map/all_to_all | solution.py:484
  (62 other events, 542.1 us)
